TPU v7x, 256 devices: a whole 4x4x8 slice. The times are simulated.
256 devices in a mesh: gx: 8 (over z), gy: 4 (over x), gz: 8 (over y, core).
Axes of the slice: x: 4, y: 4, z: 8, core: 2. Of those that a mesh axis runs over, the one named last changes fastest.
Arguments:
- right_side: float32 [256, 64, 1024], P('gx', 'gy', 'gz'), may hold values from -4 to 4
- phase_mask: int32 [256, 64, 1024], P('gx', 'gy', 'gz'), may hold values 0 or 1
Outputs:
- pressure: float32 [256, 64, 1024], P('gx', 'gy', 'gz')
- residual: float32 [256, 64, 1024], P('gx', 'gy', 'gz')
All inputs are finite; a program needn't handle non-finite values. No bound on the sum of `phase_mask` on one device may be relied on, other than what follows from the above.
Results may differ from a plain program's by a relative error of at most 0.0003.
Values sent between devices are 32-bit elements; how exact they have to be, the bound alone decides.
No kernel may reach another device: no remote copies, remote signals or barrier semaphores. Data moves between devices by JAX's collectives and lax.ppermute only.
A program may use at most 192 MiB of HBM per device.

v0:
```python
import functools

import jax
import jax.numpy as jnp
from jax import lax
from jax.experimental import pallas as pl
from jax.experimental.pallas import tpu as pltpu
from jax.sharding import PartitionSpec as P

COARSE_ITERS = 8
SMOOTH_LOW = 0.25
SMOOTH_HIGH = 2.0
COARSE_LOW = 0.02
LIQUID = 10.0
GAS = 1.0

INTERPRET = False
VMEM_LIMIT = 28 * 1024 * 1024

BX, BY, BZ = 32, 16, 128
WX = 8
X0, Y0, Z0 = BX + 2 * WX, 32, 256
X1, Y1G, Z1 = 48, 8, 128
X2 = 24
X3 = 26
F32 = jnp.float32
BF16 = jnp.bfloat16
DOWN, UP = 3, 3
UC, B0, U0, B1 = 4, 2, 4, 16


def chebyshev(low, degree):
    theta = 0.5 * (SMOOTH_HIGH + low)
    delta = 0.5 * (SMOOTH_HIGH - low)
    sigma = theta / delta
    rho_old = 1.0 / sigma
    steps = []
    for _ in range(1, degree):
        rho_new = 1.0 / (2.0 * sigma - rho_old)
        steps.append((rho_new * rho_old, 2.0 * rho_new / delta))
        rho_old = rho_new
    return 1.0 / theta, steps


FIRST, ((KEEP, GAIN),) = chebyshev(SMOOTH_LOW, 2)
COARSE_FIRST, COARSE_STEPS = chebyshev(COARSE_LOW, COARSE_ITERS)


def roll(values, shift, axis):
    return pltpu.roll(values, shift % values.shape[axis], axis)


def iota(shape, dim):
    return lax.broadcasted_iota(jnp.int32, shape, dim)


def split(values, terms):
    parts = []
    for n in range(terms):
        part = values.astype(BF16)
        parts.append(part)
        if n + 1 < terms:
            values = values - part.astype(F32)
    return parts


def times(values, matrix, terms):
    return sum(jnp.dot(p, matrix, preferred_element_type=F32) for p in split(values, terms))


def times_left(matrix, values, terms):
    return sum(jnp.dot(matrix, p, preferred_element_type=F32) for p in split(values, terms))


def lane_pairs(fine, weight, odd_only=False):
    z = iota((fine, 128), 0)
    half = z >> 1
    if fine == 128:
        half = jnp.where(z >= 96, half + 64, half)
    hit = half == iota((fine, 128), 1)
    if odd_only:
        hit = hit & ((z & 1) == 1)
    return jnp.where(hit, weight, 0.0).astype(BF16)


def lane_copies(fine):
    z = iota((128, fine), 1)
    half = z >> 1
    if fine == 128:
        half = jnp.where(z >= 96, half + 64, half)
    return jnp.where(half == iota((128, fine), 0), 1.0, 0.0).astype(BF16)


def row_pairs(rows, odd_x=False, odd_y=False):
    shape = (2 * rows, 8 * rows)
    shift = rows.bit_length() - 1
    c, f = iota(shape, 0), iota(shape, 1)
    cx, cy = c >> (shift - 1), c & (rows // 2 - 1)
    x, y = f >> shift, f & (rows - 1)
    hit = ((x >> 1) == cx) & ((y >> 1) == cy)
    if odd_x:
        hit = hit & ((x & 1) == 1)
    if odd_y:
        hit = hit & ((y & 1) == 1)
    return jnp.where(hit, 1.0, 0.0).astype(BF16)


def row_copies(rows):
    shape = (8 * rows, 2 * rows)
    shift = rows.bit_length() - 1
    f, c = iota(shape, 0), iota(shape, 1)
    hit = ((f >> (shift + 1)) == (c >> (shift - 1))) & (((f & (rows - 1)) >> 1) == (c & (rows // 2 - 1)))
    return jnp.where(hit, 1.0, 0.0).astype(BF16)


def coarsen(block, rows_matrix, lanes_matrix):
    planes, rows, lanes = block.shape
    out = times(times_left(rows_matrix, block.reshape(planes * rows, lanes), DOWN), lanes_matrix, DOWN)
    return out.reshape(4, rows // 2, 128)


def coarsen_all(planes, rows_matrix, lanes_matrix):
    return jnp.concatenate(
        [coarsen(planes[at : at + 8], rows_matrix, lanes_matrix) for at in range(0, planes.shape[0], 8)], 0)


def refine(block, rows_matrix, lanes_matrix):
    planes, rows, lanes = block.shape
    out = times_left(rows_matrix, times(block.reshape(planes * rows, lanes), lanes_matrix, UP), UP)
    return out.reshape(8, 2 * rows, lanes_matrix.shape[1])


def apply_at(v, at, planes, faces):
    fx, fy, fz, diag = faces
    here = pl.ds(at, planes)
    wide = v[pl.ds(at - 1, planes + 2)]
    x = fx[pl.ds(at - 1, planes + 1)]
    c = wide[1:-1]
    y, z = fy[here], fz[here]
    out = diag[here] * c - x[1:] * wide[2:] - x[:-1] * wide[:-2]
    out = out - y * roll(c, -1, 1) - roll(y * c, 1, 1)
    return out - z * roll(c, -1, 2) - roll(z * c, 1, 2)


def step_x(values, by):
    if by > 0:
        return jnp.concatenate([values[-1:], values[:-1]], 0)
    return jnp.concatenate([values[1:], values[:1]], 0)


def apply_to(v, faces):
    fx, fy, fz, diag = faces
    out = diag * v - fx * step_x(v, -1) - step_x(fx * v, 1)
    out = out - fy * roll(v, -1, 1) - roll(fy * v, 1, 1)
    return out - fz * roll(v, -1, 2) - roll(fz * v, 1, 2)


def inverse(diag):
    return 1.0 / jnp.where(diag > 0.0, diag, 1.0)


def level_of(fx, fx_before, fy, fz, gx, gy, gz, sizes):
    nx, ny, nz = sizes
    diag = fx + jnp.where((gx == 0) | (gx == nx), 0.0, fx_before)
    diag = diag + fy + jnp.where(gy == 0, 0.0, roll(fy, 1, 1))
    diag = diag + fz + jnp.where(gz == 0, 0.0, roll(fz, 1, 2))
    fx = jnp.where((gx == nx - 1) | (gx == -1), 0.0, fx)
    fy = jnp.where((gy == ny - 1) | (gy == -1), 0.0, fy)
    fz = jnp.where((gz == nz - 1) | (gz == -1), 0.0, fz)
    return fx, fy, fz, diag, inverse(diag)


def loop(start, stop, block, body, unroll=1):
    count = (stop - start) // block

    def step(i, carry):
        body(start + i * block, block)
        return carry

    if count:
        lax.fori_loop(0, count, step, 0, unroll=unroll)
    rest = stop - start - count * block
    if rest:
        body(stop - rest, rest)


def beside(one, two, high):
    axis = one.ndim - 1
    return jnp.where((iota(one.shape, axis) >= 64) == high, one, roll(two, 64, axis))


def sides(below, above, at):
    one, two = above[at], below[at]
    axis = one.ndim - 1
    lane = iota(one.shape, axis)
    return jnp.where(lane < 64, one, two), roll(jnp.where(lane >= 64, one, two), 64, axis)


def density_of(mask):
    return GAS + (LIQUID - GAS) * mask[...].astype(F32)


def send_z_own(mask, to_upper, to_lower):
    density = density_of(mask)
    for out, high in ((to_upper, True), (to_lower, False)):
        out[...] = beside(density[0:16], density[16:32], high)


def send_first(mask, below, above, row, plane):
    density = density_of(mask)
    one, two = sides(below, above, slice(0, 16))
    plane[:, 0:128] = density[0]
    plane[:, 128:256] = one[0]
    for x in range(BX):
        row[x : x + 1, 0:128] = density[x, 0:1]
        row[x : x + 1, 128:256] = (one[x, 0:1] if x < 16 else two[x - 16, 0:1])


def send_y(r, mask, to_upper, to_lower):
    density = density_of(mask)
    for out, rows, line in ((to_upper, slice(8, 16), 7), (to_lower, slice(0, 8), 8)):
        out[0:BX] = r[:, rows, :]
        out[BX : 2 * BX] = density[:, rows]
        for x in range(BX):
            out[2 * BX + x // 8, x % 8 : x % 8 + 1] = density[x, line : line + 1]


def send_x(lower, upper, below, above, to_upper, to_lower):
    for out, r_at, d_at, pack in ((to_upper, BX - 8, BX - 9, 3), (to_lower, 0, 0, 0)):
        for tile, source in enumerate((lower, upper, above, below)):
            rows = slice(8 * tile, 8 * tile + 8)
            out[0:8, rows] = source[r_at : r_at + 8]
            out[8:17, rows] = source[BX + d_at : BX + d_at + 9]
        out[17, 0:8] = below[2 * BX + pack]
        out[17, 8:16] = above[2 * BX + pack]
        out[17, 16:32] = jnp.zeros((16, 128), F32)


def send_z(lower, upper, below, above, x_below, x_above, to_upper, to_lower):
    for out, high in ((to_upper, True), (to_lower, False)):
        out[0:8] = beside(x_below[0:8], x_below[9:17], high)
        out[40:48] = beside(x_above[0:8], x_above[8:16], high)
        out[48] = beside(x_below[8], x_above[16], high)
        for tile, source in enumerate((lower, upper, above, below)):
            out[8:40, 8 * tile : 8 * tile + 8] = beside(source[0:BX], source[BX : 2 * BX], high)
        out[49, 0:8] = beside(x_below[17, 0:8], x_below[17, 8:16], high)
        for n in range(4):
            at = 8 * (n + 1)
            out[49 + at // 32, at % 32 : at % 32 + 8] = beside(below[2 * BX + n], above[2 * BX + n], high)
        out[50, 8:16] = beside(x_above[17, 0:8], x_above[17, 8:16], high)
        out[50, 16:32] = jnp.zeros((16, 128), F32)


def smooth_0(r, faces, inv, d0, d1, start, stop, between, again=False):
    def second(at, n):
        here = pl.ds(at, n)
        left = r[here] - apply_at(d0, at, n, faces)
        r[here] = left
        d1[here] = KEEP * d0[here] + GAIN * (left * inv[here])

    loop(start + 1, stop - 1, B0, second, U0)
    between()

    def third(at, n):
        here = pl.ds(at, n)
        left = r[here] - apply_at(d1, at, n, faces)
        r[here] = left
        if again:
            d0[here] = (FIRST * left) * inv[here]

    loop(start + 2, stop - 2, B0, third, U0)


def restrict_0(r, out):
    rows, lanes = row_pairs(16), lane_pairs(256, 0.125)
    for g in range(4):
        block = r[WX + 8 * g : WX + 8 * g + 8, 0:16, :]
        out[4 * g : 4 * g + 4] = coarsen(block, rows, lanes)


def add_own(total, terms, first):
    value = None if first else total[...]
    for term in terms:
        own = term[WX : WX + BX, 0:BY, 0:BZ]
        value = own if value is None else value + own
    total[...] = value


def face(total):
    return jnp.where(total < 5.0, 1.0, jnp.where(total < 15.0, 2.0 / 11.0, 0.1))


def own_faces_0(sizes, where, mask, below, above, row, plane, packed, rho, raw_x, raw_y, raw_z):
    nx, ny, nz = sizes
    own, side = slice(0, 128), slice(128, 256)
    rho[0:BX, :, own] = density_of(mask)
    rho[0:16, :, side], rho[16:32, :, side] = sides(below, above, slice(0, 16))
    rho[BX] = plane[...]
    shape = (BY, Z0)
    y = iota(shape, 0)
    gy = where[1] * BY + y
    lane = iota(shape, 1)
    gz = where[2] * BZ + jnp.where(lane < 192, lane, lane - 256)

    def one_plane(p, n):
        c = rho[p]
        raw_x[p] = face(c + jnp.where(where[0] * BX + p == nx - 1, GAS, rho[p + 1]))
        after = jnp.where(y == BY - 1, row[pl.ds(p, 1)], roll(c, -1, 0))
        raw_y[p] = face(c + jnp.where(gy == ny - 1, GAS, after))
        raw_z[p] = face(c + jnp.where(gz == nz - 1, GAS, roll(c, -1, 1)))

    loop(0, BX, 1, one_plane, UC)
    lanes, odd_lanes = lane_pairs(256, 0.125), lane_pairs(256, 0.125, True)
    for n, (raw, rows, columns) in enumerate((
        (raw_x, row_pairs(16, odd_x=True), lanes),
        (raw_y, row_pairs(16, odd_y=True), lanes),
        (raw_z, row_pairs(16), odd_lanes),
    )):
        for g in range(4):
            packed[16 * n + 4 * g : 16 * n + 4 * g + 4] = coarsen(raw[8 * g : 8 * g + 8], rows, columns)


def faces_0(sizes, where, lower, upper, below, above, x_below, x_above, z_below, z_above,
            fx, fy, fz, diag, inv, rho, low, up):
    nx, ny, nz = sizes
    gx0, gy0, gz0 = where[0] * BX, where[1] * BY, where[2] * BZ
    own, side = slice(0, 128), slice(128, 256)
    rho[0:9, :, own] = x_below[8:17]
    rho[41:50, :, own] = x_above[8:17]
    for tile, source in enumerate((lower, upper, above, below)):
        rho[9:41, 8 * tile : 8 * tile + 8, own] = source[BX : 2 * BX]
    low[0:8, own] = x_below[17, 0:8]
    up[0:8, own] = x_below[17, 8:16]
    low[40:48, own] = x_above[17, 0:8]
    up[40:48, own] = x_above[17, 8:16]
    for n in range(4):
        low[8 + 8 * n : 16 + 8 * n, own] = below[2 * BX + n]
        up[8 + 8 * n : 16 + 8 * n, own] = above[2 * BX + n]

    def side_planes(p, n):
        rho[pl.ds(p + 1, n), :, side] = sides(z_below, z_above, pl.ds(p, n))[1]

    loop(0, X0, 4, side_planes)
    rho[0, :, side], rho[49, :, side] = sides(z_below, z_above, 48)
    low[0:32, side], up[0:32, side] = sides(z_below, z_above, 49)
    low_rest, up_rest = sides(z_below, z_above, 50)
    low[32:48, side], up[32:48, side] = low_rest[0:16], up_rest[0:16]

    def plane(p, n):
        shape = (Y0, Z0)
        row, lane = iota(shape, 0), iota(shape, 1)
        gy = gy0 + jnp.where(row < 24, row, row - 32)
        gz = gz0 + jnp.where(lane < 192, lane, lane - 256)
        gx = gx0 + p - WX
        c = rho[p + 1]
        f_x = face(c + jnp.where(gx == nx - 1, GAS, rho[p + 2]))
        l_x = jnp.where(gx == 0, 0.0, face(c + rho[p]))
        over = jnp.where(row == 23, up[pl.ds(p, 1)], roll(c, -1, 0))
        under = jnp.where(row == 24, low[pl.ds(p, 1)], roll(c, 1, 0))
        f_y = face(c + jnp.where(gy == ny - 1, GAS, over))
        l_y = jnp.where(gy == 0, 0.0, face(c + under))
        f_z = face(c + jnp.where(gz == nz - 1, GAS, roll(c, -1, 1)))
        l_z = jnp.where(gz == 0, 0.0, roll(f_z, 1, 1))
        d = f_x + l_x + f_y + l_y + f_z + l_z
        i = 1.0 / d
        diag[p] = d
        inv[p] = i
        fx[p] = jnp.where((gx == nx - 1) | (gx == -1), 0.0, f_x)
        fy[p] = jnp.where((gy == ny - 1) | (gy == -1), 0.0, f_y)
        fz[p] = jnp.where((gz == nz - 1) | (gz == -1), 0.0, f_z)

    loop(0, X0, 1, plane, UC)


def begin(lower, upper, below, above, x_below, x_above, z_below, z_above, fx, fy, fz, diag, inv,
          r, total, packed, d0, d1):
    own, side = slice(0, 128), slice(128, 256)
    r[0:8, :, own] = x_below[0:8]
    r[40:48, :, own] = x_above[0:8]
    for tile, source in enumerate((lower, upper, above, below)):
        r[8:40, 8 * tile : 8 * tile + 8, own] = source[0:BX]

    def first(p, n):
        here = pl.ds(p, n)
        r[here, :, side] = sides(z_below, z_above, here)[0]
        d0[here] = (FIRST * r[here]) * inv[here]

    loop(0, X0, B0, first, U0)
    smooth_0(r, (fx, fy, fz, diag), inv, d0, d1, 0, X0, lambda: add_own(total, (d0, d1), True))
    restrict_0(r, packed)


def assemble_1(part, own, below, above, out):
    out[0:16] = below[part]
    out[16:32] = own[part]
    out[32:48] = above[part]


def relax_1(r, faces, inv, d0, d1, start, stop):
    def second(at, n):
        here = pl.ds(at, n)
        left = r[here] - apply_at(d0, at, n, faces)
        r[here] = left
        d1[here] = KEEP * d0[here] + GAIN * (left * inv[here])

    loop(start, stop, B1, second)


def faces_1(sizes, where, own, below, above,
            fx, fy, fz, diag, inv, gx2, gy2, gz2, diag2, inv2, packed):
    n1 = tuple(n // 2 for n in sizes)
    n2 = tuple(n // 4 for n in sizes)
    ny1 = fx.shape[1]
    ny2 = ny1 // 2
    rows, lanes, odd_lanes = row_pairs(ny1), lane_pairs(128, 0.125), lane_pairs(128, 0.125, True)
    coarse = []
    for n, (raw, rows_matrix, columns) in enumerate((
        (fx, row_pairs(ny1, odd_x=True), lanes),
        (fy, row_pairs(ny1, odd_y=True), lanes),
        (fz, rows, odd_lanes),
    )):
        assemble_1(slice(16 * n, 16 * (n + 1)), own, below, above, raw)
        coarse.append(jnp.concatenate(
            [coarsen(raw[8 * g : 8 * g + 8], rows_matrix, columns) for g in range(6)], 0))
    shape = (B1, ny1, 128)
    gy = lax.rem(where[1] * 8 + iota(shape, 1), n1[1])
    lane = iota(shape, 2)
    gz = where[2] * 64 + jnp.where(lane < 96, lane, lane - 128)

    def planes(n, count):
        at = X1 - B1 - n
        here = pl.ds(at, B1)
        gx = where[0] * 16 + at - 16 + iota(shape, 0)
        c = fx[here]
        before = jnp.concatenate([fx[pl.ds(jnp.maximum(at - 1, 0), 1)], c[:-1]], 0)
        level = level_of(c, before, fy[here], fz[here], gx, gy, gz, n1)
        fx[here], fy[here], fz[here], diag[here], inv[here] = level

    loop(0, X1, B1, planes)
    shape = (X2, ny2, 128)
    lane = iota(shape, 2)
    at_2 = (
        where[0] * 8 - 8 + iota(shape, 0),
        lax.rem(where[1] * 4 + iota(shape, 1), n2[1]),
        where[2] * 32 + jnp.where(lane < 64, lane, lane - 128),
    )
    level_2 = level_of(coarse[0], step_x(coarse[0], 1), coarse[1], coarse[2], *at_2, n2)
    gx2[...], gy2[...], gz2[...], diag2[...], inv2[...] = level_2
    sent = None
    for n, (rows_matrix, columns) in enumerate((
        (row_pairs(ny2, odd_x=True), lanes),
        (row_pairs(ny2, odd_y=True), lanes),
        (row_pairs(ny2), odd_lanes),
    )):
        at = 16 * (n + 1)
        value = roll(coarsen_all(coarse[n], rows_matrix, columns)[0:10], at, 2)
        sent = value if sent is None else jnp.where(iota(value.shape, 2) < at, sent, value)
    packed[...] = sent


def down(own, below, above, fx, fy, fz, diag, inv, gx2, gy2, gz2, diag2, inv2, *refs):
    *given, r, e, r2_out, e2_out, packed, d0, d1 = refs
    ny1 = fx.shape[1]
    ny2 = ny1 // 2
    assemble_1(slice(0, 16), own, below, above, r)
    rows, lanes = row_pairs(ny1), lane_pairs(128, 0.125)

    def begin_1(at, n):
        here = pl.ds(at, n)
        d0[here] = (FIRST * r[here]) * inv[here]

    loop(0, X1, B1, begin_1)
    faces = (fx, fy, fz, diag)
    relax_1(r, faces, inv, d0, d1, 1, X1 - 1)

    def third(at, n):
        here = pl.ds(at, n)
        r[here] = r[here] - apply_at(d1, at, n, faces)
        e[here] = d0[here] + d1[here]

    loop(2, X1 - 2, B1, third)
    e[0:2] = d0[0:2]
    e[X1 - 2 : X1] = d0[X1 - 2 : X1]
    r2 = jnp.concatenate([coarsen(r[8 * g : 8 * g + 8], rows, lanes) for g in range(6)], 0)
    faces_2 = (gx2[...], gy2[...], gz2[...], diag2[...])
    d = (FIRST * r2) * inv2[...]
    r2 = r2 - apply_to(d, faces_2)
    d_next = KEEP * d + GAIN * (r2 * inv2[...])
    r2 = r2 - apply_to(d_next, faces_2)
    r2_out[...] = r2
    e2_out[...] = d + d_next
    sent = coarsen_all(r2, row_pairs(ny2), lanes)
    if given:
        packed[...] = jnp.where(iota(packed.shape, 2) < 16, sent[0:10], given[0][...])
    else:
        packed[...] = sent[2:10]


def spread(own, below, above, out):
    shape = own.shape
    lane = iota(shape, 2)
    values = []
    for n in range(4 if out.shape[0] > shape[0] else 1):
        start = 64 * (n % 2)
        here = lane - start
        value = jnp.where(here < 16, roll(own[...], start - 16 * n, 2), 0.0)
        value = jnp.where((here >= 16) & (here < 32), roll(above[...], start + 16 - 16 * n, 2), value)
        value = jnp.where(here >= 48, roll(below[...], start + 48 - 16 * n, 2), value)
        if n % 2:
            values[-1] = jnp.where(here < 0, values[-1], value)
        else:
            values.append(value)
    for n, value in enumerate(values):
        out[shape[0] * n : shape[0] * (n + 1)] = value


def unspread(own, below, above, n):
    if own.shape[0] == 20:
        at = 10 * (n // 2)
        parts = [below[at : at + 10]] + [part[at + 2 : at + 10] for part in (own, above)]
    else:
        parts = [jnp.zeros((2,) + own.shape[1:], F32), below[...], own[...], above[...]]
    value = jnp.concatenate(parts, 0)
    lane = iota(value.shape, 2)
    near, far = (roll(value, 64, 2), value) if n % 2 else (value, roll(value, 64, 2))
    return jnp.where(lane < 32, near, jnp.where(lane >= 112, far, 0.0))


def up(sizes, last, where, own3, below3, above3, *refs):
    n3 = tuple(n // 8 for n in sizes)
    first = not last
    refs = list(refs)
    take = lambda n: [refs.pop(0) for _ in range(n)]
    if last:
        level_3 = take(5)
    gx2, gy2, gz2, diag2, inv2, r2_in, e2_in = take(7)
    fx1, fy1, fz1, diag1, inv1, r1_in, e1_in = take(7)
    fx, fy, fz, diag, inv, r_in, total_in = take(7)
    if first:
        level_3 = take(5)
        r, total, packed = take(3)
    else:
        pressure, residual = take(2)
        (r,) = take(1)
    p1, r1, a1, b1, c1, p0, d0, d1 = take(8)

    ny3 = own3.shape[1]
    shape = (X3, ny3, 128)
    r3 = unspread(own3, below3, above3, 0)
    if first:
        raw = [unspread(own3, below3, above3, n) for n in (1, 2, 3)]
        lane = iota(shape, 2)
        at = (
            where[0] * 4 - 12 + iota(shape, 0),
            lax.rem(where[1] * 2 + iota(shape, 1), n3[1]),
            where[2] * 16 + jnp.where(lane < 64, lane, lane - 128),
        )
        values = level_of(raw[0], step_x(raw[0], 1), raw[1], raw[2], *at, n3)
        for ref, value in zip(level_3, values):
            ref[...] = value
    faces = tuple(ref[...] for ref in level_3[:4])
    inv3 = level_3[4][...]
    d = (COARSE_FIRST * r3) * inv3
    total3 = d
    for keep, gain in COARSE_STEPS:
        r3 = r3 - apply_to(d, faces)
        d = keep * d + gain * (r3 * inv3)
        total3 = total3 + d

    copies_rows, copies_lanes = row_copies(2 * ny3), lane_copies(128)
    blocks = [refine(total3[8 + 4 * g : 12 + 4 * g], copies_rows, copies_lanes) for g in range(3)]
    p = jnp.concatenate(blocks, 0)
    faces = (gx2[...], gy2[...], gz2[...], diag2[...])
    r2 = r2_in[...] - apply_to(p, faces)
    d = (FIRST * r2) * inv2[...]
    r2 = r2 - apply_to(d, faces)
    d_next = KEEP * d + GAIN * (r2 * inv2[...])
    e2 = e2_in[...] + p + d + d_next

    copies_rows = row_copies(4 * ny3)
    for g in range(4):
        p1[8 + 8 * g : 16 + 8 * g] = refine(e2[4 + 4 * g : 8 + 4 * g], copies_rows, copies_lanes)
    faces = (fx1, fy1, fz1, diag1)

    def lift_1(at, n):
        here = pl.ds(at, n)
        left = r1_in[here] - apply_at(p1, at, n, faces)
        r1[here] = left
        a1[here] = (FIRST * left) * inv1[here]

    loop(11, 37, B1, lift_1)
    relax_1(r1, faces, inv1, a1, b1, 12, 36)

    def sum_1(at, n):
        here = pl.ds(at, n)
        value = e1_in[here] + p1[here] + a1[here] + b1[here]
        c1[here, 0:8] = value[:, 0:8]
        tile = (n, 8, 128)
        c1[here, 8:16] = jnp.where(iota(tile, 1) < 4, value[:, 8:16], value[:, -8:])

    loop(12, 36, B1, sum_1)

    copies_rows, copies_lanes = row_copies(32), lane_copies(256)
    for g in range(6):
        p0[8 * g : 8 * g + 8] = refine(c1[12 + 4 * g : 16 + 4 * g], copies_rows, copies_lanes)
    faces = (fx, fy, fz, diag)
    begin_at, end_at = (6, 42) if last else (2, 46)

    def lift_0(at, n):
        here = pl.ds(at, n)
        left = r_in[here] - apply_at(p0, at, n, faces)
        r[here] = left
        d0[here] = (FIRST * left) * inv[here]

    loop(begin_at, end_at, B0, lift_0, U0)
    into = pressure if last else total
    into[...] = total_in[...]
    smooth_0(r, faces, inv, d0, d1, begin_at, end_at, lambda: add_own(into, (p0, d0, d1), False), again=first)
    if last:
        residual[...] = r[WX : WX + BX, 0:BY, 0:BZ]
    else:
        smooth_0(r, faces, inv, d0, d1, 4, 44, lambda: add_own(total, (d0, d1), False))
        restrict_0(r, packed)


def call(kernel, name, args, outs, scratch=(), us=0, after=()):
    body, count = kernel, len(args)
    if after:
        def kernel(*refs):
            body(*refs[:count], *refs[count + len(after) :])

    vmem = pl.BlockSpec(memory_space=pltpu.VMEM)
    smem = pl.BlockSpec(memory_space=pltpu.SMEM)
    return pl.pallas_call(
        kernel,
        out_shape=[jax.ShapeDtypeStruct(s, F32) for s in outs],
        in_specs=[smem if a.ndim == 1 else vmem for a in args] + [pl.BlockSpec(memory_space=pl.ANY)] * len(after),
        out_specs=[vmem] * len(outs),
        scratch_shapes=[pltpu.VMEM(s, F32) for s in scratch],
        compiler_params=pltpu.CompilerParams(vmem_limit_bytes=VMEM_LIMIT),
        name=name,
        cost_estimate=pl.CostEstimate(flops=0, bytes_accessed=us * 3_500_000, transcendentals=0) if us else None,
        interpret=INTERPRET,
    )(*args, *after)


def from_below(array, axis, by=1):
    n = lax.axis_size(axis)
    return lax.ppermute(array, axis, [(i, (i + by) % n) for i in range(n)])


def from_above(array, axis, by=1):
    n = lax.axis_size(axis)
    return lax.ppermute(array, axis, [((i + by) % n, i) for i in range(n)])


def body(right_side, phase_mask):
    nx, ny, nz = (lax.axis_size(a) for a in ("gx", "gy", "gz"))
    sizes = (nx * BX, ny * BY, nz * BZ)
    where = jnp.stack([lax.axis_index(a) for a in ("gx", "gy", "gz")]).astype(jnp.int32)
    own = (BX, BY, BZ)
    full = (X0, Y0, Z0)
    full_1 = (X1, 8 * ny, 128)
    full_2 = (X2, 4 * ny, 128)
    full_3 = (X3, 2 * ny, 128)

    def along_y(packed):
        return [packed] + [from_above(packed, "gy", s) for s in range(1, ny)]

    def along_x(parts):
        rows = jnp.concatenate(parts, 1)
        return rows, from_below(rows, "gx"), from_above(rows, "gx")

    to_upper, to_lower = call(send_z_own, "send_z_own", (phase_mask,), [(16, BY, 128)] * 2)
    beside_own = (from_below(to_upper, "gz"), from_above(to_lower, "gz"))
    upper, lower = call(
        send_y, "send_y", (right_side, phase_mask), [(2 * BX + 4, 8, 128)] * 2, after=(to_upper, to_lower))
    below, above = from_below(upper, "gy"), from_above(lower, "gy")
    row, plane = call(send_first, "send_first", (phase_mask, *beside_own), [(BX, Z0), (BY, Z0)])
    row, plane = from_above(row, "gy"), from_above(plane, "gx")
    to_upper, to_lower = call(send_x, "send_x", (lower, upper, below, above), [(18, Y0, 128)] * 2, after=(row, plane))
    x_below, x_above = from_below(to_upper, "gx"), from_above(to_lower, "gx")
    pieces = (lower, upper, below, above, x_below, x_above)
    (packed,) = call(
        functools.partial(own_faces_0, sizes), "own_faces_0", (where, phase_mask, *beside_own, row, plane),
        [(48, 8, 128)], [(BX + 1, BY, Z0)] + [(BX, BY, Z0)] * 3, us=2)
    parts = along_y(packed)
    around_faces = along_x(parts)
    to_upper, to_lower = call(send_z, "send_z", pieces, [(51, Y0, 128)] * 2, after=(packed, parts[1]))
    pieces += (from_below(to_upper, "gz"), from_above(to_lower, "gz"))

    level_0 = call(
        functools.partial(faces_0, sizes), "faces_0", (where, *pieces), [full] * 5,
        [(X0 + 2, Y0, Z0), (X0, Z0), (X0, Z0)], us=4, after=around_faces[:1])
    r0, total, packed = call(
        begin, "begin", (*pieces, *level_0), [full, own, (16, 8, 128)], [full] * 2, us=6)
    *levels, faces_3 = call(
        functools.partial(faces_1, sizes), "faces_1", (where, *around_faces),
        [full_1] * 5 + [full_2] * 5 + [(10, 2 * ny, 128)], us=3)
    level_3 = []
    for cycle in range(2):
        first = cycle == 0
        r1, e1, r2, e2, packed = call(
            down, "down", (*along_x(along_y(packed)), *levels, *([faces_3] if first else [])),
            [full_1] * 2 + [full_2] * 2 + [(10 if first else 8, 2 * ny, 128)], [full_1] * 2, us=4)
        below, above = from_below(packed, "gz"), from_above(packed, "gz")
        (wide,) = call(spread, "spread", (packed, below, above), [(20 if first else 8, 2 * ny, 128)])
        gathered = (wide, from_below(wide, "gx", 2), from_above(wide, "gx", 2))
        args = (where, *gathered, *level_3, *levels[5:], r2, e2, *levels[:5], r1, e1, *level_0, r0, total)
        scratch = [full_1] * 4 + [(X1, 16, 128)] + [full] * 3
        if first:
            *level_3, r0, total, packed = call(
                functools.partial(up, sizes, False), "up", args,
                [full_3] * 5 + [full, own, (16, 8, 128)], scratch, us=15)
        else:
            return tuple(call(functools.partial(up, sizes, True), "up_last", args, [own] * 2, [full] + scratch, us=10))


def solution(mesh):
    spec = P("gx", "gy", "gz")
    return jax.shard_map(body, mesh=mesh, in_specs=(spec, spec), out_specs=(spec, spec), check_vma=False)
```

profile of v0, /device:TPU:6, one launch (start us, length us, event | category | flops | bytes accessed | tf_op | source)
XLA Modules:
  0.0 144.4 jit_solution(4185930856446093699)
XLA Ops:
  0.6 0.9 copy-done
  1.6 0.1 send_z_own.1
  1.7 0.9 copy-done.2
  2.6 0.1 send_y.1
  2.7 0.9 collective-permute-start.1
  3.6 2.4 %collective-permute-start = (f32[68,8,128]{2,1,0:T(8,128)S(1)}, f32[68,8,128]{2,1,0:T(8,128)S(1)}, u32[]{:S(2)}, u32[]{:S(2)}) collective-permute-start(f32[68,8,128]{2,1,0:T(8,128)S(1)} %get-tuple-element.52.refs_1_.refs_2_.upper), channel_id=1, source_target_pairs={{0,8},{8,16},{16,24},{24,0},{1,9},{9,17},{17,25},{25,1},{2,10},{10... | collective-permute-start | bytes 835592 | tf_op jit(solution)/shard_map/ppermute | solution.py:649
  6.0 3.0 %collective-permute-start.3 = (f32[16,16,128]{2,1,0:T(8,128)S(1)}, f32[16,16,128]{2,1,0:T(8,128)S(1)}, u32[]{:S(2)}, u32[]{:S(2)}) collective-permute-start(f32[16,16,128]{2,1,0:T(8,128)S(1)} %get-tuple-element.50.refs_3_), channel_id=1, source_target_pairs={{1,0},{2,1},{3,2},{4,3},{5,4},{6,5},{7,6},{0,7},{9,8},{10,9},{11,1... | collective-permute-start | bytes 393224 | tf_op jit(solution)/shard_map/ppermute | solution.py:654
  9.0 2.6 %collective-permute-done.2.below = f32[16,16,128]{2,1,0:T(8,128)S(1)} collective-permute-done((f32[16,16,128]{2,1,0:T(8,128)S(1)}, f32[16,16,128]{2,1,0:T(8,128)S(1)}, u32[]{:S(2)}, u32[]{:S(2)}) %collective-permute-start.2) | collective-permute-done | bytes 131104 | tf_op jit(solution)/shard_map/ppermute | solution.py:649
  11.6 0.1 send_first.1
  11.7 0.1 collective-permute-start.4
  11.8 5.9 %collective-permute-start.5 = (f32[16,256]{1,0:T(8,128)S(1)}, f32[16,256]{1,0:T(8,128)S(1)}, u32[]{:S(2)}, u32[]{:S(2)}) collective-permute-start(f32[16,256]{1,0:T(8,128)S(1)} %get-tuple-element.54), channel_id=1, source_target_pairs={{32,0},{64,32},{96,64},{128,96},{160,128},{192,160},{224,192},{0,2... | collective-permute-start | bytes 49160 | tf_op jit(solution)/shard_map/ppermute | solution.py:654
  17.7 1.4 collective-permute-done.5.refs_5_.plane
  19.2 0.1 send_x.1
  19.3 0.1 collective-permute-start.6
  19.4 3.8 %collective-permute-start.7 = (f32[18,32,128]{2,1,0:T(8,128)S(1)}, f32[18,32,128]{2,1,0:T(8,128)S(1)}, u32[]{:S(2)}, u32[]{:S(2)}) collective-permute-start(f32[18,32,128]{2,1,0:T(8,128)S(1)} %get-tuple-element.56), channel_id=1, source_target_pairs={{32,0},{64,32},{96,64},{128,96},{160,128},{192,160},{224,192},{0,2... | collective-permute-start | bytes 884744 | tf_op jit(solution)/shard_map/ppermute | solution.py:654
  23.2 0.1 pad_add_fusion.where.refs_0_
  23.2 2.3 %own_faces_0.1.refs_6_ = f32[48,8,128]{2,1,0:T(8,128)S(1)} custom-call(s32[3]{0:T(128)S(1)} %pad_add_fusion.where.refs_0_, s32[32,16,128]{2,1,0:T(8,128)S(1)} %copy-done.1, f32[16,16,128]{2,1,0:T(8,128)S(1)} %collective-permute-done.2.below, f32[16,16,128]{2,1,0:T(8,128)S(1)} %collective-permute-done.3.above, ...), custom_call_target="tpu_custom_call" | custom-call | bytes 7000000 | tf_op jit(solution)/shard_map/own_faces_0/pallas_call | solution.py:634
  25.5 0.1 collective-permute-start.8
  25.6 7.6 %collective-permute-done.8.refs_7_ = f32[48,8,128]{2,1,0:T(8,128)S(1)} collective-permute-done((f32[48,8,128]{2,1,0:T(8,128)S(1)}, f32[48,8,128]{2,1,0:T(8,128)S(1)}, u32[]{:S(2)}, u32[]{:S(2)}) %collective-permute-start.8) | collective-permute-done | bytes 196640 | tf_op jit(solution)/shard_map/ppermute | solution.py:654
  33.3 0.5 send_z.1
  33.8 2.9 %collective-permute-start.10 = (f32[51,32,128]{2,1,0:T(8,128)S(1)}, f32[51,32,128]{2,1,0:T(8,128)S(1)}, u32[]{:S(2)}, u32[]{:S(2)}) collective-permute-start(f32[51,32,128]{2,1,0:T(8,128)S(1)} %get-tuple-element.58), channel_id=1, source_target_pairs={{1,0},{2,1},{3,2},{4,3},{5,4},{6,5},{7,6},{0,7},{9,8},{10,9},{11,1... | collective-permute-start | bytes 2506760 | tf_op jit(solution)/shard_map/ppermute | solution.py:654
  36.7 1.1 collective-permute-start.12
  37.9 6.1 %collective-permute-done.12 = f32[48,8,128]{2,1,0:T(8,128)S(1)} collective-permute-done((f32[48,8,128]{2,1,0:T(8,128)S(1)}, f32[48,8,128]{2,1,0:T(8,128)S(1)}, u32[]{:S(2)}, u32[]{:S(2)}) %collective-permute-start.12) | collective-permute-done | bytes 196640 | tf_op jit(solution)/shard_map/ppermute | solution.py:654
  43.9 1.1 collective-permute-done.11
  45.0 0.1 pad_maximum_fusion.refs_9_.own
  45.1 1.8 %collective-permute-start.19 = (f32[48,32,128]{2,1,0:T(8,128)S(1)}, f32[48,32,128]{2,1,0:T(8,128)S(1)}, u32[]{:S(2)}, u32[]{:S(2)}) collective-permute-start(f32[48,32,128]{2,1,0:T(8,128)S(1)} %pad_maximum_fusion.refs_9_.own), channel_id=1, source_target_pairs={{32,0},{64,32},{96,64},{128,96},{160,128},{192,160},{224,192},{0,2... | collective-permute-start | bytes 2359304 | tf_op jit(solution)/shard_map/ppermute | solution.py:654
  46.9 0.3 collective-permute-start.18
  47.2 5.1 %faces_0.1 = (f32[48,32,256]{2,1,0:T(8,128)S(1)}, f32[48,32,256]{2,1,0:T(8,128)S(1)}, f32[48,32,256]{2,1,0:T(8,128)S(1)}, f32[48,32,256]{2,1,0:T(8,128)S(1)}, f32[48,32,256]{2,1,0:T(8,128)S(1)}) custom-call(s32[3]{0:T(128)S(1)} %pad_add_fusion.where.refs_0_, f32[68,8,128]{2,1,0:T(8,128)S(1)} %get-tuple-element.51.refs_0_.refs_1_.lower, ...), custom_call_target="tpu_custom_call" | custom-call | bytes 14000000 | tf_op jit(solution)/shard_map/faces_0/pallas_call | solution.py:634
  52.4 4.2 %begin.1 = (f32[48,32,256]{2,1,0:T(8,128)S(1)}, f32[32,16,128]{2,1,0:T(8,128)S(1)}, f32[16,8,128]{2,1,0:T(8,128)S(1)}) custom-call(f32[68,8,128]{2,1,0:T(8,128)S(1)} %get-tuple-element.51.refs_0_.refs_1_.lower, f32[68,8,128]{2,1,0:T(8,128)S(1)} %get-tuple-element.52.refs_1_.refs_2_.upper, f32[68,8,128]{2,1,0:T(8,128)S(1)} %collective-permute-done.refs_2_.refs_3_.below, ...), custom_call_target="tpu_custom_call" | custom-call | bytes 21000000 | tf_op jit(solution)/shard_map/begin/pallas_call | solution.py:634
  56.6 4.1 %collective-permute-start.15 = (f32[16,8,128]{2,1,0:T(8,128)S(1)}, f32[16,8,128]{2,1,0:T(8,128)S(1)}, u32[]{:S(2)}, u32[]{:S(2)}) collective-permute-start(f32[16,8,128]{2,1,0:T(8,128)S(1)} %get-tuple-element.64), channel_id=1, source_target_pairs={{24,0},{0,8},{8,16},{16,24},{25,1},{1,9},{9,17},{17,25},{26,2},{2,... | collective-permute-start | bytes 196616 | tf_op jit(solution)/shard_map/ppermute | solution.py:654
  60.6 1.0 collective-permute-start.13
  61.6 5.2 %collective-permute-done.13 = f32[16,8,128]{2,1,0:T(8,128)S(1)} collective-permute-done((f32[16,8,128]{2,1,0:T(8,128)S(1)}, f32[16,8,128]{2,1,0:T(8,128)S(1)}, u32[]{:S(2)}, u32[]{:S(2)}) %collective-permute-start.13) | collective-permute-done | bytes 65568 | tf_op jit(solution)/shard_map/ppermute | solution.py:654
  66.9 2.9 %collective-permute-start.17 = (f32[16,32,128]{2,1,0:T(8,128)S(1)}, f32[16,32,128]{2,1,0:T(8,128)S(1)}, u32[]{:S(2)}, u32[]{:S(2)}) collective-permute-start(f32[16,32,128]{2,1,0:T(8,128)S(1)} %constant_dynamic-update-slice_fusion.own), channel_id=1, source_target_pairs={{32,0},{64,32},{96,64},{128,96},{160,128},{192,160},{224,192},{0,2... | collective-permute-start | bytes 786440 | tf_op jit(solution)/shard_map/ppermute | solution.py:654
  69.8 3.2 %faces_1.1 = (f32[48,32,128]{2,1,0:T(8,128)S(1)}, f32[48,32,128]{2,1,0:T(8,128)S(1)}, f32[48,32,128]{2,1,0:T(8,128)S(1)}, f32[48,32,128]{2,1,0:T(8,128)S(1)}, f3...) custom-call(s32[3]{0:T(128)S(1)} %pad_add_fusion.where.refs_0_, ...), custom_call_target="tpu_custom_call" | custom-call | bytes 10500000 | tf_op jit(solution)/shard_map/faces_1/pallas_call | solution.py:634
  73.1 0.6 collective-permute-done.17.above
  73.7 3.7 %collective-permute-done.16.below = f32[16,32,128]{2,1,0:T(8,128)S(1)} collective-permute-done((f32[16,32,128]{2,1,0:T(8,128)S(1)}, f32[16,32,128]{2,1,0:T(8,128)S(1)}, u32[]{:S(2)}, u32[]{:S(2)}) %collective-permute-start.16) | collective-permute-done | bytes 262176 | tf_op jit(solution)/shard_map/ppermute | solution.py:649
  77.4 2.8 %down.2 = (f32[48,32,128]{2,1,0:T(8,128)S(1)}, f32[48,32,128]{2,1,0:T(8,128)S(1)}, f32[24,16,128]{2,1,0:T(8,128)S(1)}, f32[24,16,128]{2,1,0:T(8,128)S(1)}, f32[10,8,128]{2,1,0:T(8,128)S(1)}) custom-call(f32[16,32,128]{2,1,0:T(8,128)S(1)} %constant_dynamic-update-slice_fusion.own, f32[16,32,128]{2,1,0:T(8,128)S(1)} %collective-permute-done.16.below, ...), custom_call_target="tpu_custom_call" | custom-call | bytes 14000000 | tf_op jit(solution)/shard_map/down/pallas_call | solution.py:634
  80.3 0.6 collective-permute-start.20
  80.9 1.2 collective-permute-done.21.above
  82.0 3.0 %collective-permute-done.20.below = f32[10,8,128]{2,1,0:T(8,128)S(1)} collective-permute-done((f32[10,8,128]{2,1,0:T(8,128)S(1)}, f32[10,8,128]{2,1,0:T(8,128)S(1)}, u32[]{:S(2)}, u32[]{:S(2)}) %collective-permute-start.20) | collective-permute-done | bytes 40992 | tf_op jit(solution)/shard_map/ppermute | solution.py:649
  85.0 0.2 spread.2.own3
  85.2 0.1 collective-permute-start.23
  85.3 2.9 %collective-permute-start.22 = (f32[20,8,128]{2,1,0:T(8,128)S(1)}, f32[20,8,128]{2,1,0:T(8,128)S(1)}, u32[]{:S(2)}, u32[]{:S(2)}) collective-permute-start(f32[20,8,128]{2,1,0:T(8,128)S(1)} %spread.2.own3), channel_id=1, source_target_pairs={{0,64},{32,96},{64,128},{96,160},{128,192},{160,224},{192,0},{224,... | collective-permute-start | bytes 245768 | tf_op jit(solution)/shard_map/ppermute | solution.py:649
  88.2 2.4 %collective-permute-done.23.above3 = f32[20,8,128]{2,1,0:T(8,128)S(1)} collective-permute-done((f32[20,8,128]{2,1,0:T(8,128)S(1)}, f32[20,8,128]{2,1,0:T(8,128)S(1)}, u32[]{:S(2)}, u32[]{:S(2)}) %collective-permute-start.23) | collective-permute-done | bytes 81952 | tf_op jit(solution)/shard_map/ppermute | solution.py:654
  90.6 1.6 %collective-permute-done.22.below3 = f32[20,8,128]{2,1,0:T(8,128)S(1)} collective-permute-done((f32[20,8,128]{2,1,0:T(8,128)S(1)}, f32[20,8,128]{2,1,0:T(8,128)S(1)}, u32[]{:S(2)}, u32[]{:S(2)}) %collective-permute-start.22) | collective-permute-done | bytes 81952 | tf_op jit(solution)/shard_map/ppermute | solution.py:649
  92.2 12.3 %up.1 = (f32[26,8,128]{2,1,0:T(8,128)S(1)}, f32[26,8,128]{2,1,0:T(8,128)S(1)}, f32[26,8,128]{2,1,0:T(8,128)S(1)}, f32[26,8,128]{2,1,0:T(8,128)S(1)}, f32[26,8,12...) custom-call(s32[3]{0:T(128)S(1)} %pad_add_fusion.where.refs_0_, ...), custom_call_target="tpu_custom_call" | custom-call | bytes 52500000 | tf_op jit(solution)/shard_map/up/pallas_call | solution.py:634
  104.5 0.9 collective-permute-start.26
  105.5 0.9 collective-permute-start.25
  106.3 1.3 collective-permute-start.24
  107.6 4.3 %collective-permute-done.24 = f32[16,8,128]{2,1,0:T(8,128)S(1)} collective-permute-done((f32[16,8,128]{2,1,0:T(8,128)S(1)}, f32[16,8,128]{2,1,0:T(8,128)S(1)}, u32[]{:S(2)}, u32[]{:S(2)}) %collective-permute-start.24) | collective-permute-done | bytes 65568 | tf_op jit(solution)/shard_map/ppermute | solution.py:654
  112.0 0.1 collective-permute-start.28
  112.1 2.0 %collective-permute-start.27 = (f32[16,32,128]{2,1,0:T(8,128)S(1)}, f32[16,32,128]{2,1,0:T(8,128)S(1)}, u32[]{:S(2)}, u32[]{:S(2)}) collective-permute-start(f32[16,32,128]{2,1,0:T(8,128)S(1)} %constant_dynamic-update-slice_fusion.4.own), channel_id=1, source_target_pairs={{0,32},{32,64},{64,96},{96,128},{128,160},{160,192},{192,224},{224... | collective-permute-start | bytes 786440 | tf_op jit(solution)/shard_map/ppermute | solution.py:649
  114.1 4.3 %collective-permute-done.28.above = f32[16,32,128]{2,1,0:T(8,128)S(1)} collective-permute-done((f32[16,32,128]{2,1,0:T(8,128)S(1)}, f32[16,32,128]{2,1,0:T(8,128)S(1)}, u32[]{:S(2)}, u32[]{:S(2)}) %collective-permute-start.28) | collective-permute-done | bytes 262176 | tf_op jit(solution)/shard_map/ppermute | solution.py:654
  118.4 1.3 collective-permute-done.27.below
  119.7 2.8 %down.3 = (f32[48,32,128]{2,1,0:T(8,128)S(1)}, f32[48,32,128]{2,1,0:T(8,128)S(1)}, f32[24,16,128]{2,1,0:T(8,128)S(1)}, f32[24,16,128]{2,1,0:T(8,128)S(1)}, f32[8,8,128]{2,1,0:T(8,128)S(1)}) custom-call(f32[16,32,128]{2,1,0:T(8,128)S(1)} %constant_dynamic-update-slice_fusion.4.own, f32[16,32,128]{2,1,0:T(8,128)S(1)} %collective-permute-done.27.below, ...), custom_call_target="tpu_custom_call" | custom-call | bytes 14000000 | tf_op jit(solution)/shard_map/down/pallas_call | solution.py:634
  122.6 0.6 collective-permute-start.29
  123.2 1.1 collective-permute-done.30.above
  124.3 3.0 %collective-permute-done.29.below = f32[8,8,128]{2,1,0:T(8,128)S(1)} collective-permute-done((f32[8,8,128]{2,1,0:T(8,128)S(1)}, f32[8,8,128]{2,1,0:T(8,128)S(1)}, u32[]{:S(2)}, u32[]{:S(2)}) %collective-permute-start.29) | collective-permute-done | bytes 32800 | tf_op jit(solution)/shard_map/ppermute | solution.py:649
  127.2 0.1 spread.3.own3
  127.3 2.5 %collective-permute-start.32 = (f32[8,8,128]{2,1,0:T(8,128)S(1)}, f32[8,8,128]{2,1,0:T(8,128)S(1)}, u32[]{:S(2)}, u32[]{:S(2)}) collective-permute-start(f32[8,8,128]{2,1,0:T(8,128)S(1)} %spread.3.own3), channel_id=1, source_target_pairs={{64,0},{96,32},{128,64},{160,96},{192,128},{224,160},{0,192},{32,2... | collective-permute-start | bytes 98312 | tf_op jit(solution)/shard_map/ppermute | solution.py:654
  129.8 0.5 collective-permute-start.31
  130.3 1.9 %collective-permute-done.32.above3 = f32[8,8,128]{2,1,0:T(8,128)S(1)} collective-permute-done((f32[8,8,128]{2,1,0:T(8,128)S(1)}, f32[8,8,128]{2,1,0:T(8,128)S(1)}, u32[]{:S(2)}, u32[]{:S(2)}) %collective-permute-start.32) | collective-permute-done | bytes 32800 | tf_op jit(solution)/shard_map/ppermute | solution.py:654
  132.2 3.6 %collective-permute-done.31.below3 = f32[8,8,128]{2,1,0:T(8,128)S(1)} collective-permute-done((f32[8,8,128]{2,1,0:T(8,128)S(1)}, f32[8,8,128]{2,1,0:T(8,128)S(1)}, u32[]{:S(2)}, u32[]{:S(2)}) %collective-permute-start.31) | collective-permute-done | bytes 32800 | tf_op jit(solution)/shard_map/ppermute | solution.py:649
  135.9 8.5 %up_last.1 = (f32[32,16,128]{2,1,0:T(8,128)}, f32[32,16,128]{2,1,0:T(8,128)}) custom-call(s32[3]{0:T(128)S(1)} %pad_add_fusion.where.refs_0_, f32[8,8,128]{2,1,0:T(8,128)S(1)} %spread.3.own3, f32[8,8,128]{2,1,0:T(8,128)S(1)} %collective-permute-done.31.below3, f32[8,8,128]{2,1,0:T(8,128)S(1)} %collective-permute-done.32.above3, ...), custom_call_target="tpu_custom_call" | custom-call | bytes 35000000 | tf_op jit(solution)/shard_map/up_last/pallas_call | solution.py:634
  (33 shorter events, 0.2 us)
Async XLA Ops:
  0.6 1.0 copy-start
  1.6 21.7 %copy-start.1 = (s32[32,16,128]{2,1,0:T(8,128)S(1)}, s32[32,16,128]{2,1,0:T(8,128)}, u32[]{:S(2)}) copy-start(s32[32,16,128]{2,1,0:T(8,128)} %mask.5) | copy-start | bytes 786436
  1.7 1.0 copy-start.2
  2.7 16.5 %collective-permute-start.1 = (f32[68,8,128]{2,1,0:T(8,128)S(1)}, f32[68,8,128]{2,1,0:T(8,128)S(1)}, u32[]{:S(2)}, u32[]{:S(2)}) collective-permute-start(f32[68,8,128]{2,1,0:T(8,128)S(1)} %get-tuple-element.51.refs_0_.refs_1_.lower), channel_id=1, source_target_pairs={{8,0},{16,8},{24,16},{0,24},{9,1},{17,9},{25,17},{1,25},{10,2},{18... | collective-permute-start | bytes 835592 | tf_op jit(solution)/shard_map/ppermute | solution.py:654
  3.6 15.6 %collective-permute-start = (f32[68,8,128]{2,1,0:T(8,128)S(1)}, f32[68,8,128]{2,1,0:T(8,128)S(1)}, u32[]{:S(2)}, u32[]{:S(2)}) collective-permute-start(f32[68,8,128]{2,1,0:T(8,128)S(1)} %get-tuple-element.52.refs_1_.refs_2_.upper), channel_id=1, source_target_pairs={{0,8},{8,16},{16,24},{24,0},{1,9},{9,17},{17,25},{25,1},{2,10},{10... | collective-permute-start | bytes 835592 | tf_op jit(solution)/shard_map/ppermute | solution.py:649
  6.0 5.6 %collective-permute-start.2 = (f32[16,16,128]{2,1,0:T(8,128)S(1)}, f32[16,16,128]{2,1,0:T(8,128)S(1)}, u32[]{:S(2)}, u32[]{:S(2)}) collective-permute-start(f32[16,16,128]{2,1,0:T(8,128)S(1)} %get-tuple-element.49.refs_2_), channel_id=1, source_target_pairs={{0,1},{1,2},{2,3},{3,4},{4,5},{5,6},{6,7},{7,0},{8,9},{9,10},{10,1... | collective-permute-start | bytes 393224 | tf_op jit(solution)/shard_map/ppermute | solution.py:649
  6.0 5.6 %collective-permute-start.3 = (f32[16,16,128]{2,1,0:T(8,128)S(1)}, f32[16,16,128]{2,1,0:T(8,128)S(1)}, u32[]{:S(2)}, u32[]{:S(2)}) collective-permute-start(f32[16,16,128]{2,1,0:T(8,128)S(1)} %get-tuple-element.50.refs_3_), channel_id=1, source_target_pairs={{1,0},{2,1},{3,2},{4,3},{5,4},{6,5},{7,6},{0,7},{9,8},{10,9},{11,1... | collective-permute-start | bytes 393224 | tf_op jit(solution)/shard_map/ppermute | solution.py:654
  11.7 7.5 %collective-permute-start.4 = (f32[32,256]{1,0:T(8,128)S(1)}, f32[32,256]{1,0:T(8,128)S(1)}, u32[]{:S(2)}, u32[]{:S(2)}) collective-permute-start(f32[32,256]{1,0:T(8,128)S(1)} %get-tuple-element.53), channel_id=1, source_target_pairs={{8,0},{16,8},{24,16},{0,24},{9,1},{17,9},{25,17},{1,25},{10,2},{18... | collective-permute-start | bytes 98312 | tf_op jit(solution)/shard_map/ppermute | solution.py:654
  11.8 7.4 %collective-permute-start.5 = (f32[16,256]{1,0:T(8,128)S(1)}, f32[16,256]{1,0:T(8,128)S(1)}, u32[]{:S(2)}, u32[]{:S(2)}) collective-permute-start(f32[16,256]{1,0:T(8,128)S(1)} %get-tuple-element.54), channel_id=1, source_target_pairs={{32,0},{64,32},{96,64},{128,96},{160,128},{192,160},{224,192},{0,2... | collective-permute-start | bytes 49160 | tf_op jit(solution)/shard_map/ppermute | solution.py:654
  19.3 14.0 %collective-permute-start.6 = (f32[18,32,128]{2,1,0:T(8,128)S(1)}, f32[18,32,128]{2,1,0:T(8,128)S(1)}, u32[]{:S(2)}, u32[]{:S(2)}) collective-permute-start(f32[18,32,128]{2,1,0:T(8,128)S(1)} %get-tuple-element.55), channel_id=1, source_target_pairs={{0,32},{32,64},{64,96},{96,128},{128,160},{160,192},{192,224},{224... | collective-permute-start | bytes 884744 | tf_op jit(solution)/shard_map/ppermute | solution.py:649
  19.4 13.9 %collective-permute-start.7 = (f32[18,32,128]{2,1,0:T(8,128)S(1)}, f32[18,32,128]{2,1,0:T(8,128)S(1)}, u32[]{:S(2)}, u32[]{:S(2)}) collective-permute-start(f32[18,32,128]{2,1,0:T(8,128)S(1)} %get-tuple-element.56), channel_id=1, source_target_pairs={{32,0},{64,32},{96,64},{128,96},{160,128},{192,160},{224,192},{0,2... | collective-permute-start | bytes 884744 | tf_op jit(solution)/shard_map/ppermute | solution.py:654
  25.5 7.7 %collective-permute-start.8 = (f32[48,8,128]{2,1,0:T(8,128)S(1)}, f32[48,8,128]{2,1,0:T(8,128)S(1)}, u32[]{:S(2)}, u32[]{:S(2)}) collective-permute-start(f32[48,8,128]{2,1,0:T(8,128)S(1)} %own_faces_0.1.refs_6_), channel_id=1, source_target_pairs={{8,0},{16,8},{24,16},{0,24},{9,1},{17,9},{25,17},{1,25},{10,2},{18... | collective-permute-start | bytes 589832 | tf_op jit(solution)/shard_map/ppermute | solution.py:654
  33.8 13.4 %collective-permute-start.9 = (f32[51,32,128]{2,1,0:T(8,128)S(1)}, f32[51,32,128]{2,1,0:T(8,128)S(1)}, u32[]{:S(2)}, u32[]{:S(2)}) collective-permute-start(f32[51,32,128]{2,1,0:T(8,128)S(1)} %get-tuple-element.57), channel_id=1, source_target_pairs={{0,1},{1,2},{2,3},{3,4},{4,5},{5,6},{6,7},{7,0},{8,9},{9,10},{10,1... | collective-permute-start | bytes 2506760 | tf_op jit(solution)/shard_map/ppermute | solution.py:649
  33.8 13.4 %collective-permute-start.10 = (f32[51,32,128]{2,1,0:T(8,128)S(1)}, f32[51,32,128]{2,1,0:T(8,128)S(1)}, u32[]{:S(2)}, u32[]{:S(2)}) collective-permute-start(f32[51,32,128]{2,1,0:T(8,128)S(1)} %get-tuple-element.58), channel_id=1, source_target_pairs={{1,0},{2,1},{3,2},{4,3},{5,4},{6,5},{7,6},{0,7},{9,8},{10,9},{11,1... | collective-permute-start | bytes 2506760 | tf_op jit(solution)/shard_map/ppermute | solution.py:654
  36.7 7.2 %collective-permute-start.12 = (f32[48,8,128]{2,1,0:T(8,128)S(1)}, f32[48,8,128]{2,1,0:T(8,128)S(1)}, u32[]{:S(2)}, u32[]{:S(2)}) collective-permute-start(f32[48,8,128]{2,1,0:T(8,128)S(1)} %own_faces_0.1.refs_6_), channel_id=1, source_target_pairs={{24,0},{0,8},{8,16},{16,24},{25,1},{1,9},{9,17},{17,25},{26,2},{2,... | collective-permute-start | bytes 589832 | tf_op jit(solution)/shard_map/ppermute | solution.py:654
  37.9 7.2 %collective-permute-start.11 = (f32[48,8,128]{2,1,0:T(8,128)S(1)}, f32[48,8,128]{2,1,0:T(8,128)S(1)}, u32[]{:S(2)}, u32[]{:S(2)}) collective-permute-start(f32[48,8,128]{2,1,0:T(8,128)S(1)} %own_faces_0.1.refs_6_), channel_id=1, source_target_pairs={{16,0},{24,8},{0,16},{8,24},{17,1},{25,9},{1,17},{9,25},{18,2},{26... | collective-permute-start | bytes 589832 | tf_op jit(solution)/shard_map/ppermute | solution.py:654
  45.1 24.7 %collective-permute-start.19 = (f32[48,32,128]{2,1,0:T(8,128)S(1)}, f32[48,32,128]{2,1,0:T(8,128)S(1)}, u32[]{:S(2)}, u32[]{:S(2)}) collective-permute-start(f32[48,32,128]{2,1,0:T(8,128)S(1)} %pad_maximum_fusion.refs_9_.own), channel_id=1, source_target_pairs={{32,0},{64,32},{96,64},{128,96},{160,128},{192,160},{224,192},{0,2... | collective-permute-start | bytes 2359304 | tf_op jit(solution)/shard_map/ppermute | solution.py:654
  46.9 22.9 %collective-permute-start.18 = (f32[48,32,128]{2,1,0:T(8,128)S(1)}, f32[48,32,128]{2,1,0:T(8,128)S(1)}, u32[]{:S(2)}, u32[]{:S(2)}) collective-permute-start(f32[48,32,128]{2,1,0:T(8,128)S(1)} %pad_maximum_fusion.refs_9_.own), channel_id=1, source_target_pairs={{0,32},{32,64},{64,96},{96,128},{128,160},{160,192},{192,224},{224... | collective-permute-start | bytes 2359304 | tf_op jit(solution)/shard_map/ppermute | solution.py:649
  56.6 10.3 %collective-permute-start.15 = (f32[16,8,128]{2,1,0:T(8,128)S(1)}, f32[16,8,128]{2,1,0:T(8,128)S(1)}, u32[]{:S(2)}, u32[]{:S(2)}) collective-permute-start(f32[16,8,128]{2,1,0:T(8,128)S(1)} %get-tuple-element.64), channel_id=1, source_target_pairs={{24,0},{0,8},{8,16},{16,24},{25,1},{1,9},{9,17},{17,25},{26,2},{2,... | collective-permute-start | bytes 196616 | tf_op jit(solution)/shard_map/ppermute | solution.py:654
  60.6 6.2 %collective-permute-start.14 = (f32[16,8,128]{2,1,0:T(8,128)S(1)}, f32[16,8,128]{2,1,0:T(8,128)S(1)}, u32[]{:S(2)}, u32[]{:S(2)}) collective-permute-start(f32[16,8,128]{2,1,0:T(8,128)S(1)} %get-tuple-element.64), channel_id=1, source_target_pairs={{16,0},{24,8},{0,16},{8,24},{17,1},{25,9},{1,17},{9,25},{18,2},{26... | collective-permute-start | bytes 196616 | tf_op jit(solution)/shard_map/ppermute | solution.py:654
  60.6 6.2 %collective-permute-start.13 = (f32[16,8,128]{2,1,0:T(8,128)S(1)}, f32[16,8,128]{2,1,0:T(8,128)S(1)}, u32[]{:S(2)}, u32[]{:S(2)}) collective-permute-start(f32[16,8,128]{2,1,0:T(8,128)S(1)} %get-tuple-element.64), channel_id=1, source_target_pairs={{8,0},{16,8},{24,16},{0,24},{9,1},{17,9},{25,17},{1,25},{10,2},{18... | collective-permute-start | bytes 196616 | tf_op jit(solution)/shard_map/ppermute | solution.py:654
  66.9 6.8 %collective-permute-start.17 = (f32[16,32,128]{2,1,0:T(8,128)S(1)}, f32[16,32,128]{2,1,0:T(8,128)S(1)}, u32[]{:S(2)}, u32[]{:S(2)}) collective-permute-start(f32[16,32,128]{2,1,0:T(8,128)S(1)} %constant_dynamic-update-slice_fusion.own), channel_id=1, source_target_pairs={{32,0},{64,32},{96,64},{128,96},{160,128},{192,160},{224,192},{0,2... | collective-permute-start | bytes 786440 | tf_op jit(solution)/shard_map/ppermute | solution.py:654
  69.8 7.6 %collective-permute-start.16 = (f32[16,32,128]{2,1,0:T(8,128)S(1)}, f32[16,32,128]{2,1,0:T(8,128)S(1)}, u32[]{:S(2)}, u32[]{:S(2)}) collective-permute-start(f32[16,32,128]{2,1,0:T(8,128)S(1)} %constant_dynamic-update-slice_fusion.own), channel_id=1, source_target_pairs={{0,32},{32,64},{64,96},{96,128},{128,160},{160,192},{192,224},{224... | collective-permute-start | bytes 786440 | tf_op jit(solution)/shard_map/ppermute | solution.py:649
  80.2 1.8 %collective-permute-start.21 = (f32[10,8,128]{2,1,0:T(8,128)S(1)}, f32[10,8,128]{2,1,0:T(8,128)S(1)}, u32[]{:S(2)}, u32[]{:S(2)}) collective-permute-start(f32[10,8,128]{2,1,0:T(8,128)S(1)} %get-tuple-element.76.own), channel_id=1, source_target_pairs={{1,0},{2,1},{3,2},{4,3},{5,4},{6,5},{7,6},{0,7},{9,8},{10,9},{11,1... | collective-permute-start | bytes 122888 | tf_op jit(solution)/shard_map/ppermute | solution.py:654
  80.3 4.7 %collective-permute-start.20 = (f32[10,8,128]{2,1,0:T(8,128)S(1)}, f32[10,8,128]{2,1,0:T(8,128)S(1)}, u32[]{:S(2)}, u32[]{:S(2)}) collective-permute-start(f32[10,8,128]{2,1,0:T(8,128)S(1)} %get-tuple-element.76.own), channel_id=1, source_target_pairs={{0,1},{1,2},{2,3},{3,4},{4,5},{5,6},{6,7},{7,0},{8,9},{9,10},{10,1... | collective-permute-start | bytes 122888 | tf_op jit(solution)/shard_map/ppermute | solution.py:649
  85.2 5.4 %collective-permute-start.23 = (f32[20,8,128]{2,1,0:T(8,128)S(1)}, f32[20,8,128]{2,1,0:T(8,128)S(1)}, u32[]{:S(2)}, u32[]{:S(2)}) collective-permute-start(f32[20,8,128]{2,1,0:T(8,128)S(1)} %spread.2.own3), channel_id=1, source_target_pairs={{64,0},{96,32},{128,64},{160,96},{192,128},{224,160},{0,192},{32,2... | collective-permute-start | bytes 245768 | tf_op jit(solution)/shard_map/ppermute | solution.py:654
  85.3 7.0 %collective-permute-start.22 = (f32[20,8,128]{2,1,0:T(8,128)S(1)}, f32[20,8,128]{2,1,0:T(8,128)S(1)}, u32[]{:S(2)}, u32[]{:S(2)}) collective-permute-start(f32[20,8,128]{2,1,0:T(8,128)S(1)} %spread.2.own3), channel_id=1, source_target_pairs={{0,64},{32,96},{64,128},{96,160},{128,192},{160,224},{192,0},{224,... | collective-permute-start | bytes 245768 | tf_op jit(solution)/shard_map/ppermute | solution.py:649
  104.5 7.4 %collective-permute-start.26 = (f32[16,8,128]{2,1,0:T(8,128)S(1)}, f32[16,8,128]{2,1,0:T(8,128)S(1)}, u32[]{:S(2)}, u32[]{:S(2)}) collective-permute-start(f32[16,8,128]{2,1,0:T(8,128)S(1)} %get-tuple-element.83), channel_id=1, source_target_pairs={{24,0},{0,8},{8,16},{16,24},{25,1},{1,9},{9,17},{17,25},{26,2},{2,... | collective-permute-start | bytes 196616 | tf_op jit(solution)/shard_map/ppermute | solution.py:654
  105.5 6.5 %collective-permute-start.25 = (f32[16,8,128]{2,1,0:T(8,128)S(1)}, f32[16,8,128]{2,1,0:T(8,128)S(1)}, u32[]{:S(2)}, u32[]{:S(2)}) collective-permute-start(f32[16,8,128]{2,1,0:T(8,128)S(1)} %get-tuple-element.83), channel_id=1, source_target_pairs={{16,0},{24,8},{0,16},{8,24},{17,1},{25,9},{1,17},{9,25},{18,2},{26... | collective-permute-start | bytes 196616 | tf_op jit(solution)/shard_map/ppermute | solution.py:654
  106.3 5.6 %collective-permute-start.24 = (f32[16,8,128]{2,1,0:T(8,128)S(1)}, f32[16,8,128]{2,1,0:T(8,128)S(1)}, u32[]{:S(2)}, u32[]{:S(2)}) collective-permute-start(f32[16,8,128]{2,1,0:T(8,128)S(1)} %get-tuple-element.83), channel_id=1, source_target_pairs={{8,0},{16,8},{24,16},{0,24},{9,1},{17,9},{25,17},{1,25},{10,2},{18... | collective-permute-start | bytes 196616 | tf_op jit(solution)/shard_map/ppermute | solution.py:654
  112.0 6.5 %collective-permute-start.28 = (f32[16,32,128]{2,1,0:T(8,128)S(1)}, f32[16,32,128]{2,1,0:T(8,128)S(1)}, u32[]{:S(2)}, u32[]{:S(2)}) collective-permute-start(f32[16,32,128]{2,1,0:T(8,128)S(1)} %constant_dynamic-update-slice_fusion.4.own), channel_id=1, source_target_pairs={{32,0},{64,32},{96,64},{128,96},{160,128},{192,160},{224,192},{0,2... | collective-permute-start | bytes 786440 | tf_op jit(solution)/shard_map/ppermute | solution.py:654
  112.1 7.6 %collective-permute-start.27 = (f32[16,32,128]{2,1,0:T(8,128)S(1)}, f32[16,32,128]{2,1,0:T(8,128)S(1)}, u32[]{:S(2)}, u32[]{:S(2)}) collective-permute-start(f32[16,32,128]{2,1,0:T(8,128)S(1)} %constant_dynamic-update-slice_fusion.4.own), channel_id=1, source_target_pairs={{0,32},{32,64},{64,96},{96,128},{128,160},{160,192},{192,224},{224... | collective-permute-start | bytes 786440 | tf_op jit(solution)/shard_map/ppermute | solution.py:649
  122.6 1.7 %collective-permute-start.30 = (f32[8,8,128]{2,1,0:T(8,128)S(1)}, f32[8,8,128]{2,1,0:T(8,128)S(1)}, u32[]{:S(2)}, u32[]{:S(2)}) collective-permute-start(f32[8,8,128]{2,1,0:T(8,128)S(1)} %get-tuple-element.84.own), channel_id=1, source_target_pairs={{1,0},{2,1},{3,2},{4,3},{5,4},{6,5},{7,6},{0,7},{9,8},{10,9},{11,1... | collective-permute-start | bytes 98312 | tf_op jit(solution)/shard_map/ppermute | solution.py:654
  122.6 4.6 %collective-permute-start.29 = (f32[8,8,128]{2,1,0:T(8,128)S(1)}, f32[8,8,128]{2,1,0:T(8,128)S(1)}, u32[]{:S(2)}, u32[]{:S(2)}) collective-permute-start(f32[8,8,128]{2,1,0:T(8,128)S(1)} %get-tuple-element.84.own), channel_id=1, source_target_pairs={{0,1},{1,2},{2,3},{3,4},{4,5},{5,6},{6,7},{7,0},{8,9},{9,10},{10,1... | collective-permute-start | bytes 98312 | tf_op jit(solution)/shard_map/ppermute | solution.py:649
  127.3 4.9 %collective-permute-start.32 = (f32[8,8,128]{2,1,0:T(8,128)S(1)}, f32[8,8,128]{2,1,0:T(8,128)S(1)}, u32[]{:S(2)}, u32[]{:S(2)}) collective-permute-start(f32[8,8,128]{2,1,0:T(8,128)S(1)} %spread.3.own3), channel_id=1, source_target_pairs={{64,0},{96,32},{128,64},{160,96},{192,128},{224,160},{0,192},{32,2... | collective-permute-start | bytes 98312 | tf_op jit(solution)/shard_map/ppermute | solution.py:654
  129.8 6.0 %collective-permute-start.31 = (f32[8,8,128]{2,1,0:T(8,128)S(1)}, f32[8,8,128]{2,1,0:T(8,128)S(1)}, u32[]{:S(2)}, u32[]{:S(2)}) collective-permute-start(f32[8,8,128]{2,1,0:T(8,128)S(1)} %spread.3.own3), channel_id=1, source_target_pairs={{0,64},{32,96},{64,128},{96,160},{128,192},{160,224},{192,0},{224,... | collective-permute-start | bytes 98312 | tf_op jit(solution)/shard_map/ppermute | solution.py:649
where the time goes:
time: 145 us; the launch traced here: 144 us
  waiting for transfers between devices  56.2 us (39%)
  starting transfers between devices  42.9 us (30%)
  Pallas kernels  42.4 us (29%)
  local copies, waits for them, and re-layouts  1.94 us (1%)
    pallas_call x15, Pallas kernels, call(): pl.pallas_call(kernel, out_shape=[jax.ShapeDtypeStruct(s, F32) for s in o...  42.4 us
    ppermute x22, waiting for transfers between devices, from_above(): return lax.ppermute(array, axis, [((i + by) % n, i) for i in range(n)])  37.3 us
    ppermute x22, starting transfers between devices, from_above(): return lax.ppermute(array, axis, [((i + by) % n, i) for i in range(n)])  33.5 us
    ppermute x11, waiting for transfers between devices, from_below(): return lax.ppermute(array, axis, [(i, (i + by) % n) for i in range(n)])  18.8 us
    ppermute x11, starting transfers between devices, from_below(): return lax.ppermute(array, axis, [(i, (i + by) % n) for i in range(n)])  9.38 us
  transfers between devices with their start and end apart: 33, of which 19 were waited for; matrix products, arithmetic and copies ran while one was open for 0% of the time, Pallas kernels for 10%

commit v1 on v0

--- a/solution.py
+++ b/solution.py
@@ -15,7 +15,7 @@
 GAS = 1.0
 
 INTERPRET = False
-VMEM_LIMIT = 28 * 1024 * 1024
+VMEM_LIMIT = 24 * 1024 * 1024
 
 BX, BY, BZ = 32, 16, 128
 WX = 8
@@ -206,49 +206,46 @@
         out[...] = beside(density[0:16], density[16:32], high)
 
 
-def send_first(mask, below, above, row, plane):
+def send_y(r, mask, z_below, z_above, to_upper, to_lower, plane):
     density = density_of(mask)
-    one, two = sides(below, above, slice(0, 16))
+    side = jnp.concatenate(sides(z_below, z_above, slice(0, 16)), 0)
     plane[:, 0:128] = density[0]
-    plane[:, 128:256] = one[0]
-    for x in range(BX):
-        row[x : x + 1, 0:128] = density[x, 0:1]
-        row[x : x + 1, 128:256] = (one[x, 0:1] if x < 16 else two[x - 16, 0:1])
-
-
-def send_y(r, mask, to_upper, to_lower):
-    density = density_of(mask)
+    plane[:, 128:256] = side[0]
     for out, rows, line in ((to_upper, slice(8, 16), 7), (to_lower, slice(0, 8), 8)):
-        out[0:BX] = r[:, rows, :]
-        out[BX : 2 * BX] = density[:, rows]
+        out[0:BX, :, 0:128] = density[:, rows]
+        out[0:BX, :, 128:256] = side[:, rows]
         for x in range(BX):
-            out[2 * BX + x // 8, x % 8 : x % 8 + 1] = density[x, line : line + 1]
+            at = BX + x // 8
+            out[at, x % 8 : x % 8 + 1, 0:128] = density[x, line : line + 1]
+            out[at, x % 8 : x % 8 + 1, 128:256] = side[x, line : line + 1]
+        out[36:52, :, 0:128] = r[0:16, rows]
+        out[36:52, :, 128:256] = r[16:32, rows]
 
 
 def send_x(lower, upper, below, above, to_upper, to_lower):
-    for out, r_at, d_at, pack in ((to_upper, BX - 8, BX - 9, 3), (to_lower, 0, 0, 0)):
+    for out, at, pack, r_at, lanes in ((to_upper, BX - 9, 3, 44, slice(128, 256)), (to_lower, 0, 0, 36, slice(0, 128))):
         for tile, source in enumerate((lower, upper, above, below)):
             rows = slice(8 * tile, 8 * tile + 8)
-            out[0:8, rows] = source[r_at : r_at + 8]
-            out[8:17, rows] = source[BX + d_at : BX + d_at + 9]
-        out[17, 0:8] = below[2 * BX + pack]
-        out[17, 8:16] = above[2 * BX + pack]
-        out[17, 16:32] = jnp.zeros((16, 128), F32)
-
-
-def send_z(lower, upper, below, above, x_below, x_above, to_upper, to_lower):
+            out[0:9, rows] = source[at : at + 9]
+            out[10:14, rows, 0:128] = source[r_at : r_at + 4, :, lanes]
+            out[10:14, rows, 128:256] = source[r_at + 4 : r_at + 8, :, lanes]
+        out[9, 0:8] = below[BX + pack]
+        out[9, 8:16] = above[BX + pack]
+        out[9, 16:32] = jnp.zeros((16, Z0), F32)
+
+
+def send_z(lower, upper, below, above, x_below, x_above, own, to_upper, to_lower):
+    one, two = slice(0, 128), slice(128, 256)
+    own[0:4] = x_below[10:14, :, one]
+    own[4:8] = x_below[10:14, :, two]
+    own[40:44] = x_above[10:14, :, one]
+    own[44:48] = x_above[10:14, :, two]
+    for tile, source in enumerate((lower, upper, above, below)):
+        rows = slice(8 * tile, 8 * tile + 8)
+        own[8:24, rows] = source[36:52, :, one]
+        own[24:40, rows] = source[36:52, :, two]
     for out, high in ((to_upper, True), (to_lower, False)):
-        out[0:8] = beside(x_below[0:8], x_below[9:17], high)
-        out[40:48] = beside(x_above[0:8], x_above[8:16], high)
-        out[48] = beside(x_below[8], x_above[16], high)
-        for tile, source in enumerate((lower, upper, above, below)):
-            out[8:40, 8 * tile : 8 * tile + 8] = beside(source[0:BX], source[BX : 2 * BX], high)
-        out[49, 0:8] = beside(x_below[17, 0:8], x_below[17, 8:16], high)
-        for n in range(4):
-            at = 8 * (n + 1)
-            out[49 + at // 32, at % 32 : at % 32 + 8] = beside(below[2 * BX + n], above[2 * BX + n], high)
-        out[50, 8:16] = beside(x_above[17, 0:8], x_above[17, 8:16], high)
-        out[50, 16:32] = jnp.zeros((16, 128), F32)
+        out[...] = beside(own[0:24], own[24:48], high)
 
 
 def smooth_0(r, faces, inv, d0, d1, start, stop, between, again=False):
@@ -290,7 +287,7 @@
     return jnp.where(total < 5.0, 1.0, jnp.where(total < 15.0, 2.0 / 11.0, 0.1))
 
 
-def own_faces_0(sizes, where, mask, below, above, row, plane, packed, rho, raw_x, raw_y, raw_z):
+def own_faces_0(sizes, where, mask, below, above, rows_above, plane, packed, rho, raw_x, raw_y, raw_z):
     nx, ny, nz = sizes
     own, side = slice(0, 128), slice(128, 256)
     rho[0:BX, :, own] = density_of(mask)
@@ -305,7 +302,7 @@
     def one_plane(p, n):
         c = rho[p]
         raw_x[p] = face(c + jnp.where(where[0] * BX + p == nx - 1, GAS, rho[p + 1]))
-        after = jnp.where(y == BY - 1, row[pl.ds(p, 1)], roll(c, -1, 0))
+        after = jnp.where(y == BY - 1, rows_above[p, 0:1], roll(c, -1, 0))
         raw_y[p] = face(c + jnp.where(gy == ny - 1, GAS, after))
         raw_z[p] = face(c + jnp.where(gz == nz - 1, GAS, roll(c, -1, 1)))
 
@@ -320,31 +317,20 @@
             packed[16 * n + 4 * g : 16 * n + 4 * g + 4] = coarsen(raw[8 * g : 8 * g + 8], rows, columns)
 
 
-def faces_0(sizes, where, lower, upper, below, above, x_below, x_above, z_below, z_above,
-            fx, fy, fz, diag, inv, rho, low, up):
+def faces_0(sizes, where, lower, upper, below, above, x_below, x_above, fx, fy, fz, diag, inv, rho, low, up):
     nx, ny, nz = sizes
     gx0, gy0, gz0 = where[0] * BX, where[1] * BY, where[2] * BZ
-    own, side = slice(0, 128), slice(128, 256)
-    rho[0:9, :, own] = x_below[8:17]
-    rho[41:50, :, own] = x_above[8:17]
+    rho[0:9] = x_below[0:9]
+    rho[41:50] = x_above[0:9]
     for tile, source in enumerate((lower, upper, above, below)):
-        rho[9:41, 8 * tile : 8 * tile + 8, own] = source[BX : 2 * BX]
-    low[0:8, own] = x_below[17, 0:8]
-    up[0:8, own] = x_below[17, 8:16]
-    low[40:48, own] = x_above[17, 0:8]
-    up[40:48, own] = x_above[17, 8:16]
+        rho[9:41, 8 * tile : 8 * tile + 8] = source[0:BX]
+    low[0:8] = x_below[9, 0:8]
+    up[0:8] = x_below[9, 8:16]
+    low[40:48] = x_above[9, 0:8]
+    up[40:48] = x_above[9, 8:16]
     for n in range(4):
-        low[8 + 8 * n : 16 + 8 * n, own] = below[2 * BX + n]
-        up[8 + 8 * n : 16 + 8 * n, own] = above[2 * BX + n]
-
-    def side_planes(p, n):
-        rho[pl.ds(p + 1, n), :, side] = sides(z_below, z_above, pl.ds(p, n))[1]
-
-    loop(0, X0, 4, side_planes)
-    rho[0, :, side], rho[49, :, side] = sides(z_below, z_above, 48)
-    low[0:32, side], up[0:32, side] = sides(z_below, z_above, 49)
-    low_rest, up_rest = sides(z_below, z_above, 50)
-    low[32:48, side], up[32:48, side] = low_rest[0:16], up_rest[0:16]
+        low[8 + 8 * n : 16 + 8 * n] = below[BX + n]
+        up[8 + 8 * n : 16 + 8 * n] = above[BX + n]
 
     def plane(p, n):
         shape = (Y0, Z0)
@@ -372,20 +358,15 @@
     loop(0, X0, 1, plane, UC)
 
 
-def begin(lower, upper, below, above, x_below, x_above, z_below, z_above, fx, fy, fz, diag, inv,
-          r, total, packed, d0, d1):
-    own, side = slice(0, 128), slice(128, 256)
-    r[0:8, :, own] = x_below[0:8]
-    r[40:48, :, own] = x_above[0:8]
-    for tile, source in enumerate((lower, upper, above, below)):
-        r[8:40, 8 * tile : 8 * tile + 8, own] = source[0:BX]
-
-    def first(p, n):
-        here = pl.ds(p, n)
-        r[here, :, side] = sides(z_below, z_above, here)[0]
-        d0[here] = (FIRST * r[here]) * inv[here]
-
-    loop(0, X0, B0, first, U0)
+def begin(own, z_below, z_above, fx, fy, fz, diag, inv, r, total, packed, d0, d1):
+    def whole(p, n):
+        one, two = sides(z_below, z_above, pl.ds(p, n))
+        for here, side in ((pl.ds(p, n), one), (pl.ds(p + 24, n), two)):
+            value = jnp.concatenate([own[here], side], 2)
+            r[here] = value
+            d0[here] = (FIRST * value) * inv[here]
+
+    loop(0, 24, 4, whole)
     smooth_0(r, (fx, fy, fz, diag), inv, d0, d1, 0, X0, lambda: add_own(total, (d0, d1), True))
     restrict_0(r, packed)
 
@@ -673,27 +654,26 @@
 
     to_upper, to_lower = call(send_z_own, "send_z_own", (phase_mask,), [(16, BY, 128)] * 2)
     beside_own = (from_below(to_upper, "gz"), from_above(to_lower, "gz"))
-    upper, lower = call(
-        send_y, "send_y", (right_side, phase_mask), [(2 * BX + 4, 8, 128)] * 2, after=(to_upper, to_lower))
+    upper, lower, plane = call(
+        send_y, "send_y", (right_side, phase_mask, *beside_own), [(52, 8, Z0)] * 2 + [(BY, Z0)])
     below, above = from_below(upper, "gy"), from_above(lower, "gy")
-    row, plane = call(send_first, "send_first", (phase_mask, *beside_own), [(BX, Z0), (BY, Z0)])
-    row, plane = from_above(row, "gy"), from_above(plane, "gx")
-    to_upper, to_lower = call(send_x, "send_x", (lower, upper, below, above), [(18, Y0, 128)] * 2, after=(row, plane))
-    x_below, x_above = from_below(to_upper, "gx"), from_above(to_lower, "gx")
-    pieces = (lower, upper, below, above, x_below, x_above)
+    plane = from_above(plane, "gx")
+    pieces = (lower, upper, below, above)
+    to_upper, to_lower = call(send_x, "send_x", pieces, [(14, Y0, Z0)] * 2, after=(plane,))
+    pieces += (from_below(to_upper, "gx"), from_above(to_lower, "gx"))
     (packed,) = call(
-        functools.partial(own_faces_0, sizes), "own_faces_0", (where, phase_mask, *beside_own, row, plane),
+        functools.partial(own_faces_0, sizes), "own_faces_0", (where, phase_mask, *beside_own, above, plane),
         [(48, 8, 128)], [(BX + 1, BY, Z0)] + [(BX, BY, Z0)] * 3, us=2)
     parts = along_y(packed)
     around_faces = along_x(parts)
-    to_upper, to_lower = call(send_z, "send_z", pieces, [(51, Y0, 128)] * 2, after=(packed, parts[1]))
-    pieces += (from_below(to_upper, "gz"), from_above(to_lower, "gz"))
-
+    r_own, to_upper, to_lower = call(
+        send_z, "send_z", pieces, [(X0, Y0, 128)] + [(24, Y0, 128)] * 2, after=(packed, parts[1]))
+    residual = (r_own, from_below(to_upper, "gz"), from_above(to_lower, "gz"))
     level_0 = call(
         functools.partial(faces_0, sizes), "faces_0", (where, *pieces), [full] * 5,
-        [(X0 + 2, Y0, Z0), (X0, Z0), (X0, Z0)], us=4, after=around_faces[:1])
+        [(X0 + 2, Y0, Z0), (X0, Z0), (X0, Z0)], us=4)
     r0, total, packed = call(
-        begin, "begin", (*pieces, *level_0), [full, own, (16, 8, 128)], [full] * 2, us=6)
+        begin, "begin", (*residual, *level_0), [full, own, (16, 8, 128)], [full] * 2, us=6)
     *levels, faces_3 = call(
         functools.partial(faces_1, sizes), "faces_1", (where, *around_faces),
         [full_1] * 5 + [full_2] * 5 + [(10, 2 * ny, 128)], us=3)

time: 145 us -> 143 us (0.986)
  waiting for transfers between devices: 56.2 us -> 50.6 us
  starting transfers between devices: 42.9 us -> 47 us
    ppermute x22 -> x21, waiting for transfers between devices: 37.3 us -> 31 us  [from_above(): return lax.ppermute(array, axis, [((i + by) % n, i) for i in range(n)])]
    ppermute x22 -> x21, starting transfers between devices: 33.5 us -> 36.3 us  [from_above(): return lax.ppermute(array, axis, [((i + by) % n, i) for i in range(n)])]
    pallas_call x15 -> x14, Pallas kernels: 42.4 us -> 42.6 us  [call(): pl.pallas_call(kernel, out_shape=[jax.ShapeDtypeStruct(s, F32) for s in o...]
  transfers between devices with their start and end apart: 33 -> 32, of which waited for: 19 -> 19; matrix products, arithmetic and copies ran while one was open for 0% -> 0% of each run, Pallas kernels for 10% -> 10%
where the time goes in v1:
time: 143 us
  waiting for transfers between devices  50.6 us (35%)
  starting transfers between devices  47 us (33%)
  Pallas kernels  42.6 us (30%)
  local copies, waits for them, and re-layouts  1.95 us (1%)
    pallas_call x14, Pallas kernels, call(): pl.pallas_call(kernel, out_shape=[jax.ShapeDtypeStruct(s, F32) for s in o...  42.6 us
    ppermute x21, starting transfers between devices, from_above(): return lax.ppermute(array, axis, [((i + by) % n, i) for i in range(n)])  36.3 us
    ppermute x21, waiting for transfers between devices, from_above(): return lax.ppermute(array, axis, [((i + by) % n, i) for i in range(n)])  31 us
    ppermute x11, waiting for transfers between devices, from_below(): return lax.ppermute(array, axis, [(i, (i + by) % n) for i in range(n)])  19.6 us
    ppermute x11, starting transfers between devices, from_below(): return lax.ppermute(array, axis, [(i, (i + by) % n) for i in range(n)])  10.7 us
  transfers between devices with their start and end apart: 32, of which 19 were waited for; matrix products, arithmetic and copies ran while one was open for 0% of the time, Pallas kernels for 10%

profile of v1, /device:TPU:6, one launch (start us, length us, event | category | flops | bytes accessed | tf_op | source)
XLA Modules:
  0.0 143.2 jit_solution(8687247019097879207)
XLA Ops:
  0.6 0.9 copy-done
  1.6 0.1 send_z_own.1
  1.7 2.9 %collective-permute-start.1 = (f32[16,16,128]{2,1,0:T(8,128)S(1)}, f32[16,16,128]{2,1,0:T(8,128)S(1)}, u32[]{:S(2)}, u32[]{:S(2)}) collective-permute-start(f32[16,16,128]{2,1,0:T(8,128)S(1)} %get-tuple-element.50), channel_id=1, source_target_pairs={{1,0},{2,1},{3,2},{4,3},{5,4},{6,5},{7,6},{0,7},{9,8},{10,9},{11,1... | collective-permute-start | bytes 393224 | tf_op jit(solution)/shard_map/ppermute | solution.py:635
  4.7 2.6 %collective-permute-done.z_below.below = f32[16,16,128]{2,1,0:T(8,128)S(1)} collective-permute-done((f32[16,16,128]{2,1,0:T(8,128)S(1)}, f32[16,16,128]{2,1,0:T(8,128)S(1)}, u32[]{:S(2)}, u32[]{:S(2)}) %collective-permute-start) | collective-permute-done | bytes 131104 | tf_op jit(solution)/shard_map/ppermute | solution.py:630
  7.3 0.9 copy-done.2
  8.3 0.2 send_y.1
  8.4 0.9 collective-permute-start.3
  9.3 2.4 %collective-permute-start.2 = (f32[52,8,256]{2,1,0:T(8,128)S(1)}, f32[52,8,256]{2,1,0:T(8,128)S(1)}, u32[]{:S(2)}, u32[]{:S(2)}) collective-permute-start(f32[52,8,256]{2,1,0:T(8,128)S(1)} %get-tuple-element.52.refs_1_.upper), channel_id=1, source_target_pairs={{0,8},{8,16},{16,24},{24,0},{1,9},{9,17},{17,25},{25,1},{2,10},{10... | collective-permute-start | bytes 1277960 | tf_op jit(solution)/shard_map/ppermute | solution.py:630
  11.7 5.9 %collective-permute-start.4 = (f32[16,256]{1,0:T(8,128)S(1)}, f32[16,256]{1,0:T(8,128)S(1)}, u32[]{:S(2)}, u32[]{:S(2)}) collective-permute-start(f32[16,256]{1,0:T(8,128)S(1)} %get-tuple-element.53), channel_id=1, source_target_pairs={{32,0},{64,32},{96,64},{128,96},{160,128},{192,160},{224,192},{0,2... | collective-permute-start | bytes 49160 | tf_op jit(solution)/shard_map/ppermute | solution.py:635
  17.6 1.4 %collective-permute-done.4.refs_4_.plane = f32[16,256]{1,0:T(8,128)S(1)} collective-permute-done((f32[16,256]{1,0:T(8,128)S(1)}, f32[16,256]{1,0:T(8,128)S(1)}, u32[]{:S(2)}, u32[]{:S(2)}) %collective-permute-start.4) | collective-permute-done | bytes 16416 | tf_op jit(solution)/shard_map/ppermute | solution.py:635
  19.0 2.9 %collective-permute-done.3.refs_3_.rows_above.above = f32[52,8,256]{2,1,0:T(8,128)S(1)} collective-permute-done((f32[52,8,256]{2,1,0:T(8,128)S(1)}, f32[52,8,256]{2,1,0:T(8,128)S(1)}, u32[]{:S(2)}, u32[]{:S(2)}) %collective-permute-start.3) | collective-permute-done | bytes 426016 | tf_op jit(solution)/shard_map/ppermute | solution.py:635
  21.9 1.0 send_x.1
  22.9 1.9 %collective-permute-start.5 = (f32[14,32,256]{2,1,0:T(8,128)}, f32[14,32,256]{2,1,0:T(8,128)S(1)}, u32[]{:S(2)}, u32[]{:S(2)}) collective-permute-start(f32[14,32,256]{2,1,0:T(8,128)} %get-tuple-element.54), channel_id=1, source_target_pairs={{0,32},{32,64},{64,96},{96,128},{128,160},{160,192},{192,224},{224... | collective-permute-start | bytes 1376264 | tf_op jit(solution)/shard_map/ppermute | solution.py:630
  24.8 3.9 %collective-permute-start.6 = (f32[14,32,256]{2,1,0:T(8,128)}, f32[14,32,256]{2,1,0:T(8,128)S(1)}, u32[]{:S(2)}, u32[]{:S(2)}) collective-permute-start(f32[14,32,256]{2,1,0:T(8,128)} %get-tuple-element.55), channel_id=1, source_target_pairs={{32,0},{64,32},{96,64},{128,96},{160,128},{192,160},{224,192},{0,2... | collective-permute-start | bytes 1376264 | tf_op jit(solution)/shard_map/ppermute | solution.py:635
  28.8 0.1 pad_add_fusion.where
  28.9 2.3 %own_faces_0.1.refs_6_ = f32[48,8,128]{2,1,0:T(8,128)S(1)} custom-call(s32[3]{0:T(128)S(1)} %pad_add_fusion.where, s32[32,16,128]{2,1,0:T(8,128)S(1)} %copy-done.1, f32[16,16,128]{2,1,0:T(8,128)S(1)} %collective-permute-done.z_below.below, f32[16,16,128]{2,1,0:T(8,128)S(1)} %collective-permute-done.1.z_above.above, ...), custom_call_target="tpu_custom_call" | custom-call | bytes 7000000 | tf_op jit(solution)/shard_map/own_faces_0/pallas_call | solution.py:615
  31.1 0.1 collective-permute-start.7
  31.2 3.2 %collective-permute-start.16 = (f32[48,8,128]{2,1,0:T(8,128)S(1)}, f32[48,8,128]{2,1,0:T(8,128)S(1)}, u32[]{:S(2)}, u32[]{:S(2)}) collective-permute-start(f32[48,8,128]{2,1,0:T(8,128)S(1)} %own_faces_0.1.refs_6_), channel_id=1, source_target_pairs={{24,0},{0,8},{8,16},{16,24},{25,1},{1,9},{9,17},{17,25},{26,2},{2,... | collective-permute-start | bytes 589832 | tf_op jit(solution)/shard_map/ppermute | solution.py:635
  34.4 1.2 collective-permute-start.15
  35.6 4.1 %collective-permute-done.7.refs_7_ = f32[48,8,128]{2,1,0:T(8,128)S(1)} collective-permute-done((f32[48,8,128]{2,1,0:T(8,128)S(1)}, f32[48,8,128]{2,1,0:T(8,128)S(1)}, u32[]{:S(2)}, u32[]{:S(2)}) %collective-permute-start.7) | collective-permute-done | bytes 196640 | tf_op jit(solution)/shard_map/ppermute | solution.py:635
  39.7 0.3 send_z.1
  40.0 2.9 %collective-permute-start.9 = (f32[24,32,128]{2,1,0:T(8,128)S(1)}, f32[24,32,128]{2,1,0:T(8,128)S(1)}, u32[]{:S(2)}, u32[]{:S(2)}) collective-permute-start(f32[24,32,128]{2,1,0:T(8,128)S(1)} %get-tuple-element.58), channel_id=1, source_target_pairs={{1,0},{2,1},{3,2},{4,3},{5,4},{6,5},{7,6},{0,7},{9,8},{10,9},{11,1... | collective-permute-start | bytes 1179656 | tf_op jit(solution)/shard_map/ppermute | solution.py:635
  43.0 0.7 collective-permute-done.15
  43.7 0.1 pad_maximum_fusion.own
  43.8 1.9 %collective-permute-start.18 = (f32[48,32,128]{2,1,0:T(8,128)S(1)}, f32[48,32,128]{2,1,0:T(8,128)S(1)}, u32[]{:S(2)}, u32[]{:S(2)}) collective-permute-start(f32[48,32,128]{2,1,0:T(8,128)S(1)} %pad_maximum_fusion.own), channel_id=1, source_target_pairs={{32,0},{64,32},{96,64},{128,96},{160,128},{192,160},{224,192},{0,2... | collective-permute-start | bytes 2359304 | tf_op jit(solution)/shard_map/ppermute | solution.py:635
  45.7 0.2 collective-permute-start.17
  45.9 4.1 %faces_0.1 = (f32[48,32,256]{2,1,0:T(8,128)S(1)}, f32[48,32,256]{2,1,0:T(8,128)S(1)}, f32[48,32,256]{2,1,0:T(8,128)S(1)}, f32[48,32,256]{2,1,0:T(8,128)S(1)}, f32[48,32,256]{2,1,0:T(8,128)S(1)}) custom-call(s32[3]{0:T(128)S(1)} %pad_add_fusion.where, f32[52,8,256]{2,1,0:T(8,128)S(1)} %get-tuple-element.51.refs_0_.lower, ...), custom_call_target="tpu_custom_call" | custom-call | bytes 14000000 | tf_op jit(solution)/shard_map/faces_0/pallas_call | solution.py:615
  50.1 4.6 %begin.1 = (f32[48,32,256]{2,1,0:T(8,128)S(1)}, f32[32,16,128]{2,1,0:T(8,128)S(1)}, f32[16,8,128]{2,1,0:T(8,128)S(1)}) custom-call(f32[48,32,128]{2,1,0:T(8,128)S(1)} %get-tuple-element.56.own, f32[24,32,128]{2,1,0:T(8,128)S(1)} %collective-permute-done.8.z_below, f32[24,32,128]{2,1,0:T(8,128)S(1)} %collective-permute-done.9.z_above, ...), custom_call_target="tpu_custom_call" | custom-call | bytes 21000000 | tf_op jit(solution)/shard_map/begin/pallas_call | solution.py:615
  54.7 2.5 %collective-permute-start.12 = (f32[16,8,128]{2,1,0:T(8,128)S(1)}, f32[16,8,128]{2,1,0:T(8,128)S(1)}, u32[]{:S(2)}, u32[]{:S(2)}) collective-permute-start(f32[16,8,128]{2,1,0:T(8,128)S(1)} %get-tuple-element.64), channel_id=1, source_target_pairs={{24,0},{0,8},{8,16},{16,24},{25,1},{1,9},{9,17},{17,25},{26,2},{2,... | collective-permute-start | bytes 196616 | tf_op jit(solution)/shard_map/ppermute | solution.py:635
  57.2 0.7 collective-permute-start.11
  58.0 0.2 collective-permute-start.10
  58.2 5.5 %collective-permute-done.10 = f32[16,8,128]{2,1,0:T(8,128)S(1)} collective-permute-done((f32[16,8,128]{2,1,0:T(8,128)S(1)}, f32[16,8,128]{2,1,0:T(8,128)S(1)}, u32[]{:S(2)}, u32[]{:S(2)}) %collective-permute-start.10) | collective-permute-done | bytes 65568 | tf_op jit(solution)/shard_map/ppermute | solution.py:635
  63.8 3.3 %collective-permute-start.14 = (f32[16,32,128]{2,1,0:T(8,128)S(1)}, f32[16,32,128]{2,1,0:T(8,128)S(1)}, u32[]{:S(2)}, u32[]{:S(2)}) collective-permute-start(f32[16,32,128]{2,1,0:T(8,128)S(1)} %constant_dynamic-update-slice_fusion.own), channel_id=1, source_target_pairs={{32,0},{64,32},{96,64},{128,96},{160,128},{192,160},{224,192},{0,2... | collective-permute-start | bytes 786440 | tf_op jit(solution)/shard_map/ppermute | solution.py:635
  67.1 3.2 %faces_1.1 = (f32[48,32,128]{2,1,0:T(8,128)S(1)}, f32[48,32,128]{2,1,0:T(8,128)S(1)}, f32[48,32,128]{2,1,0:T(8,128)S(1)}, f32[48,32,128]{2,1,0:T(8,128)S(1)}, f3...) custom-call(s32[3]{0:T(128)S(1)} %pad_add_fusion.where, ...), custom_call_target="tpu_custom_call" | custom-call | bytes 10500000 | tf_op jit(solution)/shard_map/faces_1/pallas_call | solution.py:615
  70.3 0.6 collective-permute-done.14.above
  71.0 3.7 %collective-permute-done.13.below = f32[16,32,128]{2,1,0:T(8,128)S(1)} collective-permute-done((f32[16,32,128]{2,1,0:T(8,128)S(1)}, f32[16,32,128]{2,1,0:T(8,128)S(1)}, u32[]{:S(2)}, u32[]{:S(2)}) %collective-permute-start.13) | collective-permute-done | bytes 262176 | tf_op jit(solution)/shard_map/ppermute | solution.py:630
  74.6 2.8 %down.2 = (f32[48,32,128]{2,1,0:T(8,128)S(1)}, f32[48,32,128]{2,1,0:T(8,128)S(1)}, f32[24,16,128]{2,1,0:T(8,128)S(1)}, f32[24,16,128]{2,1,0:T(8,128)S(1)}, f32[10,8,128]{2,1,0:T(8,128)S(1)}) custom-call(f32[16,32,128]{2,1,0:T(8,128)S(1)} %constant_dynamic-update-slice_fusion.own, f32[16,32,128]{2,1,0:T(8,128)S(1)} %collective-permute-done.13.below, ...), custom_call_target="tpu_custom_call" | custom-call | bytes 14000000 | tf_op jit(solution)/shard_map/down/pallas_call | solution.py:615
  77.5 0.6 collective-permute-start.19
  78.1 1.2 collective-permute-done.20.above
  79.3 3.0 %collective-permute-done.19.below = f32[10,8,128]{2,1,0:T(8,128)S(1)} collective-permute-done((f32[10,8,128]{2,1,0:T(8,128)S(1)}, f32[10,8,128]{2,1,0:T(8,128)S(1)}, u32[]{:S(2)}, u32[]{:S(2)}) %collective-permute-start.19) | collective-permute-done | bytes 40992 | tf_op jit(solution)/shard_map/ppermute | solution.py:630
  82.2 0.2 spread.2.own3
  82.4 0.1 collective-permute-start.22
  82.5 2.9 %collective-permute-start.21 = (f32[20,8,128]{2,1,0:T(8,128)S(1)}, f32[20,8,128]{2,1,0:T(8,128)S(1)}, u32[]{:S(2)}, u32[]{:S(2)}) collective-permute-start(f32[20,8,128]{2,1,0:T(8,128)S(1)} %spread.2.own3), channel_id=1, source_target_pairs={{0,64},{32,96},{64,128},{96,160},{128,192},{160,224},{192,0},{224,... | collective-permute-start | bytes 245768 | tf_op jit(solution)/shard_map/ppermute | solution.py:630
  85.4 2.5 %collective-permute-done.22.above3 = f32[20,8,128]{2,1,0:T(8,128)S(1)} collective-permute-done((f32[20,8,128]{2,1,0:T(8,128)S(1)}, f32[20,8,128]{2,1,0:T(8,128)S(1)}, u32[]{:S(2)}, u32[]{:S(2)}) %collective-permute-start.22) | collective-permute-done | bytes 81952 | tf_op jit(solution)/shard_map/ppermute | solution.py:635
  88.0 2.4 %collective-permute-done.21.below3 = f32[20,8,128]{2,1,0:T(8,128)S(1)} collective-permute-done((f32[20,8,128]{2,1,0:T(8,128)S(1)}, f32[20,8,128]{2,1,0:T(8,128)S(1)}, u32[]{:S(2)}, u32[]{:S(2)}) %collective-permute-start.21) | collective-permute-done | bytes 81952 | tf_op jit(solution)/shard_map/ppermute | solution.py:630
  90.3 12.3 %up.1 = (f32[26,8,128]{2,1,0:T(8,128)S(1)}, f32[26,8,128]{2,1,0:T(8,128)S(1)}, f32[26,8,128]{2,1,0:T(8,128)S(1)}, f32[26,8,128]{2,1,0:T(8,128)S(1)}, f32[26,8,12...) custom-call(s32[3]{0:T(128)S(1)} %pad_add_fusion.where, ...), custom_call_target="tpu_custom_call" | custom-call | bytes 52500000 | tf_op jit(solution)/shard_map/up/pallas_call | solution.py:615
  102.6 1.2 collective-permute-start.25
  103.8 0.9 collective-permute-start.24
  104.7 1.3 collective-permute-start.23
  106.0 4.3 %collective-permute-done.23 = f32[16,8,128]{2,1,0:T(8,128)S(1)} collective-permute-done((f32[16,8,128]{2,1,0:T(8,128)S(1)}, f32[16,8,128]{2,1,0:T(8,128)S(1)}, u32[]{:S(2)}, u32[]{:S(2)}) %collective-permute-start.23) | collective-permute-done | bytes 65568 | tf_op jit(solution)/shard_map/ppermute | solution.py:635
  110.3 0.1 collective-permute-start.27
  110.4 2.0 %collective-permute-start.26 = (f32[16,32,128]{2,1,0:T(8,128)S(1)}, f32[16,32,128]{2,1,0:T(8,128)S(1)}, u32[]{:S(2)}, u32[]{:S(2)}) collective-permute-start(f32[16,32,128]{2,1,0:T(8,128)S(1)} %constant_dynamic-update-slice_fusion.4.own), channel_id=1, source_target_pairs={{0,32},{32,64},{64,96},{96,128},{128,160},{160,192},{192,224},{224... | collective-permute-start | bytes 786440 | tf_op jit(solution)/shard_map/ppermute | solution.py:630
  112.4 4.3 %collective-permute-done.27.above = f32[16,32,128]{2,1,0:T(8,128)S(1)} collective-permute-done((f32[16,32,128]{2,1,0:T(8,128)S(1)}, f32[16,32,128]{2,1,0:T(8,128)S(1)}, u32[]{:S(2)}, u32[]{:S(2)}) %collective-permute-start.27) | collective-permute-done | bytes 262176 | tf_op jit(solution)/shard_map/ppermute | solution.py:635
  116.8 1.3 collective-permute-done.26.below
  118.1 2.8 %down.3 = (f32[48,32,128]{2,1,0:T(8,128)S(1)}, f32[48,32,128]{2,1,0:T(8,128)S(1)}, f32[24,16,128]{2,1,0:T(8,128)S(1)}, f32[24,16,128]{2,1,0:T(8,128)S(1)}, f32[8,8,128]{2,1,0:T(8,128)S(1)}) custom-call(f32[16,32,128]{2,1,0:T(8,128)S(1)} %constant_dynamic-update-slice_fusion.4.own, f32[16,32,128]{2,1,0:T(8,128)S(1)} %collective-permute-done.26.below, ...), custom_call_target="tpu_custom_call" | custom-call | bytes 14000000 | tf_op jit(solution)/shard_map/down/pallas_call | solution.py:615
  121.0 0.6 collective-permute-start.28
  121.6 1.1 collective-permute-done.29.above
  122.6 3.0 %collective-permute-done.28.below = f32[8,8,128]{2,1,0:T(8,128)S(1)} collective-permute-done((f32[8,8,128]{2,1,0:T(8,128)S(1)}, f32[8,8,128]{2,1,0:T(8,128)S(1)}, u32[]{:S(2)}, u32[]{:S(2)}) %collective-permute-start.28) | collective-permute-done | bytes 32800 | tf_op jit(solution)/shard_map/ppermute | solution.py:630
  125.6 0.1 spread.3.own3
  125.7 2.9 %collective-permute-start.31 = (f32[8,8,128]{2,1,0:T(8,128)S(1)}, f32[8,8,128]{2,1,0:T(8,128)S(1)}, u32[]{:S(2)}, u32[]{:S(2)}) collective-permute-start(f32[8,8,128]{2,1,0:T(8,128)S(1)} %spread.3.own3), channel_id=1, source_target_pairs={{64,0},{96,32},{128,64},{160,96},{192,128},{224,160},{0,192},{32,2... | collective-permute-start | bytes 98312 | tf_op jit(solution)/shard_map/ppermute | solution.py:635
  128.6 0.1 collective-permute-start.30
  128.7 2.2 %collective-permute-done.31.above3 = f32[8,8,128]{2,1,0:T(8,128)S(1)} collective-permute-done((f32[8,8,128]{2,1,0:T(8,128)S(1)}, f32[8,8,128]{2,1,0:T(8,128)S(1)}, u32[]{:S(2)}, u32[]{:S(2)}) %collective-permute-start.31) | collective-permute-done | bytes 32800 | tf_op jit(solution)/shard_map/ppermute | solution.py:635
  130.9 3.7 %collective-permute-done.30.below3 = f32[8,8,128]{2,1,0:T(8,128)S(1)} collective-permute-done((f32[8,8,128]{2,1,0:T(8,128)S(1)}, f32[8,8,128]{2,1,0:T(8,128)S(1)}, u32[]{:S(2)}, u32[]{:S(2)}) %collective-permute-start.30) | collective-permute-done | bytes 32800 | tf_op jit(solution)/shard_map/ppermute | solution.py:630
  134.6 8.5 %up_last.1 = (f32[32,16,128]{2,1,0:T(8,128)}, f32[32,16,128]{2,1,0:T(8,128)}) custom-call(s32[3]{0:T(128)S(1)} %pad_add_fusion.where, f32[8,8,128]{2,1,0:T(8,128)S(1)} %spread.3.own3, f32[8,8,128]{2,1,0:T(8,128)S(1)} %collective-permute-done.30.below3, f32[8,8,128]{2,1,0:T(8,128)S(1)} %collective-permute-done.31.above3, ...), custom_call_target="tpu_custom_call" | custom-call | bytes 35000000 | tf_op jit(solution)/shard_map/up_last/pallas_call | solution.py:615
  (30 shorter events, 0.2 us)
Async XLA Ops:
  0.6 1.0 copy-start
  1.6 27.3 %copy-start.1 = (s32[32,16,128]{2,1,0:T(8,128)S(1)}, s32[32,16,128]{2,1,0:T(8,128)}, u32[]{:S(2)}) copy-start(s32[32,16,128]{2,1,0:T(8,128)} %mask.5) | copy-start | bytes 786436
  1.7 5.6 %collective-permute-start = (f32[16,16,128]{2,1,0:T(8,128)S(1)}, f32[16,16,128]{2,1,0:T(8,128)S(1)}, u32[]{:S(2)}, u32[]{:S(2)}) collective-permute-start(f32[16,16,128]{2,1,0:T(8,128)S(1)} %get-tuple-element.49), channel_id=1, source_target_pairs={{0,1},{1,2},{2,3},{3,4},{4,5},{5,6},{6,7},{7,0},{8,9},{9,10},{10,1... | collective-permute-start | bytes 393224 | tf_op jit(solution)/shard_map/ppermute | solution.py:630
  1.7 5.6 %collective-permute-start.1 = (f32[16,16,128]{2,1,0:T(8,128)S(1)}, f32[16,16,128]{2,1,0:T(8,128)S(1)}, u32[]{:S(2)}, u32[]{:S(2)}) collective-permute-start(f32[16,16,128]{2,1,0:T(8,128)S(1)} %get-tuple-element.50), channel_id=1, source_target_pairs={{1,0},{2,1},{3,2},{4,3},{5,4},{6,5},{7,6},{0,7},{9,8},{10,9},{11,1... | collective-permute-start | bytes 393224 | tf_op jit(solution)/shard_map/ppermute | solution.py:635
  7.3 1.0 copy-start.2
  8.4 13.5 %collective-permute-start.3 = (f32[52,8,256]{2,1,0:T(8,128)S(1)}, f32[52,8,256]{2,1,0:T(8,128)S(1)}, u32[]{:S(2)}, u32[]{:S(2)}) collective-permute-start(f32[52,8,256]{2,1,0:T(8,128)S(1)} %get-tuple-element.51.refs_0_.lower), channel_id=1, source_target_pairs={{8,0},{16,8},{24,16},{0,24},{9,1},{17,9},{25,17},{1,25},{10,2},{18... | collective-permute-start | bytes 1277960 | tf_op jit(solution)/shard_map/ppermute | solution.py:635
  9.3 12.6 %collective-permute-start.2 = (f32[52,8,256]{2,1,0:T(8,128)S(1)}, f32[52,8,256]{2,1,0:T(8,128)S(1)}, u32[]{:S(2)}, u32[]{:S(2)}) collective-permute-start(f32[52,8,256]{2,1,0:T(8,128)S(1)} %get-tuple-element.52.refs_1_.upper), channel_id=1, source_target_pairs={{0,8},{8,16},{16,24},{24,0},{1,9},{9,17},{17,25},{25,1},{2,10},{10... | collective-permute-start | bytes 1277960 | tf_op jit(solution)/shard_map/ppermute | solution.py:630
  11.7 7.3 %collective-permute-start.4 = (f32[16,256]{1,0:T(8,128)S(1)}, f32[16,256]{1,0:T(8,128)S(1)}, u32[]{:S(2)}, u32[]{:S(2)}) collective-permute-start(f32[16,256]{1,0:T(8,128)S(1)} %get-tuple-element.53), channel_id=1, source_target_pairs={{32,0},{64,32},{96,64},{128,96},{160,128},{192,160},{224,192},{0,2... | collective-permute-start | bytes 49160 | tf_op jit(solution)/shard_map/ppermute | solution.py:635
  22.9 16.8 %collective-permute-start.5 = (f32[14,32,256]{2,1,0:T(8,128)}, f32[14,32,256]{2,1,0:T(8,128)S(1)}, u32[]{:S(2)}, u32[]{:S(2)}) collective-permute-start(f32[14,32,256]{2,1,0:T(8,128)} %get-tuple-element.54), channel_id=1, source_target_pairs={{0,32},{32,64},{64,96},{96,128},{128,160},{160,192},{192,224},{224... | collective-permute-start | bytes 1376264 | tf_op jit(solution)/shard_map/ppermute | solution.py:630
  24.8 14.9 %collective-permute-start.6 = (f32[14,32,256]{2,1,0:T(8,128)}, f32[14,32,256]{2,1,0:T(8,128)S(1)}, u32[]{:S(2)}, u32[]{:S(2)}) collective-permute-start(f32[14,32,256]{2,1,0:T(8,128)} %get-tuple-element.55), channel_id=1, source_target_pairs={{32,0},{64,32},{96,64},{128,96},{160,128},{192,160},{224,192},{0,2... | collective-permute-start | bytes 1376264 | tf_op jit(solution)/shard_map/ppermute | solution.py:635
  31.1 8.6 %collective-permute-start.7 = (f32[48,8,128]{2,1,0:T(8,128)S(1)}, f32[48,8,128]{2,1,0:T(8,128)S(1)}, u32[]{:S(2)}, u32[]{:S(2)}) collective-permute-start(f32[48,8,128]{2,1,0:T(8,128)S(1)} %own_faces_0.1.refs_6_), channel_id=1, source_target_pairs={{8,0},{16,8},{24,16},{0,24},{9,1},{17,9},{25,17},{1,25},{10,2},{18... | collective-permute-start | bytes 589832 | tf_op jit(solution)/shard_map/ppermute | solution.py:635
  31.2 11.8 %collective-permute-start.16 = (f32[48,8,128]{2,1,0:T(8,128)S(1)}, f32[48,8,128]{2,1,0:T(8,128)S(1)}, u32[]{:S(2)}, u32[]{:S(2)}) collective-permute-start(f32[48,8,128]{2,1,0:T(8,128)S(1)} %own_faces_0.1.refs_6_), channel_id=1, source_target_pairs={{24,0},{0,8},{8,16},{16,24},{25,1},{1,9},{9,17},{17,25},{26,2},{2,... | collective-permute-start | bytes 589832 | tf_op jit(solution)/shard_map/ppermute | solution.py:635
  34.4 9.3 %collective-permute-start.15 = (f32[48,8,128]{2,1,0:T(8,128)S(1)}, f32[48,8,128]{2,1,0:T(8,128)S(1)}, u32[]{:S(2)}, u32[]{:S(2)}) collective-permute-start(f32[48,8,128]{2,1,0:T(8,128)S(1)} %own_faces_0.1.refs_6_), channel_id=1, source_target_pairs={{16,0},{24,8},{0,16},{8,24},{17,1},{25,9},{1,17},{9,25},{18,2},{26... | collective-permute-start | bytes 589832 | tf_op jit(solution)/shard_map/ppermute | solution.py:635
  40.0 10.0 %collective-permute-start.8 = (f32[24,32,128]{2,1,0:T(8,128)S(1)}, f32[24,32,128]{2,1,0:T(8,128)S(1)}, u32[]{:S(2)}, u32[]{:S(2)}) collective-permute-start(f32[24,32,128]{2,1,0:T(8,128)S(1)} %get-tuple-element.57), channel_id=1, source_target_pairs={{0,1},{1,2},{2,3},{3,4},{4,5},{5,6},{6,7},{7,0},{8,9},{9,10},{10,1... | collective-permute-start | bytes 1179656 | tf_op jit(solution)/shard_map/ppermute | solution.py:630
  40.0 10.0 %collective-permute-start.9 = (f32[24,32,128]{2,1,0:T(8,128)S(1)}, f32[24,32,128]{2,1,0:T(8,128)S(1)}, u32[]{:S(2)}, u32[]{:S(2)}) collective-permute-start(f32[24,32,128]{2,1,0:T(8,128)S(1)} %get-tuple-element.58), channel_id=1, source_target_pairs={{1,0},{2,1},{3,2},{4,3},{5,4},{6,5},{7,6},{0,7},{9,8},{10,9},{11,1... | collective-permute-start | bytes 1179656 | tf_op jit(solution)/shard_map/ppermute | solution.py:635
  43.8 23.3 %collective-permute-start.18 = (f32[48,32,128]{2,1,0:T(8,128)S(1)}, f32[48,32,128]{2,1,0:T(8,128)S(1)}, u32[]{:S(2)}, u32[]{:S(2)}) collective-permute-start(f32[48,32,128]{2,1,0:T(8,128)S(1)} %pad_maximum_fusion.own), channel_id=1, source_target_pairs={{32,0},{64,32},{96,64},{128,96},{160,128},{192,160},{224,192},{0,2... | collective-permute-start | bytes 2359304 | tf_op jit(solution)/shard_map/ppermute | solution.py:635
  45.7 21.3 %collective-permute-start.17 = (f32[48,32,128]{2,1,0:T(8,128)S(1)}, f32[48,32,128]{2,1,0:T(8,128)S(1)}, u32[]{:S(2)}, u32[]{:S(2)}) collective-permute-start(f32[48,32,128]{2,1,0:T(8,128)S(1)} %pad_maximum_fusion.own), channel_id=1, source_target_pairs={{0,32},{32,64},{64,96},{96,128},{128,160},{160,192},{192,224},{224... | collective-permute-start | bytes 2359304 | tf_op jit(solution)/shard_map/ppermute | solution.py:630
  54.7 9.1 %collective-permute-start.12 = (f32[16,8,128]{2,1,0:T(8,128)S(1)}, f32[16,8,128]{2,1,0:T(8,128)S(1)}, u32[]{:S(2)}, u32[]{:S(2)}) collective-permute-start(f32[16,8,128]{2,1,0:T(8,128)S(1)} %get-tuple-element.64), channel_id=1, source_target_pairs={{24,0},{0,8},{8,16},{16,24},{25,1},{1,9},{9,17},{17,25},{26,2},{2,... | collective-permute-start | bytes 196616 | tf_op jit(solution)/shard_map/ppermute | solution.py:635
  57.2 6.5 %collective-permute-start.11 = (f32[16,8,128]{2,1,0:T(8,128)S(1)}, f32[16,8,128]{2,1,0:T(8,128)S(1)}, u32[]{:S(2)}, u32[]{:S(2)}) collective-permute-start(f32[16,8,128]{2,1,0:T(8,128)S(1)} %get-tuple-element.64), channel_id=1, source_target_pairs={{16,0},{24,8},{0,16},{8,24},{17,1},{25,9},{1,17},{9,25},{18,2},{26... | collective-permute-start | bytes 196616 | tf_op jit(solution)/shard_map/ppermute | solution.py:635
  58.0 5.7 %collective-permute-start.10 = (f32[16,8,128]{2,1,0:T(8,128)S(1)}, f32[16,8,128]{2,1,0:T(8,128)S(1)}, u32[]{:S(2)}, u32[]{:S(2)}) collective-permute-start(f32[16,8,128]{2,1,0:T(8,128)S(1)} %get-tuple-element.64), channel_id=1, source_target_pairs={{8,0},{16,8},{24,16},{0,24},{9,1},{17,9},{25,17},{1,25},{10,2},{18... | collective-permute-start | bytes 196616 | tf_op jit(solution)/shard_map/ppermute | solution.py:635
  63.8 7.2 %collective-permute-start.14 = (f32[16,32,128]{2,1,0:T(8,128)S(1)}, f32[16,32,128]{2,1,0:T(8,128)S(1)}, u32[]{:S(2)}, u32[]{:S(2)}) collective-permute-start(f32[16,32,128]{2,1,0:T(8,128)S(1)} %constant_dynamic-update-slice_fusion.own), channel_id=1, source_target_pairs={{32,0},{64,32},{96,64},{128,96},{160,128},{192,160},{224,192},{0,2... | collective-permute-start | bytes 786440 | tf_op jit(solution)/shard_map/ppermute | solution.py:635
  67.1 7.6 %collective-permute-start.13 = (f32[16,32,128]{2,1,0:T(8,128)S(1)}, f32[16,32,128]{2,1,0:T(8,128)S(1)}, u32[]{:S(2)}, u32[]{:S(2)}) collective-permute-start(f32[16,32,128]{2,1,0:T(8,128)S(1)} %constant_dynamic-update-slice_fusion.own), channel_id=1, source_target_pairs={{0,32},{32,64},{64,96},{96,128},{128,160},{160,192},{192,224},{224... | collective-permute-start | bytes 786440 | tf_op jit(solution)/shard_map/ppermute | solution.py:630
  77.5 1.8 %collective-permute-start.20 = (f32[10,8,128]{2,1,0:T(8,128)S(1)}, f32[10,8,128]{2,1,0:T(8,128)S(1)}, u32[]{:S(2)}, u32[]{:S(2)}) collective-permute-start(f32[10,8,128]{2,1,0:T(8,128)S(1)} %get-tuple-element.76.own), channel_id=1, source_target_pairs={{1,0},{2,1},{3,2},{4,3},{5,4},{6,5},{7,6},{0,7},{9,8},{10,9},{11,1... | collective-permute-start | bytes 122888 | tf_op jit(solution)/shard_map/ppermute | solution.py:635
  77.5 4.7 %collective-permute-start.19 = (f32[10,8,128]{2,1,0:T(8,128)S(1)}, f32[10,8,128]{2,1,0:T(8,128)S(1)}, u32[]{:S(2)}, u32[]{:S(2)}) collective-permute-start(f32[10,8,128]{2,1,0:T(8,128)S(1)} %get-tuple-element.76.own), channel_id=1, source_target_pairs={{0,1},{1,2},{2,3},{3,4},{4,5},{5,6},{6,7},{7,0},{8,9},{9,10},{10,1... | collective-permute-start | bytes 122888 | tf_op jit(solution)/shard_map/ppermute | solution.py:630
  82.4 5.5 %collective-permute-start.22 = (f32[20,8,128]{2,1,0:T(8,128)S(1)}, f32[20,8,128]{2,1,0:T(8,128)S(1)}, u32[]{:S(2)}, u32[]{:S(2)}) collective-permute-start(f32[20,8,128]{2,1,0:T(8,128)S(1)} %spread.2.own3), channel_id=1, source_target_pairs={{64,0},{96,32},{128,64},{160,96},{192,128},{224,160},{0,192},{32,2... | collective-permute-start | bytes 245768 | tf_op jit(solution)/shard_map/ppermute | solution.py:635
  82.5 7.8 %collective-permute-start.21 = (f32[20,8,128]{2,1,0:T(8,128)S(1)}, f32[20,8,128]{2,1,0:T(8,128)S(1)}, u32[]{:S(2)}, u32[]{:S(2)}) collective-permute-start(f32[20,8,128]{2,1,0:T(8,128)S(1)} %spread.2.own3), channel_id=1, source_target_pairs={{0,64},{32,96},{64,128},{96,160},{128,192},{160,224},{192,0},{224,... | collective-permute-start | bytes 245768 | tf_op jit(solution)/shard_map/ppermute | solution.py:630
  102.6 7.7 %collective-permute-start.25 = (f32[16,8,128]{2,1,0:T(8,128)S(1)}, f32[16,8,128]{2,1,0:T(8,128)S(1)}, u32[]{:S(2)}, u32[]{:S(2)}) collective-permute-start(f32[16,8,128]{2,1,0:T(8,128)S(1)} %get-tuple-element.83), channel_id=1, source_target_pairs={{24,0},{0,8},{8,16},{16,24},{25,1},{1,9},{9,17},{17,25},{26,2},{2,... | collective-permute-start | bytes 196616 | tf_op jit(solution)/shard_map/ppermute | solution.py:635
  103.8 6.5 %collective-permute-start.24 = (f32[16,8,128]{2,1,0:T(8,128)S(1)}, f32[16,8,128]{2,1,0:T(8,128)S(1)}, u32[]{:S(2)}, u32[]{:S(2)}) collective-permute-start(f32[16,8,128]{2,1,0:T(8,128)S(1)} %get-tuple-element.83), channel_id=1, source_target_pairs={{16,0},{24,8},{0,16},{8,24},{17,1},{25,9},{1,17},{9,25},{18,2},{26... | collective-permute-start | bytes 196616 | tf_op jit(solution)/shard_map/ppermute | solution.py:635
  104.7 5.6 %collective-permute-start.23 = (f32[16,8,128]{2,1,0:T(8,128)S(1)}, f32[16,8,128]{2,1,0:T(8,128)S(1)}, u32[]{:S(2)}, u32[]{:S(2)}) collective-permute-start(f32[16,8,128]{2,1,0:T(8,128)S(1)} %get-tuple-element.83), channel_id=1, source_target_pairs={{8,0},{16,8},{24,16},{0,24},{9,1},{17,9},{25,17},{1,25},{10,2},{18... | collective-permute-start | bytes 196616 | tf_op jit(solution)/shard_map/ppermute | solution.py:635
  110.3 6.5 %collective-permute-start.27 = (f32[16,32,128]{2,1,0:T(8,128)S(1)}, f32[16,32,128]{2,1,0:T(8,128)S(1)}, u32[]{:S(2)}, u32[]{:S(2)}) collective-permute-start(f32[16,32,128]{2,1,0:T(8,128)S(1)} %constant_dynamic-update-slice_fusion.4.own), channel_id=1, source_target_pairs={{32,0},{64,32},{96,64},{128,96},{160,128},{192,160},{224,192},{0,2... | collective-permute-start | bytes 786440 | tf_op jit(solution)/shard_map/ppermute | solution.py:635
  110.4 7.7 %collective-permute-start.26 = (f32[16,32,128]{2,1,0:T(8,128)S(1)}, f32[16,32,128]{2,1,0:T(8,128)S(1)}, u32[]{:S(2)}, u32[]{:S(2)}) collective-permute-start(f32[16,32,128]{2,1,0:T(8,128)S(1)} %constant_dynamic-update-slice_fusion.4.own), channel_id=1, source_target_pairs={{0,32},{32,64},{64,96},{96,128},{128,160},{160,192},{192,224},{224... | collective-permute-start | bytes 786440 | tf_op jit(solution)/shard_map/ppermute | solution.py:630
  120.9 1.7 %collective-permute-start.29 = (f32[8,8,128]{2,1,0:T(8,128)S(1)}, f32[8,8,128]{2,1,0:T(8,128)S(1)}, u32[]{:S(2)}, u32[]{:S(2)}) collective-permute-start(f32[8,8,128]{2,1,0:T(8,128)S(1)} %get-tuple-element.84.own), channel_id=1, source_target_pairs={{1,0},{2,1},{3,2},{4,3},{5,4},{6,5},{7,6},{0,7},{9,8},{10,9},{11,1... | collective-permute-start | bytes 98312 | tf_op jit(solution)/shard_map/ppermute | solution.py:635
  121.0 4.6 %collective-permute-start.28 = (f32[8,8,128]{2,1,0:T(8,128)S(1)}, f32[8,8,128]{2,1,0:T(8,128)S(1)}, u32[]{:S(2)}, u32[]{:S(2)}) collective-permute-start(f32[8,8,128]{2,1,0:T(8,128)S(1)} %get-tuple-element.84.own), channel_id=1, source_target_pairs={{0,1},{1,2},{2,3},{3,4},{4,5},{5,6},{6,7},{7,0},{8,9},{9,10},{10,1... | collective-permute-start | bytes 98312 | tf_op jit(solution)/shard_map/ppermute | solution.py:630
  125.7 5.2 %collective-permute-start.31 = (f32[8,8,128]{2,1,0:T(8,128)S(1)}, f32[8,8,128]{2,1,0:T(8,128)S(1)}, u32[]{:S(2)}, u32[]{:S(2)}) collective-permute-start(f32[8,8,128]{2,1,0:T(8,128)S(1)} %spread.3.own3), channel_id=1, source_target_pairs={{64,0},{96,32},{128,64},{160,96},{192,128},{224,160},{0,192},{32,2... | collective-permute-start | bytes 98312 | tf_op jit(solution)/shard_map/ppermute | solution.py:635
  128.6 6.0 %collective-permute-start.30 = (f32[8,8,128]{2,1,0:T(8,128)S(1)}, f32[8,8,128]{2,1,0:T(8,128)S(1)}, u32[]{:S(2)}, u32[]{:S(2)}) collective-permute-start(f32[8,8,128]{2,1,0:T(8,128)S(1)} %spread.3.own3), channel_id=1, source_target_pairs={{0,64},{32,96},{64,128},{96,160},{128,192},{160,224},{192,0},{224,... | collective-permute-start | bytes 98312 | tf_op jit(solution)/shard_map/ppermute | solution.py:630

commit v2 on v1

--- a/solution.py
+++ b/solution.py
@@ -248,7 +248,25 @@
         out[...] = beside(own[0:24], own[24:48], high)
 
 
-def smooth_0(r, faces, inv, d0, d1, start, stop, between, again=False):
+def last_sweep_0(r, faces, d1, residual):
+    fx, fy, fz, diag = faces
+    rows, lanes = slice(0, BY), slice(0, BZ)
+
+    def own(at, n):
+        here = pl.ds(at, n)
+        wide = d1[pl.ds(at - 1, n + 2), rows, lanes]
+        x = fx[pl.ds(at - 1, n + 1), rows, lanes]
+        out = diag[here, rows, lanes] * wide[1:-1] - x[1:] * wide[2:] - x[:-1] * wide[:-2]
+        c, y = d1[here, :, lanes], fy[here, :, lanes]
+        out = out - y[:, rows] * roll(c, -1, 1)[:, rows] - roll(y * c, 1, 1)[:, rows]
+        c, z = d1[here, rows, :], fz[here, rows, :]
+        out = out - z[:, :, lanes] * roll(c, -1, 2)[:, :, lanes] - roll(z * c, 1, 2)[:, :, lanes]
+        residual[pl.ds(at - WX, n)] = r[here, rows, lanes] - out
+
+    loop(WX, WX + BX, B0, own, U0)
+
+
+def smooth_0(r, faces, inv, d0, d1, start, stop, between, again=False, residual=None):
     def second(at, n):
         here = pl.ds(at, n)
         left = r[here] - apply_at(d0, at, n, faces)
@@ -257,6 +275,9 @@
 
     loop(start + 1, stop - 1, B0, second, U0)
     between()
+    if residual is not None:
+        last_sweep_0(r, faces, d1, residual)
+        return
 
     def third(at, n):
         here = pl.ds(at, n)
@@ -596,10 +617,9 @@
     loop(begin_at, end_at, B0, lift_0, U0)
     into = pressure if last else total
     into[...] = total_in[...]
-    smooth_0(r, faces, inv, d0, d1, begin_at, end_at, lambda: add_own(into, (p0, d0, d1), False), again=first)
-    if last:
-        residual[...] = r[WX : WX + BX, 0:BY, 0:BZ]
-    else:
+    smooth_0(r, faces, inv, d0, d1, begin_at, end_at, lambda: add_own(into, (p0, d0, d1), False),
+             again=first, residual=residual if last else None)
+    if not last:
         smooth_0(r, faces, inv, d0, d1, 4, 44, lambda: add_own(total, (d0, d1), False))
         restrict_0(r, packed)
 

time: 143 us -> 143 us (level)
  no operation moved by 1% of the time
where the time goes in v2:
time: 143 us
  waiting for transfers between devices  50.6 us (35%)
  starting transfers between devices  47 us (33%)
  Pallas kernels  42.1 us (29%)
  local copies, waits for them, and re-layouts  1.95 us (1%)
    pallas_call x14, Pallas kernels, call(): pl.pallas_call(kernel, out_shape=[jax.ShapeDtypeStruct(s, F32) for s in o...  42.1 us
    ppermute x21, starting transfers between devices, from_above(): return lax.ppermute(array, axis, [((i + by) % n, i) for i in range(n)])  36.3 us
    ppermute x21, waiting for transfers between devices, from_above(): return lax.ppermute(array, axis, [((i + by) % n, i) for i in range(n)])  31 us
    ppermute x11, waiting for transfers between devices, from_below(): return lax.ppermute(array, axis, [(i, (i + by) % n) for i in range(n)])  19.6 us
    ppermute x11, starting transfers between devices, from_below(): return lax.ppermute(array, axis, [(i, (i + by) % n) for i in range(n)])  10.7 us
  transfers between devices with their start and end apart: 32, of which 19 were waited for; matrix products, arithmetic and copies ran while one was open for 0% of the time, Pallas kernels for 10%

profile of v2, /device:TPU:6, one launch (start us, length us, event | category | flops | bytes accessed | tf_op | source)
XLA Modules:
  0.0 142.7 jit_solution(1780777470128809908)
XLA Ops:
  0.6 0.9 copy-done
  1.6 0.1 send_z_own.1
  1.7 2.9 %collective-permute-start.1 = (f32[16,16,128]{2,1,0:T(8,128)S(1)}, f32[16,16,128]{2,1,0:T(8,128)S(1)}, u32[]{:S(2)}, u32[]{:S(2)}) collective-permute-start(f32[16,16,128]{2,1,0:T(8,128)S(1)} %get-tuple-element.50), channel_id=1, source_target_pairs={{1,0},{2,1},{3,2},{4,3},{5,4},{6,5},{7,6},{0,7},{9,8},{10,9},{11,1... | collective-permute-start | bytes 393224 | tf_op jit(solution)/shard_map/ppermute | solution.py:655
  4.7 2.6 %collective-permute-done.z_below.below = f32[16,16,128]{2,1,0:T(8,128)S(1)} collective-permute-done((f32[16,16,128]{2,1,0:T(8,128)S(1)}, f32[16,16,128]{2,1,0:T(8,128)S(1)}, u32[]{:S(2)}, u32[]{:S(2)}) %collective-permute-start) | collective-permute-done | bytes 131104 | tf_op jit(solution)/shard_map/ppermute | solution.py:650
  7.3 0.9 copy-done.2
  8.3 0.2 send_y.1
  8.4 0.9 collective-permute-start.3
  9.3 2.4 %collective-permute-start.2 = (f32[52,8,256]{2,1,0:T(8,128)S(1)}, f32[52,8,256]{2,1,0:T(8,128)S(1)}, u32[]{:S(2)}, u32[]{:S(2)}) collective-permute-start(f32[52,8,256]{2,1,0:T(8,128)S(1)} %get-tuple-element.52.refs_1_.upper), channel_id=1, source_target_pairs={{0,8},{8,16},{16,24},{24,0},{1,9},{9,17},{17,25},{25,1},{2,10},{10... | collective-permute-start | bytes 1277960 | tf_op jit(solution)/shard_map/ppermute | solution.py:650
  11.7 5.9 %collective-permute-start.4 = (f32[16,256]{1,0:T(8,128)S(1)}, f32[16,256]{1,0:T(8,128)S(1)}, u32[]{:S(2)}, u32[]{:S(2)}) collective-permute-start(f32[16,256]{1,0:T(8,128)S(1)} %get-tuple-element.53), channel_id=1, source_target_pairs={{32,0},{64,32},{96,64},{128,96},{160,128},{192,160},{224,192},{0,2... | collective-permute-start | bytes 49160 | tf_op jit(solution)/shard_map/ppermute | solution.py:655
  17.6 1.4 %collective-permute-done.4.refs_4_.plane = f32[16,256]{1,0:T(8,128)S(1)} collective-permute-done((f32[16,256]{1,0:T(8,128)S(1)}, f32[16,256]{1,0:T(8,128)S(1)}, u32[]{:S(2)}, u32[]{:S(2)}) %collective-permute-start.4) | collective-permute-done | bytes 16416 | tf_op jit(solution)/shard_map/ppermute | solution.py:655
  19.0 2.9 %collective-permute-done.3.refs_3_.rows_above.above = f32[52,8,256]{2,1,0:T(8,128)S(1)} collective-permute-done((f32[52,8,256]{2,1,0:T(8,128)S(1)}, f32[52,8,256]{2,1,0:T(8,128)S(1)}, u32[]{:S(2)}, u32[]{:S(2)}) %collective-permute-start.3) | collective-permute-done | bytes 426016 | tf_op jit(solution)/shard_map/ppermute | solution.py:655
  21.9 1.0 send_x.1
  22.9 1.9 %collective-permute-start.5 = (f32[14,32,256]{2,1,0:T(8,128)}, f32[14,32,256]{2,1,0:T(8,128)S(1)}, u32[]{:S(2)}, u32[]{:S(2)}) collective-permute-start(f32[14,32,256]{2,1,0:T(8,128)} %get-tuple-element.54), channel_id=1, source_target_pairs={{0,32},{32,64},{64,96},{96,128},{128,160},{160,192},{192,224},{224... | collective-permute-start | bytes 1376264 | tf_op jit(solution)/shard_map/ppermute | solution.py:650
  24.8 3.9 %collective-permute-start.6 = (f32[14,32,256]{2,1,0:T(8,128)}, f32[14,32,256]{2,1,0:T(8,128)S(1)}, u32[]{:S(2)}, u32[]{:S(2)}) collective-permute-start(f32[14,32,256]{2,1,0:T(8,128)} %get-tuple-element.55), channel_id=1, source_target_pairs={{32,0},{64,32},{96,64},{128,96},{160,128},{192,160},{224,192},{0,2... | collective-permute-start | bytes 1376264 | tf_op jit(solution)/shard_map/ppermute | solution.py:655
  28.8 0.1 pad_add_fusion.where
  28.9 2.3 %own_faces_0.1.refs_6_ = f32[48,8,128]{2,1,0:T(8,128)S(1)} custom-call(s32[3]{0:T(128)S(1)} %pad_add_fusion.where, s32[32,16,128]{2,1,0:T(8,128)S(1)} %copy-done.1, f32[16,16,128]{2,1,0:T(8,128)S(1)} %collective-permute-done.z_below.below, f32[16,16,128]{2,1,0:T(8,128)S(1)} %collective-permute-done.1.z_above.above, ...), custom_call_target="tpu_custom_call" | custom-call | bytes 7000000 | tf_op jit(solution)/shard_map/own_faces_0/pallas_call | solution.py:635
  31.1 0.1 collective-permute-start.7
  31.2 3.2 %collective-permute-start.16 = (f32[48,8,128]{2,1,0:T(8,128)S(1)}, f32[48,8,128]{2,1,0:T(8,128)S(1)}, u32[]{:S(2)}, u32[]{:S(2)}) collective-permute-start(f32[48,8,128]{2,1,0:T(8,128)S(1)} %own_faces_0.1.refs_6_), channel_id=1, source_target_pairs={{24,0},{0,8},{8,16},{16,24},{25,1},{1,9},{9,17},{17,25},{26,2},{2,... | collective-permute-start | bytes 589832 | tf_op jit(solution)/shard_map/ppermute | solution.py:655
  34.4 1.2 collective-permute-start.15
  35.6 4.1 %collective-permute-done.7.refs_7_ = f32[48,8,128]{2,1,0:T(8,128)S(1)} collective-permute-done((f32[48,8,128]{2,1,0:T(8,128)S(1)}, f32[48,8,128]{2,1,0:T(8,128)S(1)}, u32[]{:S(2)}, u32[]{:S(2)}) %collective-permute-start.7) | collective-permute-done | bytes 196640 | tf_op jit(solution)/shard_map/ppermute | solution.py:655
  39.7 0.3 send_z.1
  40.0 2.9 %collective-permute-start.9 = (f32[24,32,128]{2,1,0:T(8,128)S(1)}, f32[24,32,128]{2,1,0:T(8,128)S(1)}, u32[]{:S(2)}, u32[]{:S(2)}) collective-permute-start(f32[24,32,128]{2,1,0:T(8,128)S(1)} %get-tuple-element.58), channel_id=1, source_target_pairs={{1,0},{2,1},{3,2},{4,3},{5,4},{6,5},{7,6},{0,7},{9,8},{10,9},{11,1... | collective-permute-start | bytes 1179656 | tf_op jit(solution)/shard_map/ppermute | solution.py:655
  43.0 0.7 collective-permute-done.15
  43.7 0.1 pad_maximum_fusion.own
  43.8 1.9 %collective-permute-start.18 = (f32[48,32,128]{2,1,0:T(8,128)S(1)}, f32[48,32,128]{2,1,0:T(8,128)S(1)}, u32[]{:S(2)}, u32[]{:S(2)}) collective-permute-start(f32[48,32,128]{2,1,0:T(8,128)S(1)} %pad_maximum_fusion.own), channel_id=1, source_target_pairs={{32,0},{64,32},{96,64},{128,96},{160,128},{192,160},{224,192},{0,2... | collective-permute-start | bytes 2359304 | tf_op jit(solution)/shard_map/ppermute | solution.py:655
  45.7 0.2 collective-permute-start.17
  45.9 4.1 %faces_0.1 = (f32[48,32,256]{2,1,0:T(8,128)S(1)}, f32[48,32,256]{2,1,0:T(8,128)S(1)}, f32[48,32,256]{2,1,0:T(8,128)S(1)}, f32[48,32,256]{2,1,0:T(8,128)S(1)}, f32[48,32,256]{2,1,0:T(8,128)S(1)}) custom-call(s32[3]{0:T(128)S(1)} %pad_add_fusion.where, f32[52,8,256]{2,1,0:T(8,128)S(1)} %get-tuple-element.51.refs_0_.lower, ...), custom_call_target="tpu_custom_call" | custom-call | bytes 14000000 | tf_op jit(solution)/shard_map/faces_0/pallas_call | solution.py:635
  50.1 4.6 %begin.1 = (f32[48,32,256]{2,1,0:T(8,128)S(1)}, f32[32,16,128]{2,1,0:T(8,128)S(1)}, f32[16,8,128]{2,1,0:T(8,128)S(1)}) custom-call(f32[48,32,128]{2,1,0:T(8,128)S(1)} %get-tuple-element.56.own, f32[24,32,128]{2,1,0:T(8,128)S(1)} %collective-permute-done.8.z_below, f32[24,32,128]{2,1,0:T(8,128)S(1)} %collective-permute-done.9.z_above, ...), custom_call_target="tpu_custom_call" | custom-call | bytes 21000000 | tf_op jit(solution)/shard_map/begin/pallas_call | solution.py:635
  54.7 2.5 %collective-permute-start.12 = (f32[16,8,128]{2,1,0:T(8,128)S(1)}, f32[16,8,128]{2,1,0:T(8,128)S(1)}, u32[]{:S(2)}, u32[]{:S(2)}) collective-permute-start(f32[16,8,128]{2,1,0:T(8,128)S(1)} %get-tuple-element.64), channel_id=1, source_target_pairs={{24,0},{0,8},{8,16},{16,24},{25,1},{1,9},{9,17},{17,25},{26,2},{2,... | collective-permute-start | bytes 196616 | tf_op jit(solution)/shard_map/ppermute | solution.py:655
  57.2 0.7 collective-permute-start.11
  58.0 0.2 collective-permute-start.10
  58.2 5.5 %collective-permute-done.10 = f32[16,8,128]{2,1,0:T(8,128)S(1)} collective-permute-done((f32[16,8,128]{2,1,0:T(8,128)S(1)}, f32[16,8,128]{2,1,0:T(8,128)S(1)}, u32[]{:S(2)}, u32[]{:S(2)}) %collective-permute-start.10) | collective-permute-done | bytes 65568 | tf_op jit(solution)/shard_map/ppermute | solution.py:655
  63.8 3.3 %collective-permute-start.14 = (f32[16,32,128]{2,1,0:T(8,128)S(1)}, f32[16,32,128]{2,1,0:T(8,128)S(1)}, u32[]{:S(2)}, u32[]{:S(2)}) collective-permute-start(f32[16,32,128]{2,1,0:T(8,128)S(1)} %constant_dynamic-update-slice_fusion.own), channel_id=1, source_target_pairs={{32,0},{64,32},{96,64},{128,96},{160,128},{192,160},{224,192},{0,2... | collective-permute-start | bytes 786440 | tf_op jit(solution)/shard_map/ppermute | solution.py:655
  67.1 3.2 %faces_1.1 = (f32[48,32,128]{2,1,0:T(8,128)S(1)}, f32[48,32,128]{2,1,0:T(8,128)S(1)}, f32[48,32,128]{2,1,0:T(8,128)S(1)}, f32[48,32,128]{2,1,0:T(8,128)S(1)}, f3...) custom-call(s32[3]{0:T(128)S(1)} %pad_add_fusion.where, ...), custom_call_target="tpu_custom_call" | custom-call | bytes 10500000 | tf_op jit(solution)/shard_map/faces_1/pallas_call | solution.py:635
  70.3 0.6 collective-permute-done.14.above
  71.0 3.7 %collective-permute-done.13.below = f32[16,32,128]{2,1,0:T(8,128)S(1)} collective-permute-done((f32[16,32,128]{2,1,0:T(8,128)S(1)}, f32[16,32,128]{2,1,0:T(8,128)S(1)}, u32[]{:S(2)}, u32[]{:S(2)}) %collective-permute-start.13) | collective-permute-done | bytes 262176 | tf_op jit(solution)/shard_map/ppermute | solution.py:650
  74.6 2.8 %down.2 = (f32[48,32,128]{2,1,0:T(8,128)S(1)}, f32[48,32,128]{2,1,0:T(8,128)S(1)}, f32[24,16,128]{2,1,0:T(8,128)S(1)}, f32[24,16,128]{2,1,0:T(8,128)S(1)}, f32[10,8,128]{2,1,0:T(8,128)S(1)}) custom-call(f32[16,32,128]{2,1,0:T(8,128)S(1)} %constant_dynamic-update-slice_fusion.own, f32[16,32,128]{2,1,0:T(8,128)S(1)} %collective-permute-done.13.below, ...), custom_call_target="tpu_custom_call" | custom-call | bytes 14000000 | tf_op jit(solution)/shard_map/down/pallas_call | solution.py:635
  77.5 0.6 collective-permute-start.19
  78.1 1.2 collective-permute-done.20.above
  79.3 3.0 %collective-permute-done.19.below = f32[10,8,128]{2,1,0:T(8,128)S(1)} collective-permute-done((f32[10,8,128]{2,1,0:T(8,128)S(1)}, f32[10,8,128]{2,1,0:T(8,128)S(1)}, u32[]{:S(2)}, u32[]{:S(2)}) %collective-permute-start.19) | collective-permute-done | bytes 40992 | tf_op jit(solution)/shard_map/ppermute | solution.py:650
  82.2 0.2 spread.2.own3
  82.4 0.1 collective-permute-start.22
  82.5 2.9 %collective-permute-start.21 = (f32[20,8,128]{2,1,0:T(8,128)S(1)}, f32[20,8,128]{2,1,0:T(8,128)S(1)}, u32[]{:S(2)}, u32[]{:S(2)}) collective-permute-start(f32[20,8,128]{2,1,0:T(8,128)S(1)} %spread.2.own3), channel_id=1, source_target_pairs={{0,64},{32,96},{64,128},{96,160},{128,192},{160,224},{192,0},{224,... | collective-permute-start | bytes 245768 | tf_op jit(solution)/shard_map/ppermute | solution.py:650
  85.4 2.5 %collective-permute-done.22.above3 = f32[20,8,128]{2,1,0:T(8,128)S(1)} collective-permute-done((f32[20,8,128]{2,1,0:T(8,128)S(1)}, f32[20,8,128]{2,1,0:T(8,128)S(1)}, u32[]{:S(2)}, u32[]{:S(2)}) %collective-permute-start.22) | collective-permute-done | bytes 81952 | tf_op jit(solution)/shard_map/ppermute | solution.py:655
  88.0 2.4 %collective-permute-done.21.below3 = f32[20,8,128]{2,1,0:T(8,128)S(1)} collective-permute-done((f32[20,8,128]{2,1,0:T(8,128)S(1)}, f32[20,8,128]{2,1,0:T(8,128)S(1)}, u32[]{:S(2)}, u32[]{:S(2)}) %collective-permute-start.21) | collective-permute-done | bytes 81952 | tf_op jit(solution)/shard_map/ppermute | solution.py:650
  90.3 12.3 %up.1 = (f32[26,8,128]{2,1,0:T(8,128)S(1)}, f32[26,8,128]{2,1,0:T(8,128)S(1)}, f32[26,8,128]{2,1,0:T(8,128)S(1)}, f32[26,8,128]{2,1,0:T(8,128)S(1)}, f32[26,8,12...) custom-call(s32[3]{0:T(128)S(1)} %pad_add_fusion.where, ...), custom_call_target="tpu_custom_call" | custom-call | bytes 52500000 | tf_op jit(solution)/shard_map/up/pallas_call | solution.py:635
  102.6 1.2 collective-permute-start.25
  103.8 0.9 collective-permute-start.24
  104.7 1.3 collective-permute-start.23
  106.0 4.3 %collective-permute-done.23 = f32[16,8,128]{2,1,0:T(8,128)S(1)} collective-permute-done((f32[16,8,128]{2,1,0:T(8,128)S(1)}, f32[16,8,128]{2,1,0:T(8,128)S(1)}, u32[]{:S(2)}, u32[]{:S(2)}) %collective-permute-start.23) | collective-permute-done | bytes 65568 | tf_op jit(solution)/shard_map/ppermute | solution.py:655
  110.3 0.1 collective-permute-start.27
  110.4 2.0 %collective-permute-start.26 = (f32[16,32,128]{2,1,0:T(8,128)S(1)}, f32[16,32,128]{2,1,0:T(8,128)S(1)}, u32[]{:S(2)}, u32[]{:S(2)}) collective-permute-start(f32[16,32,128]{2,1,0:T(8,128)S(1)} %constant_dynamic-update-slice_fusion.4.own), channel_id=1, source_target_pairs={{0,32},{32,64},{64,96},{96,128},{128,160},{160,192},{192,224},{224... | collective-permute-start | bytes 786440 | tf_op jit(solution)/shard_map/ppermute | solution.py:650
  112.4 4.3 %collective-permute-done.27.above = f32[16,32,128]{2,1,0:T(8,128)S(1)} collective-permute-done((f32[16,32,128]{2,1,0:T(8,128)S(1)}, f32[16,32,128]{2,1,0:T(8,128)S(1)}, u32[]{:S(2)}, u32[]{:S(2)}) %collective-permute-start.27) | collective-permute-done | bytes 262176 | tf_op jit(solution)/shard_map/ppermute | solution.py:655
  116.8 1.3 collective-permute-done.26.below
  118.1 2.8 %down.3 = (f32[48,32,128]{2,1,0:T(8,128)S(1)}, f32[48,32,128]{2,1,0:T(8,128)S(1)}, f32[24,16,128]{2,1,0:T(8,128)S(1)}, f32[24,16,128]{2,1,0:T(8,128)S(1)}, f32[8,8,128]{2,1,0:T(8,128)S(1)}) custom-call(f32[16,32,128]{2,1,0:T(8,128)S(1)} %constant_dynamic-update-slice_fusion.4.own, f32[16,32,128]{2,1,0:T(8,128)S(1)} %collective-permute-done.26.below, ...), custom_call_target="tpu_custom_call" | custom-call | bytes 14000000 | tf_op jit(solution)/shard_map/down/pallas_call | solution.py:635
  121.0 0.6 collective-permute-start.28
  121.6 1.1 collective-permute-done.29.above
  122.6 3.0 %collective-permute-done.28.below = f32[8,8,128]{2,1,0:T(8,128)S(1)} collective-permute-done((f32[8,8,128]{2,1,0:T(8,128)S(1)}, f32[8,8,128]{2,1,0:T(8,128)S(1)}, u32[]{:S(2)}, u32[]{:S(2)}) %collective-permute-start.28) | collective-permute-done | bytes 32800 | tf_op jit(solution)/shard_map/ppermute | solution.py:650
  125.6 0.1 spread.3.own3
  125.7 2.9 %collective-permute-start.31 = (f32[8,8,128]{2,1,0:T(8,128)S(1)}, f32[8,8,128]{2,1,0:T(8,128)S(1)}, u32[]{:S(2)}, u32[]{:S(2)}) collective-permute-start(f32[8,8,128]{2,1,0:T(8,128)S(1)} %spread.3.own3), channel_id=1, source_target_pairs={{64,0},{96,32},{128,64},{160,96},{192,128},{224,160},{0,192},{32,2... | collective-permute-start | bytes 98312 | tf_op jit(solution)/shard_map/ppermute | solution.py:655
  128.6 0.1 collective-permute-start.30
  128.7 2.2 %collective-permute-done.31.above3 = f32[8,8,128]{2,1,0:T(8,128)S(1)} collective-permute-done((f32[8,8,128]{2,1,0:T(8,128)S(1)}, f32[8,8,128]{2,1,0:T(8,128)S(1)}, u32[]{:S(2)}, u32[]{:S(2)}) %collective-permute-start.31) | collective-permute-done | bytes 32800 | tf_op jit(solution)/shard_map/ppermute | solution.py:655
  130.9 3.7 %collective-permute-done.30.below3 = f32[8,8,128]{2,1,0:T(8,128)S(1)} collective-permute-done((f32[8,8,128]{2,1,0:T(8,128)S(1)}, f32[8,8,128]{2,1,0:T(8,128)S(1)}, u32[]{:S(2)}, u32[]{:S(2)}) %collective-permute-start.30) | collective-permute-done | bytes 32800 | tf_op jit(solution)/shard_map/ppermute | solution.py:650
  134.6 8.1 %up_last.1 = (f32[32,16,128]{2,1,0:T(8,128)}, f32[32,16,128]{2,1,0:T(8,128)}) custom-call(s32[3]{0:T(128)S(1)} %pad_add_fusion.where, f32[8,8,128]{2,1,0:T(8,128)S(1)} %spread.3.own3, f32[8,8,128]{2,1,0:T(8,128)S(1)} %collective-permute-done.30.below3, f32[8,8,128]{2,1,0:T(8,128)S(1)} %collective-permute-done.31.above3, ...), custom_call_target="tpu_custom_call" | custom-call | bytes 35000000 | tf_op jit(solution)/shard_map/up_last/pallas_call | solution.py:635
  (30 shorter events, 0.2 us)
Async XLA Ops:
  0.6 1.0 copy-start
  1.6 27.3 %copy-start.1 = (s32[32,16,128]{2,1,0:T(8,128)S(1)}, s32[32,16,128]{2,1,0:T(8,128)}, u32[]{:S(2)}) copy-start(s32[32,16,128]{2,1,0:T(8,128)} %mask.5) | copy-start | bytes 786436
  1.7 5.6 %collective-permute-start = (f32[16,16,128]{2,1,0:T(8,128)S(1)}, f32[16,16,128]{2,1,0:T(8,128)S(1)}, u32[]{:S(2)}, u32[]{:S(2)}) collective-permute-start(f32[16,16,128]{2,1,0:T(8,128)S(1)} %get-tuple-element.49), channel_id=1, source_target_pairs={{0,1},{1,2},{2,3},{3,4},{4,5},{5,6},{6,7},{7,0},{8,9},{9,10},{10,1... | collective-permute-start | bytes 393224 | tf_op jit(solution)/shard_map/ppermute | solution.py:650
  1.7 5.6 %collective-permute-start.1 = (f32[16,16,128]{2,1,0:T(8,128)S(1)}, f32[16,16,128]{2,1,0:T(8,128)S(1)}, u32[]{:S(2)}, u32[]{:S(2)}) collective-permute-start(f32[16,16,128]{2,1,0:T(8,128)S(1)} %get-tuple-element.50), channel_id=1, source_target_pairs={{1,0},{2,1},{3,2},{4,3},{5,4},{6,5},{7,6},{0,7},{9,8},{10,9},{11,1... | collective-permute-start | bytes 393224 | tf_op jit(solution)/shard_map/ppermute | solution.py:655
  7.3 1.0 copy-start.2
  8.4 13.5 %collective-permute-start.3 = (f32[52,8,256]{2,1,0:T(8,128)S(1)}, f32[52,8,256]{2,1,0:T(8,128)S(1)}, u32[]{:S(2)}, u32[]{:S(2)}) collective-permute-start(f32[52,8,256]{2,1,0:T(8,128)S(1)} %get-tuple-element.51.refs_0_.lower), channel_id=1, source_target_pairs={{8,0},{16,8},{24,16},{0,24},{9,1},{17,9},{25,17},{1,25},{10,2},{18... | collective-permute-start | bytes 1277960 | tf_op jit(solution)/shard_map/ppermute | solution.py:655
  9.3 12.6 %collective-permute-start.2 = (f32[52,8,256]{2,1,0:T(8,128)S(1)}, f32[52,8,256]{2,1,0:T(8,128)S(1)}, u32[]{:S(2)}, u32[]{:S(2)}) collective-permute-start(f32[52,8,256]{2,1,0:T(8,128)S(1)} %get-tuple-element.52.refs_1_.upper), channel_id=1, source_target_pairs={{0,8},{8,16},{16,24},{24,0},{1,9},{9,17},{17,25},{25,1},{2,10},{10... | collective-permute-start | bytes 1277960 | tf_op jit(solution)/shard_map/ppermute | solution.py:650
  11.7 7.3 %collective-permute-start.4 = (f32[16,256]{1,0:T(8,128)S(1)}, f32[16,256]{1,0:T(8,128)S(1)}, u32[]{:S(2)}, u32[]{:S(2)}) collective-permute-start(f32[16,256]{1,0:T(8,128)S(1)} %get-tuple-element.53), channel_id=1, source_target_pairs={{32,0},{64,32},{96,64},{128,96},{160,128},{192,160},{224,192},{0,2... | collective-permute-start | bytes 49160 | tf_op jit(solution)/shard_map/ppermute | solution.py:655
  22.9 16.8 %collective-permute-start.5 = (f32[14,32,256]{2,1,0:T(8,128)}, f32[14,32,256]{2,1,0:T(8,128)S(1)}, u32[]{:S(2)}, u32[]{:S(2)}) collective-permute-start(f32[14,32,256]{2,1,0:T(8,128)} %get-tuple-element.54), channel_id=1, source_target_pairs={{0,32},{32,64},{64,96},{96,128},{128,160},{160,192},{192,224},{224... | collective-permute-start | bytes 1376264 | tf_op jit(solution)/shard_map/ppermute | solution.py:650
  24.8 14.9 %collective-permute-start.6 = (f32[14,32,256]{2,1,0:T(8,128)}, f32[14,32,256]{2,1,0:T(8,128)S(1)}, u32[]{:S(2)}, u32[]{:S(2)}) collective-permute-start(f32[14,32,256]{2,1,0:T(8,128)} %get-tuple-element.55), channel_id=1, source_target_pairs={{32,0},{64,32},{96,64},{128,96},{160,128},{192,160},{224,192},{0,2... | collective-permute-start | bytes 1376264 | tf_op jit(solution)/shard_map/ppermute | solution.py:655
  31.1 8.6 %collective-permute-start.7 = (f32[48,8,128]{2,1,0:T(8,128)S(1)}, f32[48,8,128]{2,1,0:T(8,128)S(1)}, u32[]{:S(2)}, u32[]{:S(2)}) collective-permute-start(f32[48,8,128]{2,1,0:T(8,128)S(1)} %own_faces_0.1.refs_6_), channel_id=1, source_target_pairs={{8,0},{16,8},{24,16},{0,24},{9,1},{17,9},{25,17},{1,25},{10,2},{18... | collective-permute-start | bytes 589832 | tf_op jit(solution)/shard_map/ppermute | solution.py:655
  31.2 11.8 %collective-permute-start.16 = (f32[48,8,128]{2,1,0:T(8,128)S(1)}, f32[48,8,128]{2,1,0:T(8,128)S(1)}, u32[]{:S(2)}, u32[]{:S(2)}) collective-permute-start(f32[48,8,128]{2,1,0:T(8,128)S(1)} %own_faces_0.1.refs_6_), channel_id=1, source_target_pairs={{24,0},{0,8},{8,16},{16,24},{25,1},{1,9},{9,17},{17,25},{26,2},{2,... | collective-permute-start | bytes 589832 | tf_op jit(solution)/shard_map/ppermute | solution.py:655
  34.4 9.3 %collective-permute-start.15 = (f32[48,8,128]{2,1,0:T(8,128)S(1)}, f32[48,8,128]{2,1,0:T(8,128)S(1)}, u32[]{:S(2)}, u32[]{:S(2)}) collective-permute-start(f32[48,8,128]{2,1,0:T(8,128)S(1)} %own_faces_0.1.refs_6_), channel_id=1, source_target_pairs={{16,0},{24,8},{0,16},{8,24},{17,1},{25,9},{1,17},{9,25},{18,2},{26... | collective-permute-start | bytes 589832 | tf_op jit(solution)/shard_map/ppermute | solution.py:655
  40.0 10.0 %collective-permute-start.8 = (f32[24,32,128]{2,1,0:T(8,128)S(1)}, f32[24,32,128]{2,1,0:T(8,128)S(1)}, u32[]{:S(2)}, u32[]{:S(2)}) collective-permute-start(f32[24,32,128]{2,1,0:T(8,128)S(1)} %get-tuple-element.57), channel_id=1, source_target_pairs={{0,1},{1,2},{2,3},{3,4},{4,5},{5,6},{6,7},{7,0},{8,9},{9,10},{10,1... | collective-permute-start | bytes 1179656 | tf_op jit(solution)/shard_map/ppermute | solution.py:650
  40.0 10.0 %collective-permute-start.9 = (f32[24,32,128]{2,1,0:T(8,128)S(1)}, f32[24,32,128]{2,1,0:T(8,128)S(1)}, u32[]{:S(2)}, u32[]{:S(2)}) collective-permute-start(f32[24,32,128]{2,1,0:T(8,128)S(1)} %get-tuple-element.58), channel_id=1, source_target_pairs={{1,0},{2,1},{3,2},{4,3},{5,4},{6,5},{7,6},{0,7},{9,8},{10,9},{11,1... | collective-permute-start | bytes 1179656 | tf_op jit(solution)/shard_map/ppermute | solution.py:655
  43.8 23.3 %collective-permute-start.18 = (f32[48,32,128]{2,1,0:T(8,128)S(1)}, f32[48,32,128]{2,1,0:T(8,128)S(1)}, u32[]{:S(2)}, u32[]{:S(2)}) collective-permute-start(f32[48,32,128]{2,1,0:T(8,128)S(1)} %pad_maximum_fusion.own), channel_id=1, source_target_pairs={{32,0},{64,32},{96,64},{128,96},{160,128},{192,160},{224,192},{0,2... | collective-permute-start | bytes 2359304 | tf_op jit(solution)/shard_map/ppermute | solution.py:655
  45.7 21.3 %collective-permute-start.17 = (f32[48,32,128]{2,1,0:T(8,128)S(1)}, f32[48,32,128]{2,1,0:T(8,128)S(1)}, u32[]{:S(2)}, u32[]{:S(2)}) collective-permute-start(f32[48,32,128]{2,1,0:T(8,128)S(1)} %pad_maximum_fusion.own), channel_id=1, source_target_pairs={{0,32},{32,64},{64,96},{96,128},{128,160},{160,192},{192,224},{224... | collective-permute-start | bytes 2359304 | tf_op jit(solution)/shard_map/ppermute | solution.py:650
  54.7 9.1 %collective-permute-start.12 = (f32[16,8,128]{2,1,0:T(8,128)S(1)}, f32[16,8,128]{2,1,0:T(8,128)S(1)}, u32[]{:S(2)}, u32[]{:S(2)}) collective-permute-start(f32[16,8,128]{2,1,0:T(8,128)S(1)} %get-tuple-element.64), channel_id=1, source_target_pairs={{24,0},{0,8},{8,16},{16,24},{25,1},{1,9},{9,17},{17,25},{26,2},{2,... | collective-permute-start | bytes 196616 | tf_op jit(solution)/shard_map/ppermute | solution.py:655
  57.2 6.5 %collective-permute-start.11 = (f32[16,8,128]{2,1,0:T(8,128)S(1)}, f32[16,8,128]{2,1,0:T(8,128)S(1)}, u32[]{:S(2)}, u32[]{:S(2)}) collective-permute-start(f32[16,8,128]{2,1,0:T(8,128)S(1)} %get-tuple-element.64), channel_id=1, source_target_pairs={{16,0},{24,8},{0,16},{8,24},{17,1},{25,9},{1,17},{9,25},{18,2},{26... | collective-permute-start | bytes 196616 | tf_op jit(solution)/shard_map/ppermute | solution.py:655
  58.0 5.7 %collective-permute-start.10 = (f32[16,8,128]{2,1,0:T(8,128)S(1)}, f32[16,8,128]{2,1,0:T(8,128)S(1)}, u32[]{:S(2)}, u32[]{:S(2)}) collective-permute-start(f32[16,8,128]{2,1,0:T(8,128)S(1)} %get-tuple-element.64), channel_id=1, source_target_pairs={{8,0},{16,8},{24,16},{0,24},{9,1},{17,9},{25,17},{1,25},{10,2},{18... | collective-permute-start | bytes 196616 | tf_op jit(solution)/shard_map/ppermute | solution.py:655
  63.8 7.2 %collective-permute-start.14 = (f32[16,32,128]{2,1,0:T(8,128)S(1)}, f32[16,32,128]{2,1,0:T(8,128)S(1)}, u32[]{:S(2)}, u32[]{:S(2)}) collective-permute-start(f32[16,32,128]{2,1,0:T(8,128)S(1)} %constant_dynamic-update-slice_fusion.own), channel_id=1, source_target_pairs={{32,0},{64,32},{96,64},{128,96},{160,128},{192,160},{224,192},{0,2... | collective-permute-start | bytes 786440 | tf_op jit(solution)/shard_map/ppermute | solution.py:655
  67.1 7.6 %collective-permute-start.13 = (f32[16,32,128]{2,1,0:T(8,128)S(1)}, f32[16,32,128]{2,1,0:T(8,128)S(1)}, u32[]{:S(2)}, u32[]{:S(2)}) collective-permute-start(f32[16,32,128]{2,1,0:T(8,128)S(1)} %constant_dynamic-update-slice_fusion.own), channel_id=1, source_target_pairs={{0,32},{32,64},{64,96},{96,128},{128,160},{160,192},{192,224},{224... | collective-permute-start | bytes 786440 | tf_op jit(solution)/shard_map/ppermute | solution.py:650
  77.5 1.8 %collective-permute-start.20 = (f32[10,8,128]{2,1,0:T(8,128)S(1)}, f32[10,8,128]{2,1,0:T(8,128)S(1)}, u32[]{:S(2)}, u32[]{:S(2)}) collective-permute-start(f32[10,8,128]{2,1,0:T(8,128)S(1)} %get-tuple-element.76.own), channel_id=1, source_target_pairs={{1,0},{2,1},{3,2},{4,3},{5,4},{6,5},{7,6},{0,7},{9,8},{10,9},{11,1... | collective-permute-start | bytes 122888 | tf_op jit(solution)/shard_map/ppermute | solution.py:655
  77.5 4.7 %collective-permute-start.19 = (f32[10,8,128]{2,1,0:T(8,128)S(1)}, f32[10,8,128]{2,1,0:T(8,128)S(1)}, u32[]{:S(2)}, u32[]{:S(2)}) collective-permute-start(f32[10,8,128]{2,1,0:T(8,128)S(1)} %get-tuple-element.76.own), channel_id=1, source_target_pairs={{0,1},{1,2},{2,3},{3,4},{4,5},{5,6},{6,7},{7,0},{8,9},{9,10},{10,1... | collective-permute-start | bytes 122888 | tf_op jit(solution)/shard_map/ppermute | solution.py:650
  82.4 5.5 %collective-permute-start.22 = (f32[20,8,128]{2,1,0:T(8,128)S(1)}, f32[20,8,128]{2,1,0:T(8,128)S(1)}, u32[]{:S(2)}, u32[]{:S(2)}) collective-permute-start(f32[20,8,128]{2,1,0:T(8,128)S(1)} %spread.2.own3), channel_id=1, source_target_pairs={{64,0},{96,32},{128,64},{160,96},{192,128},{224,160},{0,192},{32,2... | collective-permute-start | bytes 245768 | tf_op jit(solution)/shard_map/ppermute | solution.py:655
  82.5 7.8 %collective-permute-start.21 = (f32[20,8,128]{2,1,0:T(8,128)S(1)}, f32[20,8,128]{2,1,0:T(8,128)S(1)}, u32[]{:S(2)}, u32[]{:S(2)}) collective-permute-start(f32[20,8,128]{2,1,0:T(8,128)S(1)} %spread.2.own3), channel_id=1, source_target_pairs={{0,64},{32,96},{64,128},{96,160},{128,192},{160,224},{192,0},{224,... | collective-permute-start | bytes 245768 | tf_op jit(solution)/shard_map/ppermute | solution.py:650
  102.6 7.7 %collective-permute-start.25 = (f32[16,8,128]{2,1,0:T(8,128)S(1)}, f32[16,8,128]{2,1,0:T(8,128)S(1)}, u32[]{:S(2)}, u32[]{:S(2)}) collective-permute-start(f32[16,8,128]{2,1,0:T(8,128)S(1)} %get-tuple-element.83), channel_id=1, source_target_pairs={{24,0},{0,8},{8,16},{16,24},{25,1},{1,9},{9,17},{17,25},{26,2},{2,... | collective-permute-start | bytes 196616 | tf_op jit(solution)/shard_map/ppermute | solution.py:655
  103.8 6.5 %collective-permute-start.24 = (f32[16,8,128]{2,1,0:T(8,128)S(1)}, f32[16,8,128]{2,1,0:T(8,128)S(1)}, u32[]{:S(2)}, u32[]{:S(2)}) collective-permute-start(f32[16,8,128]{2,1,0:T(8,128)S(1)} %get-tuple-element.83), channel_id=1, source_target_pairs={{16,0},{24,8},{0,16},{8,24},{17,1},{25,9},{1,17},{9,25},{18,2},{26... | collective-permute-start | bytes 196616 | tf_op jit(solution)/shard_map/ppermute | solution.py:655
  104.7 5.6 %collective-permute-start.23 = (f32[16,8,128]{2,1,0:T(8,128)S(1)}, f32[16,8,128]{2,1,0:T(8,128)S(1)}, u32[]{:S(2)}, u32[]{:S(2)}) collective-permute-start(f32[16,8,128]{2,1,0:T(8,128)S(1)} %get-tuple-element.83), channel_id=1, source_target_pairs={{8,0},{16,8},{24,16},{0,24},{9,1},{17,9},{25,17},{1,25},{10,2},{18... | collective-permute-start | bytes 196616 | tf_op jit(solution)/shard_map/ppermute | solution.py:655
  110.3 6.5 %collective-permute-start.27 = (f32[16,32,128]{2,1,0:T(8,128)S(1)}, f32[16,32,128]{2,1,0:T(8,128)S(1)}, u32[]{:S(2)}, u32[]{:S(2)}) collective-permute-start(f32[16,32,128]{2,1,0:T(8,128)S(1)} %constant_dynamic-update-slice_fusion.4.own), channel_id=1, source_target_pairs={{32,0},{64,32},{96,64},{128,96},{160,128},{192,160},{224,192},{0,2... | collective-permute-start | bytes 786440 | tf_op jit(solution)/shard_map/ppermute | solution.py:655
  110.4 7.7 %collective-permute-start.26 = (f32[16,32,128]{2,1,0:T(8,128)S(1)}, f32[16,32,128]{2,1,0:T(8,128)S(1)}, u32[]{:S(2)}, u32[]{:S(2)}) collective-permute-start(f32[16,32,128]{2,1,0:T(8,128)S(1)} %constant_dynamic-update-slice_fusion.4.own), channel_id=1, source_target_pairs={{0,32},{32,64},{64,96},{96,128},{128,160},{160,192},{192,224},{224... | collective-permute-start | bytes 786440 | tf_op jit(solution)/shard_map/ppermute | solution.py:650
  120.9 1.7 %collective-permute-start.29 = (f32[8,8,128]{2,1,0:T(8,128)S(1)}, f32[8,8,128]{2,1,0:T(8,128)S(1)}, u32[]{:S(2)}, u32[]{:S(2)}) collective-permute-start(f32[8,8,128]{2,1,0:T(8,128)S(1)} %get-tuple-element.84.own), channel_id=1, source_target_pairs={{1,0},{2,1},{3,2},{4,3},{5,4},{6,5},{7,6},{0,7},{9,8},{10,9},{11,1... | collective-permute-start | bytes 98312 | tf_op jit(solution)/shard_map/ppermute | solution.py:655
  121.0 4.6 %collective-permute-start.28 = (f32[8,8,128]{2,1,0:T(8,128)S(1)}, f32[8,8,128]{2,1,0:T(8,128)S(1)}, u32[]{:S(2)}, u32[]{:S(2)}) collective-permute-start(f32[8,8,128]{2,1,0:T(8,128)S(1)} %get-tuple-element.84.own), channel_id=1, source_target_pairs={{0,1},{1,2},{2,3},{3,4},{4,5},{5,6},{6,7},{7,0},{8,9},{9,10},{10,1... | collective-permute-start | bytes 98312 | tf_op jit(solution)/shard_map/ppermute | solution.py:650
  125.7 5.2 %collective-permute-start.31 = (f32[8,8,128]{2,1,0:T(8,128)S(1)}, f32[8,8,128]{2,1,0:T(8,128)S(1)}, u32[]{:S(2)}, u32[]{:S(2)}) collective-permute-start(f32[8,8,128]{2,1,0:T(8,128)S(1)} %spread.3.own3), channel_id=1, source_target_pairs={{64,0},{96,32},{128,64},{160,96},{192,128},{224,160},{0,192},{32,2... | collective-permute-start | bytes 98312 | tf_op jit(solution)/shard_map/ppermute | solution.py:655
  128.6 6.0 %collective-permute-start.30 = (f32[8,8,128]{2,1,0:T(8,128)S(1)}, f32[8,8,128]{2,1,0:T(8,128)S(1)}, u32[]{:S(2)}, u32[]{:S(2)}) collective-permute-start(f32[8,8,128]{2,1,0:T(8,128)S(1)} %spread.3.own3), channel_id=1, source_target_pairs={{0,64},{32,96},{64,128},{96,160},{128,192},{160,224},{192,0},{224,... | collective-permute-start | bytes 98312 | tf_op jit(solution)/shard_map/ppermute | solution.py:650

commit v3 on v2

--- a/solution.py
+++ b/solution.py
@@ -392,10 +392,15 @@
     restrict_0(r, packed)
 
 
-def assemble_1(part, own, below, above, out):
-    out[0:16] = below[part]
-    out[16:32] = own[part]
-    out[32:48] = above[part]
+def assemble_1(n, own, below, above, out):
+    width = below.shape[0] // (own.shape[0] // 16)
+    part = slice(width * n, width * (n + 1))
+    out[16:32] = own[16 * n : 16 * n + 16]
+    out[16 - width : 16] = below[part]
+    out[32 : 32 + width] = above[part]
+    rest = jnp.zeros((16 - width,) + own.shape[1:], F32)
+    out[0 : 16 - width] = rest
+    out[32 + width : 48] = rest
 
 
 def relax_1(r, faces, inv, d0, d1, start, stop):
@@ -421,7 +426,7 @@
         (fy, row_pairs(ny1, odd_y=True), lanes),
         (fz, rows, odd_lanes),
     )):
-        assemble_1(slice(16 * n, 16 * (n + 1)), own, below, above, raw)
+        assemble_1(n, own, below, above, raw)
         coarse.append(jnp.concatenate(
             [coarsen(raw[8 * g : 8 * g + 8], rows_matrix, columns) for g in range(6)], 0))
     shape = (B1, ny1, 128)
@@ -464,7 +469,7 @@
     *given, r, e, r2_out, e2_out, packed, d0, d1 = refs
     ny1 = fx.shape[1]
     ny2 = ny1 // 2
-    assemble_1(slice(0, 16), own, below, above, r)
+    assemble_1(0, own, below, above, r)
     rows, lanes = row_pairs(ny1), lane_pairs(128, 0.125)
 
     def begin_1(at, n):
@@ -668,9 +673,11 @@
     def along_y(packed):
         return [packed] + [from_above(packed, "gy", s) for s in range(1, ny)]
 
-    def along_x(parts):
+    def along_x(parts, width):
         rows = jnp.concatenate(parts, 1)
-        return rows, from_below(rows, "gx"), from_above(rows, "gx")
+        planes = rows.reshape((-1, 16) + rows.shape[1:])
+        last, first = (p.reshape((-1,) + rows.shape[1:]) for p in (planes[:, 16 - width :], planes[:, :width]))
+        return rows, from_below(last, "gx"), from_above(first, "gx")
 
     to_upper, to_lower = call(send_z_own, "send_z_own", (phase_mask,), [(16, BY, 128)] * 2)
     beside_own = (from_below(to_upper, "gz"), from_above(to_lower, "gz"))
@@ -685,7 +692,7 @@
         functools.partial(own_faces_0, sizes), "own_faces_0", (where, phase_mask, *beside_own, above, plane),
         [(48, 8, 128)], [(BX + 1, BY, Z0)] + [(BX, BY, Z0)] * 3, us=2)
     parts = along_y(packed)
-    around_faces = along_x(parts)
+    around_faces = along_x(parts, 15)
     r_own, to_upper, to_lower = call(
         send_z, "send_z", pieces, [(X0, Y0, 128)] + [(24, Y0, 128)] * 2, after=(packed, parts[1]))
     residual = (r_own, from_below(to_upper, "gz"), from_above(to_lower, "gz"))
@@ -701,7 +708,7 @@
     for cycle in range(2):
         first = cycle == 0
         r1, e1, r2, e2, packed = call(
-            down, "down", (*along_x(along_y(packed)), *levels, *([faces_3] if first else [])),
+            down, "down", (*along_x(along_y(packed), 14), *levels, *([faces_3] if first else [])),
             [full_1] * 2 + [full_2] * 2 + [(10 if first else 8, 2 * ny, 128)], [full_1] * 2, us=4)
         below, above = from_below(packed, "gz"), from_above(packed, "gz")
         (wide,) = call(spread, "spread", (packed, below, above), [(20 if first else 8, 2 * ny, 128)])

time: 143 us -> 143 us (level)
  no operation moved by 1% of the time
where the time goes in v3:
time: 143 us
  waiting for transfers between devices  50.7 us (35%)
  starting transfers between devices  47.2 us (33%)
  Pallas kernels  42 us (29%)
  local copies, waits for them, and re-layouts  2.13 us (1%)
    pallas_call x14, Pallas kernels, call(): pl.pallas_call(kernel, out_shape=[jax.ShapeDtypeStruct(s, F32) for s in o...  42 us
    ppermute x21, starting transfers between devices, from_above(): return lax.ppermute(array, axis, [((i + by) % n, i) for i in range(n)])  37 us
    ppermute x21, waiting for transfers between devices, from_above(): return lax.ppermute(array, axis, [((i + by) % n, i) for i in range(n)])  31.5 us
    ppermute x11, waiting for transfers between devices, from_below(): return lax.ppermute(array, axis, [(i, (i + by) % n) for i in range(n)])  19.2 us
    ppermute x11, starting transfers between devices, from_below(): return lax.ppermute(array, axis, [(i, (i + by) % n) for i in range(n)])  10.2 us
  transfers between devices with their start and end apart: 32, of which 19 were waited for; matrix products, arithmetic and copies ran while one was open for 0% of the time, Pallas kernels for 10%

profile of v3, /device:TPU:6, one launch (start us, length us, event | category | flops | bytes accessed | tf_op | source)
XLA Modules:
  0.0 143.0 jit_solution(2162870940611636155)
XLA Ops:
  0.6 0.9 copy-done
  1.6 0.1 send_z_own.1
  1.7 2.9 %collective-permute-start.1 = (f32[16,16,128]{2,1,0:T(8,128)S(1)}, f32[16,16,128]{2,1,0:T(8,128)S(1)}, u32[]{:S(2)}, u32[]{:S(2)}) collective-permute-start(f32[16,16,128]{2,1,0:T(8,128)S(1)} %get-tuple-element.50), channel_id=1, source_target_pairs={{1,0},{2,1},{3,2},{4,3},{5,4},{6,5},{7,6},{0,7},{9,8},{10,9},{11,1... | collective-permute-start | bytes 393224 | tf_op jit(solution)/shard_map/ppermute | solution.py:660
  4.7 2.6 %collective-permute-done.z_below.below = f32[16,16,128]{2,1,0:T(8,128)S(1)} collective-permute-done((f32[16,16,128]{2,1,0:T(8,128)S(1)}, f32[16,16,128]{2,1,0:T(8,128)S(1)}, u32[]{:S(2)}, u32[]{:S(2)}) %collective-permute-start) | collective-permute-done | bytes 131104 | tf_op jit(solution)/shard_map/ppermute | solution.py:655
  7.3 0.9 copy-done.2
  8.3 0.2 send_y.1
  8.4 0.9 collective-permute-start.3
  9.3 2.4 %collective-permute-start.2 = (f32[52,8,256]{2,1,0:T(8,128)S(1)}, f32[52,8,256]{2,1,0:T(8,128)S(1)}, u32[]{:S(2)}, u32[]{:S(2)}) collective-permute-start(f32[52,8,256]{2,1,0:T(8,128)S(1)} %get-tuple-element.52.refs_1_.upper), channel_id=1, source_target_pairs={{0,8},{8,16},{16,24},{24,0},{1,9},{9,17},{17,25},{25,1},{2,10},{10... | collective-permute-start | bytes 1277960 | tf_op jit(solution)/shard_map/ppermute | solution.py:655
  11.7 5.9 %collective-permute-start.4 = (f32[16,256]{1,0:T(8,128)S(1)}, f32[16,256]{1,0:T(8,128)S(1)}, u32[]{:S(2)}, u32[]{:S(2)}) collective-permute-start(f32[16,256]{1,0:T(8,128)S(1)} %get-tuple-element.53), channel_id=1, source_target_pairs={{32,0},{64,32},{96,64},{128,96},{160,128},{192,160},{224,192},{0,2... | collective-permute-start | bytes 49160 | tf_op jit(solution)/shard_map/ppermute | solution.py:660
  17.6 1.4 %collective-permute-done.4.refs_4_.plane = f32[16,256]{1,0:T(8,128)S(1)} collective-permute-done((f32[16,256]{1,0:T(8,128)S(1)}, f32[16,256]{1,0:T(8,128)S(1)}, u32[]{:S(2)}, u32[]{:S(2)}) %collective-permute-start.4) | collective-permute-done | bytes 16416 | tf_op jit(solution)/shard_map/ppermute | solution.py:660
  19.0 2.9 %collective-permute-done.3.refs_3_.rows_above.above = f32[52,8,256]{2,1,0:T(8,128)S(1)} collective-permute-done((f32[52,8,256]{2,1,0:T(8,128)S(1)}, f32[52,8,256]{2,1,0:T(8,128)S(1)}, u32[]{:S(2)}, u32[]{:S(2)}) %collective-permute-start.3) | collective-permute-done | bytes 426016 | tf_op jit(solution)/shard_map/ppermute | solution.py:660
  21.9 1.0 send_x.1
  22.9 1.9 %collective-permute-start.5 = (f32[14,32,256]{2,1,0:T(8,128)}, f32[14,32,256]{2,1,0:T(8,128)S(1)}, u32[]{:S(2)}, u32[]{:S(2)}) collective-permute-start(f32[14,32,256]{2,1,0:T(8,128)} %get-tuple-element.54), channel_id=1, source_target_pairs={{0,32},{32,64},{64,96},{96,128},{128,160},{160,192},{192,224},{224... | collective-permute-start | bytes 1376264 | tf_op jit(solution)/shard_map/ppermute | solution.py:655
  24.8 3.9 %collective-permute-start.6 = (f32[14,32,256]{2,1,0:T(8,128)}, f32[14,32,256]{2,1,0:T(8,128)S(1)}, u32[]{:S(2)}, u32[]{:S(2)}) collective-permute-start(f32[14,32,256]{2,1,0:T(8,128)} %get-tuple-element.55), channel_id=1, source_target_pairs={{32,0},{64,32},{96,64},{128,96},{160,128},{192,160},{224,192},{0,2... | collective-permute-start | bytes 1376264 | tf_op jit(solution)/shard_map/ppermute | solution.py:660
  28.8 0.1 pad_add_fusion.where
  28.9 2.3 %own_faces_0.1.refs_6_ = f32[48,8,128]{2,1,0:T(8,128)S(1)} custom-call(s32[3]{0:T(128)S(1)} %pad_add_fusion.where, s32[32,16,128]{2,1,0:T(8,128)S(1)} %copy-done.1, f32[16,16,128]{2,1,0:T(8,128)S(1)} %collective-permute-done.z_below.below, f32[16,16,128]{2,1,0:T(8,128)S(1)} %collective-permute-done.1.z_above.above, ...), custom_call_target="tpu_custom_call" | custom-call | bytes 7000000 | tf_op jit(solution)/shard_map/own_faces_0/pallas_call | solution.py:640
  31.1 0.1 collective-permute-start.7
  31.2 3.2 %collective-permute-start.16 = (f32[48,8,128]{2,1,0:T(8,128)S(1)}, f32[48,8,128]{2,1,0:T(8,128)S(1)}, u32[]{:S(2)}, u32[]{:S(2)}) collective-permute-start(f32[48,8,128]{2,1,0:T(8,128)S(1)} %own_faces_0.1.refs_6_), channel_id=1, source_target_pairs={{24,0},{0,8},{8,16},{16,24},{25,1},{1,9},{9,17},{17,25},{26,2},{2,... | collective-permute-start | bytes 589832 | tf_op jit(solution)/shard_map/ppermute | solution.py:660
  34.4 1.2 collective-permute-start.15
  35.6 4.1 %collective-permute-done.7.refs_7_ = f32[48,8,128]{2,1,0:T(8,128)S(1)} collective-permute-done((f32[48,8,128]{2,1,0:T(8,128)S(1)}, f32[48,8,128]{2,1,0:T(8,128)S(1)}, u32[]{:S(2)}, u32[]{:S(2)}) %collective-permute-start.7) | collective-permute-done | bytes 196640 | tf_op jit(solution)/shard_map/ppermute | solution.py:660
  39.7 0.3 send_z.1
  40.0 2.9 %collective-permute-start.9 = (f32[24,32,128]{2,1,0:T(8,128)S(1)}, f32[24,32,128]{2,1,0:T(8,128)S(1)}, u32[]{:S(2)}, u32[]{:S(2)}) collective-permute-start(f32[24,32,128]{2,1,0:T(8,128)S(1)} %get-tuple-element.58), channel_id=1, source_target_pairs={{1,0},{2,1},{3,2},{4,3},{5,4},{6,5},{7,6},{0,7},{9,8},{10,9},{11,1... | collective-permute-start | bytes 1179656 | tf_op jit(solution)/shard_map/ppermute | solution.py:660
  43.0 0.7 collective-permute-done.15
  43.8 0.1 fusion
  43.9 0.1 collective-permute-start.17
  44.0 3.2 %collective-permute-start.18 = (f32[45,32,128]{2,1,0:T(8,128)S(1)}, f32[45,32,128]{2,1,0:T(8,128)S(1)}, u32[]{:S(2)}, u32[]{:S(2)}) collective-permute-start(f32[45,32,128]{2,1,0:T(8,128)S(1)} %bitcast.19), channel_id=1, source_target_pairs={{32,0},{64,32},{96,64},{128,96},{160,128},{192,160},{224,192},{0,2... | collective-permute-start | bytes 2211848 | tf_op jit(solution)/shard_map/ppermute | solution.py:660
  47.2 4.1 %faces_0.1 = (f32[48,32,256]{2,1,0:T(8,128)S(1)}, f32[48,32,256]{2,1,0:T(8,128)S(1)}, f32[48,32,256]{2,1,0:T(8,128)S(1)}, f32[48,32,256]{2,1,0:T(8,128)S(1)}, f32[48,32,256]{2,1,0:T(8,128)S(1)}) custom-call(s32[3]{0:T(128)S(1)} %pad_add_fusion.where, f32[52,8,256]{2,1,0:T(8,128)S(1)} %get-tuple-element.51.refs_0_.lower, ...), custom_call_target="tpu_custom_call" | custom-call | bytes 14000000 | tf_op jit(solution)/shard_map/faces_0/pallas_call | solution.py:640
  51.4 4.5 %begin.1 = (f32[48,32,256]{2,1,0:T(8,128)S(1)}, f32[32,16,128]{2,1,0:T(8,128)S(1)}, f32[16,8,128]{2,1,0:T(8,128)S(1)}) custom-call(f32[48,32,128]{2,1,0:T(8,128)S(1)} %get-tuple-element.56.own, f32[24,32,128]{2,1,0:T(8,128)S(1)} %collective-permute-done.8.z_below, f32[24,32,128]{2,1,0:T(8,128)S(1)} %collective-permute-done.9.z_above, ...), custom_call_target="tpu_custom_call" | custom-call | bytes 21000000 | tf_op jit(solution)/shard_map/begin/pallas_call | solution.py:640
  55.9 2.2 %collective-permute-start.12 = (f32[16,8,128]{2,1,0:T(8,128)S(1)}, f32[16,8,128]{2,1,0:T(8,128)S(1)}, u32[]{:S(2)}, u32[]{:S(2)}) collective-permute-start(f32[16,8,128]{2,1,0:T(8,128)S(1)} %get-tuple-element.64), channel_id=1, source_target_pairs={{24,0},{0,8},{8,16},{16,24},{25,1},{1,9},{9,17},{17,25},{26,2},{2,... | collective-permute-start | bytes 196616 | tf_op jit(solution)/shard_map/ppermute | solution.py:660
  58.1 1.1 collective-permute-start.11
  59.2 5.5 %collective-permute-done.10 = f32[16,8,128]{2,1,0:T(8,128)S(1)} collective-permute-done((f32[16,8,128]{2,1,0:T(8,128)S(1)}, f32[16,8,128]{2,1,0:T(8,128)S(1)}, u32[]{:S(2)}, u32[]{:S(2)}) %collective-permute-start.10) | collective-permute-done | bytes 65568 | tf_op jit(solution)/shard_map/ppermute | solution.py:660
  64.7 1.1 collective-permute-start.14
  65.9 1.0 collective-permute-start.13
  66.9 3.2 %faces_1.1 = (f32[48,32,128]{2,1,0:T(8,128)S(1)}, f32[48,32,128]{2,1,0:T(8,128)S(1)}, f32[48,32,128]{2,1,0:T(8,128)S(1)}, f32[48,32,128]{2,1,0:T(8,128)S(1)}, f3...) custom-call(s32[3]{0:T(128)S(1)} %pad_add_fusion.where, ...), custom_call_target="tpu_custom_call" | custom-call | bytes 10500000 | tf_op jit(solution)/shard_map/faces_1/pallas_call | solution.py:640
  70.1 0.8 collective-permute-done.14.above
  70.8 2.3 %collective-permute-done.13.below = f32[14,32,128]{2,1,0:T(8,128)S(1)} collective-permute-done((f32[14,32,128]{2,1,0:T(8,128)S(1)}, f32[14,32,128]{2,1,0:T(8,128)S(1)}, u32[]{:S(2)}, u32[]{:S(2)}) %collective-permute-start.13) | collective-permute-done | bytes 229408 | tf_op jit(solution)/shard_map/ppermute | solution.py:655
  73.1 2.8 %down.2 = (f32[48,32,128]{2,1,0:T(8,128)S(1)}, f32[48,32,128]{2,1,0:T(8,128)S(1)}, f32[24,16,128]{2,1,0:T(8,128)S(1)}, f32[24,16,128]{2,1,0:T(8,128)S(1)}, f32[10,8,128]{2,1,0:T(8,128)S(1)}) custom-call(f32[16,32,128]{2,1,0:T(8,128)S(1)} %constant_dynamic-update-slice_fusion.own, f32[14,32,128]{2,1,0:T(8,128)S(1)} %collective-permute-done.13.below, ...), custom_call_target="tpu_custom_call" | custom-call | bytes 14000000 | tf_op jit(solution)/shard_map/down/pallas_call | solution.py:640
  76.0 0.4 collective-permute-start.20
  76.3 0.3 collective-permute-start.19
  76.6 1.4 collective-permute-done.20.above
  78.0 3.0 %collective-permute-done.19.below = f32[10,8,128]{2,1,0:T(8,128)S(1)} collective-permute-done((f32[10,8,128]{2,1,0:T(8,128)S(1)}, f32[10,8,128]{2,1,0:T(8,128)S(1)}, u32[]{:S(2)}, u32[]{:S(2)}) %collective-permute-start.19) | collective-permute-done | bytes 40992 | tf_op jit(solution)/shard_map/ppermute | solution.py:655
  81.0 0.2 spread.2.own3
  81.2 1.1 collective-permute-start.22
  82.3 1.9 %collective-permute-start.21 = (f32[20,8,128]{2,1,0:T(8,128)S(1)}, f32[20,8,128]{2,1,0:T(8,128)S(1)}, u32[]{:S(2)}, u32[]{:S(2)}) collective-permute-start(f32[20,8,128]{2,1,0:T(8,128)S(1)} %spread.2.own3), channel_id=1, source_target_pairs={{0,64},{32,96},{64,128},{96,160},{128,192},{160,224},{192,0},{224,... | collective-permute-start | bytes 245768 | tf_op jit(solution)/shard_map/ppermute | solution.py:655
  84.2 3.3 %collective-permute-done.22.above3 = f32[20,8,128]{2,1,0:T(8,128)S(1)} collective-permute-done((f32[20,8,128]{2,1,0:T(8,128)S(1)}, f32[20,8,128]{2,1,0:T(8,128)S(1)}, u32[]{:S(2)}, u32[]{:S(2)}) %collective-permute-start.22) | collective-permute-done | bytes 81952 | tf_op jit(solution)/shard_map/ppermute | solution.py:660
  87.5 3.1 %collective-permute-done.21.below3 = f32[20,8,128]{2,1,0:T(8,128)S(1)} collective-permute-done((f32[20,8,128]{2,1,0:T(8,128)S(1)}, f32[20,8,128]{2,1,0:T(8,128)S(1)}, u32[]{:S(2)}, u32[]{:S(2)}) %collective-permute-start.21) | collective-permute-done | bytes 81952 | tf_op jit(solution)/shard_map/ppermute | solution.py:655
  90.6 12.3 %up.1 = (f32[26,8,128]{2,1,0:T(8,128)S(1)}, f32[26,8,128]{2,1,0:T(8,128)S(1)}, f32[26,8,128]{2,1,0:T(8,128)S(1)}, f32[26,8,128]{2,1,0:T(8,128)S(1)}, f32[26,8,12...) custom-call(s32[3]{0:T(128)S(1)} %pad_add_fusion.where, ...), custom_call_target="tpu_custom_call" | custom-call | bytes 52500000 | tf_op jit(solution)/shard_map/up/pallas_call | solution.py:640
  102.9 1.3 collective-permute-start.25
  104.1 0.9 collective-permute-start.24
  105.0 1.3 collective-permute-start.23
  106.3 4.3 %collective-permute-done.23 = f32[16,8,128]{2,1,0:T(8,128)S(1)} collective-permute-done((f32[16,8,128]{2,1,0:T(8,128)S(1)}, f32[16,8,128]{2,1,0:T(8,128)S(1)}, u32[]{:S(2)}, u32[]{:S(2)}) %collective-permute-start.23) | collective-permute-done | bytes 65568 | tf_op jit(solution)/shard_map/ppermute | solution.py:660
  110.7 0.1 collective-permute-start.27
  110.8 2.0 %collective-permute-start.26 = (f32[14,32,128]{2,1,0:T(8,128)S(1)}, f32[14,32,128]{2,1,0:T(8,128)S(1)}, u32[]{:S(2)}, u32[]{:S(2)}) collective-permute-start(f32[14,32,128]{2,1,0:T(8,128)S(1)} %get-tuple-element.99), channel_id=1, source_target_pairs={{0,32},{32,64},{64,96},{96,128},{128,160},{160,192},{192,224},{224... | collective-permute-start | bytes 688136 | tf_op jit(solution)/shard_map/ppermute | solution.py:655
  112.8 4.0 %collective-permute-done.27.above = f32[14,32,128]{2,1,0:T(8,128)S(1)} collective-permute-done((f32[14,32,128]{2,1,0:T(8,128)S(1)}, f32[14,32,128]{2,1,0:T(8,128)S(1)}, u32[]{:S(2)}, u32[]{:S(2)}) %collective-permute-start.27) | collective-permute-done | bytes 229408 | tf_op jit(solution)/shard_map/ppermute | solution.py:660
  116.8 1.3 collective-permute-done.26.below
  118.1 2.8 %down.3 = (f32[48,32,128]{2,1,0:T(8,128)S(1)}, f32[48,32,128]{2,1,0:T(8,128)S(1)}, f32[24,16,128]{2,1,0:T(8,128)S(1)}, f32[24,16,128]{2,1,0:T(8,128)S(1)}, f32[8,8,128]{2,1,0:T(8,128)S(1)}) custom-call(f32[16,32,128]{2,1,0:T(8,128)S(1)} %constant_dynamic-update-slice_fusion.4.own, f32[14,32,128]{2,1,0:T(8,128)S(1)} %collective-permute-done.26.below, ...), custom_call_target="tpu_custom_call" | custom-call | bytes 14000000 | tf_op jit(solution)/shard_map/down/pallas_call | solution.py:640
  121.0 0.6 collective-permute-start.28
  121.6 1.1 collective-permute-done.29.above
  122.7 3.0 %collective-permute-done.28.below = f32[8,8,128]{2,1,0:T(8,128)S(1)} collective-permute-done((f32[8,8,128]{2,1,0:T(8,128)S(1)}, f32[8,8,128]{2,1,0:T(8,128)S(1)}, u32[]{:S(2)}, u32[]{:S(2)}) %collective-permute-start.28) | collective-permute-done | bytes 32800 | tf_op jit(solution)/shard_map/ppermute | solution.py:655
  125.6 0.1 spread.3.own3
  125.7 3.2 %collective-permute-start.31 = (f32[8,8,128]{2,1,0:T(8,128)S(1)}, f32[8,8,128]{2,1,0:T(8,128)S(1)}, u32[]{:S(2)}, u32[]{:S(2)}) collective-permute-start(f32[8,8,128]{2,1,0:T(8,128)S(1)} %spread.3.own3), channel_id=1, source_target_pairs={{64,0},{96,32},{128,64},{160,96},{192,128},{224,160},{0,192},{32,2... | collective-permute-start | bytes 98312 | tf_op jit(solution)/shard_map/ppermute | solution.py:660
  128.9 2.0 %collective-permute-done.31.above3 = f32[8,8,128]{2,1,0:T(8,128)S(1)} collective-permute-done((f32[8,8,128]{2,1,0:T(8,128)S(1)}, f32[8,8,128]{2,1,0:T(8,128)S(1)}, u32[]{:S(2)}, u32[]{:S(2)}) %collective-permute-start.31) | collective-permute-done | bytes 32800 | tf_op jit(solution)/shard_map/ppermute | solution.py:660
  130.9 4.0 %collective-permute-done.30.below3 = f32[8,8,128]{2,1,0:T(8,128)S(1)} collective-permute-done((f32[8,8,128]{2,1,0:T(8,128)S(1)}, f32[8,8,128]{2,1,0:T(8,128)S(1)}, u32[]{:S(2)}, u32[]{:S(2)}) %collective-permute-start.30) | collective-permute-done | bytes 32800 | tf_op jit(solution)/shard_map/ppermute | solution.py:655
  135.0 8.1 %up_last.1 = (f32[32,16,128]{2,1,0:T(8,128)}, f32[32,16,128]{2,1,0:T(8,128)}) custom-call(s32[3]{0:T(128)S(1)} %pad_add_fusion.where, f32[8,8,128]{2,1,0:T(8,128)S(1)} %spread.3.own3, f32[8,8,128]{2,1,0:T(8,128)S(1)} %collective-permute-done.30.below3, f32[8,8,128]{2,1,0:T(8,128)S(1)} %collective-permute-done.31.above3, ...), custom_call_target="tpu_custom_call" | custom-call | bytes 35000000 | tf_op jit(solution)/shard_map/up_last/pallas_call | solution.py:640
  (33 shorter events, 0.3 us)
Async XLA Ops:
  0.6 1.0 copy-start
  1.6 27.3 %copy-start.1 = (s32[32,16,128]{2,1,0:T(8,128)S(1)}, s32[32,16,128]{2,1,0:T(8,128)}, u32[]{:S(2)}) copy-start(s32[32,16,128]{2,1,0:T(8,128)} %mask.5) | copy-start | bytes 786436
  1.7 5.6 %collective-permute-start = (f32[16,16,128]{2,1,0:T(8,128)S(1)}, f32[16,16,128]{2,1,0:T(8,128)S(1)}, u32[]{:S(2)}, u32[]{:S(2)}) collective-permute-start(f32[16,16,128]{2,1,0:T(8,128)S(1)} %get-tuple-element.49), channel_id=1, source_target_pairs={{0,1},{1,2},{2,3},{3,4},{4,5},{5,6},{6,7},{7,0},{8,9},{9,10},{10,1... | collective-permute-start | bytes 393224 | tf_op jit(solution)/shard_map/ppermute | solution.py:655
  1.7 5.6 %collective-permute-start.1 = (f32[16,16,128]{2,1,0:T(8,128)S(1)}, f32[16,16,128]{2,1,0:T(8,128)S(1)}, u32[]{:S(2)}, u32[]{:S(2)}) collective-permute-start(f32[16,16,128]{2,1,0:T(8,128)S(1)} %get-tuple-element.50), channel_id=1, source_target_pairs={{1,0},{2,1},{3,2},{4,3},{5,4},{6,5},{7,6},{0,7},{9,8},{10,9},{11,1... | collective-permute-start | bytes 393224 | tf_op jit(solution)/shard_map/ppermute | solution.py:660
  7.3 1.0 copy-start.2
  8.4 13.5 %collective-permute-start.3 = (f32[52,8,256]{2,1,0:T(8,128)S(1)}, f32[52,8,256]{2,1,0:T(8,128)S(1)}, u32[]{:S(2)}, u32[]{:S(2)}) collective-permute-start(f32[52,8,256]{2,1,0:T(8,128)S(1)} %get-tuple-element.51.refs_0_.lower), channel_id=1, source_target_pairs={{8,0},{16,8},{24,16},{0,24},{9,1},{17,9},{25,17},{1,25},{10,2},{18... | collective-permute-start | bytes 1277960 | tf_op jit(solution)/shard_map/ppermute | solution.py:660
  9.3 12.6 %collective-permute-start.2 = (f32[52,8,256]{2,1,0:T(8,128)S(1)}, f32[52,8,256]{2,1,0:T(8,128)S(1)}, u32[]{:S(2)}, u32[]{:S(2)}) collective-permute-start(f32[52,8,256]{2,1,0:T(8,128)S(1)} %get-tuple-element.52.refs_1_.upper), channel_id=1, source_target_pairs={{0,8},{8,16},{16,24},{24,0},{1,9},{9,17},{17,25},{25,1},{2,10},{10... | collective-permute-start | bytes 1277960 | tf_op jit(solution)/shard_map/ppermute | solution.py:655
  11.7 7.3 %collective-permute-start.4 = (f32[16,256]{1,0:T(8,128)S(1)}, f32[16,256]{1,0:T(8,128)S(1)}, u32[]{:S(2)}, u32[]{:S(2)}) collective-permute-start(f32[16,256]{1,0:T(8,128)S(1)} %get-tuple-element.53), channel_id=1, source_target_pairs={{32,0},{64,32},{96,64},{128,96},{160,128},{192,160},{224,192},{0,2... | collective-permute-start | bytes 49160 | tf_op jit(solution)/shard_map/ppermute | solution.py:660
  22.9 16.8 %collective-permute-start.5 = (f32[14,32,256]{2,1,0:T(8,128)}, f32[14,32,256]{2,1,0:T(8,128)S(1)}, u32[]{:S(2)}, u32[]{:S(2)}) collective-permute-start(f32[14,32,256]{2,1,0:T(8,128)} %get-tuple-element.54), channel_id=1, source_target_pairs={{0,32},{32,64},{64,96},{96,128},{128,160},{160,192},{192,224},{224... | collective-permute-start | bytes 1376264 | tf_op jit(solution)/shard_map/ppermute | solution.py:655
  24.8 14.9 %collective-permute-start.6 = (f32[14,32,256]{2,1,0:T(8,128)}, f32[14,32,256]{2,1,0:T(8,128)S(1)}, u32[]{:S(2)}, u32[]{:S(2)}) collective-permute-start(f32[14,32,256]{2,1,0:T(8,128)} %get-tuple-element.55), channel_id=1, source_target_pairs={{32,0},{64,32},{96,64},{128,96},{160,128},{192,160},{224,192},{0,2... | collective-permute-start | bytes 1376264 | tf_op jit(solution)/shard_map/ppermute | solution.py:660
  31.1 8.6 %collective-permute-start.7 = (f32[48,8,128]{2,1,0:T(8,128)S(1)}, f32[48,8,128]{2,1,0:T(8,128)S(1)}, u32[]{:S(2)}, u32[]{:S(2)}) collective-permute-start(f32[48,8,128]{2,1,0:T(8,128)S(1)} %own_faces_0.1.refs_6_), channel_id=1, source_target_pairs={{8,0},{16,8},{24,16},{0,24},{9,1},{17,9},{25,17},{1,25},{10,2},{18... | collective-permute-start | bytes 589832 | tf_op jit(solution)/shard_map/ppermute | solution.py:660
  31.2 11.8 %collective-permute-start.16 = (f32[48,8,128]{2,1,0:T(8,128)S(1)}, f32[48,8,128]{2,1,0:T(8,128)S(1)}, u32[]{:S(2)}, u32[]{:S(2)}) collective-permute-start(f32[48,8,128]{2,1,0:T(8,128)S(1)} %own_faces_0.1.refs_6_), channel_id=1, source_target_pairs={{24,0},{0,8},{8,16},{16,24},{25,1},{1,9},{9,17},{17,25},{26,2},{2,... | collective-permute-start | bytes 589832 | tf_op jit(solution)/shard_map/ppermute | solution.py:660
  34.4 9.3 %collective-permute-start.15 = (f32[48,8,128]{2,1,0:T(8,128)S(1)}, f32[48,8,128]{2,1,0:T(8,128)S(1)}, u32[]{:S(2)}, u32[]{:S(2)}) collective-permute-start(f32[48,8,128]{2,1,0:T(8,128)S(1)} %own_faces_0.1.refs_6_), channel_id=1, source_target_pairs={{16,0},{24,8},{0,16},{8,24},{17,1},{25,9},{1,17},{9,25},{18,2},{26... | collective-permute-start | bytes 589832 | tf_op jit(solution)/shard_map/ppermute | solution.py:660
  40.0 11.3 %collective-permute-start.8 = (f32[24,32,128]{2,1,0:T(8,128)S(1)}, f32[24,32,128]{2,1,0:T(8,128)S(1)}, u32[]{:S(2)}, u32[]{:S(2)}) collective-permute-start(f32[24,32,128]{2,1,0:T(8,128)S(1)} %get-tuple-element.57), channel_id=1, source_target_pairs={{0,1},{1,2},{2,3},{3,4},{4,5},{5,6},{6,7},{7,0},{8,9},{9,10},{10,1... | collective-permute-start | bytes 1179656 | tf_op jit(solution)/shard_map/ppermute | solution.py:655
  40.0 11.3 %collective-permute-start.9 = (f32[24,32,128]{2,1,0:T(8,128)S(1)}, f32[24,32,128]{2,1,0:T(8,128)S(1)}, u32[]{:S(2)}, u32[]{:S(2)}) collective-permute-start(f32[24,32,128]{2,1,0:T(8,128)S(1)} %get-tuple-element.58), channel_id=1, source_target_pairs={{1,0},{2,1},{3,2},{4,3},{5,4},{6,5},{7,6},{0,7},{9,8},{10,9},{11,1... | collective-permute-start | bytes 1179656 | tf_op jit(solution)/shard_map/ppermute | solution.py:660
  43.9 23.0 %collective-permute-start.17 = (f32[45,32,128]{2,1,0:T(8,128)S(1)}, f32[45,32,128]{2,1,0:T(8,128)S(1)}, u32[]{:S(2)}, u32[]{:S(2)}) collective-permute-start(f32[45,32,128]{2,1,0:T(8,128)S(1)} %bitcast.20), channel_id=1, source_target_pairs={{0,32},{32,64},{64,96},{96,128},{128,160},{160,192},{192,224},{224... | collective-permute-start | bytes 2211848 | tf_op jit(solution)/shard_map/ppermute | solution.py:655
  44.0 22.9 %collective-permute-start.18 = (f32[45,32,128]{2,1,0:T(8,128)S(1)}, f32[45,32,128]{2,1,0:T(8,128)S(1)}, u32[]{:S(2)}, u32[]{:S(2)}) collective-permute-start(f32[45,32,128]{2,1,0:T(8,128)S(1)} %bitcast.19), channel_id=1, source_target_pairs={{32,0},{64,32},{96,64},{128,96},{160,128},{192,160},{224,192},{0,2... | collective-permute-start | bytes 2211848 | tf_op jit(solution)/shard_map/ppermute | solution.py:660
  55.9 8.8 %collective-permute-start.12 = (f32[16,8,128]{2,1,0:T(8,128)S(1)}, f32[16,8,128]{2,1,0:T(8,128)S(1)}, u32[]{:S(2)}, u32[]{:S(2)}) collective-permute-start(f32[16,8,128]{2,1,0:T(8,128)S(1)} %get-tuple-element.64), channel_id=1, source_target_pairs={{24,0},{0,8},{8,16},{16,24},{25,1},{1,9},{9,17},{17,25},{26,2},{2,... | collective-permute-start | bytes 196616 | tf_op jit(solution)/shard_map/ppermute | solution.py:660
  58.1 6.6 %collective-permute-start.11 = (f32[16,8,128]{2,1,0:T(8,128)S(1)}, f32[16,8,128]{2,1,0:T(8,128)S(1)}, u32[]{:S(2)}, u32[]{:S(2)}) collective-permute-start(f32[16,8,128]{2,1,0:T(8,128)S(1)} %get-tuple-element.64), channel_id=1, source_target_pairs={{16,0},{24,8},{0,16},{8,24},{17,1},{25,9},{1,17},{9,25},{18,2},{26... | collective-permute-start | bytes 196616 | tf_op jit(solution)/shard_map/ppermute | solution.py:660
  59.2 5.5 %collective-permute-start.10 = (f32[16,8,128]{2,1,0:T(8,128)S(1)}, f32[16,8,128]{2,1,0:T(8,128)S(1)}, u32[]{:S(2)}, u32[]{:S(2)}) collective-permute-start(f32[16,8,128]{2,1,0:T(8,128)S(1)} %get-tuple-element.64), channel_id=1, source_target_pairs={{8,0},{16,8},{24,16},{0,24},{9,1},{17,9},{25,17},{1,25},{10,2},{18... | collective-permute-start | bytes 196616 | tf_op jit(solution)/shard_map/ppermute | solution.py:660
  64.7 6.1 %collective-permute-start.14 = (f32[14,32,128]{2,1,0:T(8,128)S(1)}, f32[14,32,128]{2,1,0:T(8,128)S(1)}, u32[]{:S(2)}, u32[]{:S(2)}) collective-permute-start(f32[14,32,128]{2,1,0:T(8,128)S(1)} %get-tuple-element.100), channel_id=1, source_target_pairs={{32,0},{64,32},{96,64},{128,96},{160,128},{192,160},{224,192},{0,2... | collective-permute-start | bytes 688136 | tf_op jit(solution)/shard_map/ppermute | solution.py:660
  65.9 7.2 %collective-permute-start.13 = (f32[14,32,128]{2,1,0:T(8,128)S(1)}, f32[14,32,128]{2,1,0:T(8,128)S(1)}, u32[]{:S(2)}, u32[]{:S(2)}) collective-permute-start(f32[14,32,128]{2,1,0:T(8,128)S(1)} %get-tuple-element.101), channel_id=1, source_target_pairs={{0,32},{32,64},{64,96},{96,128},{128,160},{160,192},{192,224},{224... | collective-permute-start | bytes 688136 | tf_op jit(solution)/shard_map/ppermute | solution.py:655
  76.0 2.0 %collective-permute-start.20 = (f32[10,8,128]{2,1,0:T(8,128)S(1)}, f32[10,8,128]{2,1,0:T(8,128)S(1)}, u32[]{:S(2)}, u32[]{:S(2)}) collective-permute-start(f32[10,8,128]{2,1,0:T(8,128)S(1)} %get-tuple-element.76.own), channel_id=1, source_target_pairs={{1,0},{2,1},{3,2},{4,3},{5,4},{6,5},{7,6},{0,7},{9,8},{10,9},{11,1... | collective-permute-start | bytes 122888 | tf_op jit(solution)/shard_map/ppermute | solution.py:660
  76.3 4.6 %collective-permute-start.19 = (f32[10,8,128]{2,1,0:T(8,128)S(1)}, f32[10,8,128]{2,1,0:T(8,128)S(1)}, u32[]{:S(2)}, u32[]{:S(2)}) collective-permute-start(f32[10,8,128]{2,1,0:T(8,128)S(1)} %get-tuple-element.76.own), channel_id=1, source_target_pairs={{0,1},{1,2},{2,3},{3,4},{4,5},{5,6},{6,7},{7,0},{8,9},{9,10},{10,1... | collective-permute-start | bytes 122888 | tf_op jit(solution)/shard_map/ppermute | solution.py:655
  81.2 6.3 %collective-permute-start.22 = (f32[20,8,128]{2,1,0:T(8,128)S(1)}, f32[20,8,128]{2,1,0:T(8,128)S(1)}, u32[]{:S(2)}, u32[]{:S(2)}) collective-permute-start(f32[20,8,128]{2,1,0:T(8,128)S(1)} %spread.2.own3), channel_id=1, source_target_pairs={{64,0},{96,32},{128,64},{160,96},{192,128},{224,160},{0,192},{32,2... | collective-permute-start | bytes 245768 | tf_op jit(solution)/shard_map/ppermute | solution.py:660
  82.3 8.3 %collective-permute-start.21 = (f32[20,8,128]{2,1,0:T(8,128)S(1)}, f32[20,8,128]{2,1,0:T(8,128)S(1)}, u32[]{:S(2)}, u32[]{:S(2)}) collective-permute-start(f32[20,8,128]{2,1,0:T(8,128)S(1)} %spread.2.own3), channel_id=1, source_target_pairs={{0,64},{32,96},{64,128},{96,160},{128,192},{160,224},{192,0},{224,... | collective-permute-start | bytes 245768 | tf_op jit(solution)/shard_map/ppermute | solution.py:655
  102.9 7.8 %collective-permute-start.25 = (f32[16,8,128]{2,1,0:T(8,128)S(1)}, f32[16,8,128]{2,1,0:T(8,128)S(1)}, u32[]{:S(2)}, u32[]{:S(2)}) collective-permute-start(f32[16,8,128]{2,1,0:T(8,128)S(1)} %get-tuple-element.83), channel_id=1, source_target_pairs={{24,0},{0,8},{8,16},{16,24},{25,1},{1,9},{9,17},{17,25},{26,2},{2,... | collective-permute-start | bytes 196616 | tf_op jit(solution)/shard_map/ppermute | solution.py:660
  104.1 6.5 %collective-permute-start.24 = (f32[16,8,128]{2,1,0:T(8,128)S(1)}, f32[16,8,128]{2,1,0:T(8,128)S(1)}, u32[]{:S(2)}, u32[]{:S(2)}) collective-permute-start(f32[16,8,128]{2,1,0:T(8,128)S(1)} %get-tuple-element.83), channel_id=1, source_target_pairs={{16,0},{24,8},{0,16},{8,24},{17,1},{25,9},{1,17},{9,25},{18,2},{26... | collective-permute-start | bytes 196616 | tf_op jit(solution)/shard_map/ppermute | solution.py:660
  105.0 5.6 %collective-permute-start.23 = (f32[16,8,128]{2,1,0:T(8,128)S(1)}, f32[16,8,128]{2,1,0:T(8,128)S(1)}, u32[]{:S(2)}, u32[]{:S(2)}) collective-permute-start(f32[16,8,128]{2,1,0:T(8,128)S(1)} %get-tuple-element.83), channel_id=1, source_target_pairs={{8,0},{16,8},{24,16},{0,24},{9,1},{17,9},{25,17},{1,25},{10,2},{18... | collective-permute-start | bytes 196616 | tf_op jit(solution)/shard_map/ppermute | solution.py:660
  110.7 6.1 %collective-permute-start.27 = (f32[14,32,128]{2,1,0:T(8,128)S(1)}, f32[14,32,128]{2,1,0:T(8,128)S(1)}, u32[]{:S(2)}, u32[]{:S(2)}) collective-permute-start(f32[14,32,128]{2,1,0:T(8,128)S(1)} %get-tuple-element.98), channel_id=1, source_target_pairs={{32,0},{64,32},{96,64},{128,96},{160,128},{192,160},{224,192},{0,2... | collective-permute-start | bytes 688136 | tf_op jit(solution)/shard_map/ppermute | solution.py:660
  110.8 7.3 %collective-permute-start.26 = (f32[14,32,128]{2,1,0:T(8,128)S(1)}, f32[14,32,128]{2,1,0:T(8,128)S(1)}, u32[]{:S(2)}, u32[]{:S(2)}) collective-permute-start(f32[14,32,128]{2,1,0:T(8,128)S(1)} %get-tuple-element.99), channel_id=1, source_target_pairs={{0,32},{32,64},{64,96},{96,128},{128,160},{160,192},{192,224},{224... | collective-permute-start | bytes 688136 | tf_op jit(solution)/shard_map/ppermute | solution.py:655
  121.0 1.7 %collective-permute-start.29 = (f32[8,8,128]{2,1,0:T(8,128)S(1)}, f32[8,8,128]{2,1,0:T(8,128)S(1)}, u32[]{:S(2)}, u32[]{:S(2)}) collective-permute-start(f32[8,8,128]{2,1,0:T(8,128)S(1)} %get-tuple-element.84.own), channel_id=1, source_target_pairs={{1,0},{2,1},{3,2},{4,3},{5,4},{6,5},{7,6},{0,7},{9,8},{10,9},{11,1... | collective-permute-start | bytes 98312 | tf_op jit(solution)/shard_map/ppermute | solution.py:660
  121.0 4.6 %collective-permute-start.28 = (f32[8,8,128]{2,1,0:T(8,128)S(1)}, f32[8,8,128]{2,1,0:T(8,128)S(1)}, u32[]{:S(2)}, u32[]{:S(2)}) collective-permute-start(f32[8,8,128]{2,1,0:T(8,128)S(1)} %get-tuple-element.84.own), channel_id=1, source_target_pairs={{0,1},{1,2},{2,3},{3,4},{4,5},{5,6},{6,7},{7,0},{8,9},{9,10},{10,1... | collective-permute-start | bytes 98312 | tf_op jit(solution)/shard_map/ppermute | solution.py:655
  125.7 5.2 %collective-permute-start.31 = (f32[8,8,128]{2,1,0:T(8,128)S(1)}, f32[8,8,128]{2,1,0:T(8,128)S(1)}, u32[]{:S(2)}, u32[]{:S(2)}) collective-permute-start(f32[8,8,128]{2,1,0:T(8,128)S(1)} %spread.3.own3), channel_id=1, source_target_pairs={{64,0},{96,32},{128,64},{160,96},{192,128},{224,160},{0,192},{32,2... | collective-permute-start | bytes 98312 | tf_op jit(solution)/shard_map/ppermute | solution.py:660
  128.9 6.0 %collective-permute-start.30 = (f32[8,8,128]{2,1,0:T(8,128)S(1)}, f32[8,8,128]{2,1,0:T(8,128)S(1)}, u32[]{:S(2)}, u32[]{:S(2)}) collective-permute-start(f32[8,8,128]{2,1,0:T(8,128)S(1)} %spread.3.own3), channel_id=1, source_target_pairs={{0,64},{32,96},{64,128},{96,160},{128,192},{160,224},{192,0},{224,... | collective-permute-start | bytes 98312 | tf_op jit(solution)/shard_map/ppermute | solution.py:655
